TPU v7x, 32 devices: a whole 2x2x4 slice. The times are simulated.
32 devices in a mesh: branch: 4 (over y, x), seq: 8 (over z, core).
Axes of the slice: x: 2, y: 2, z: 4, core: 2. Of those that a mesh axis runs over, the one named last changes fastest.
Arguments:
- tokens: bfloat16 [2, 4096, 768], P(None, 'seq'), may hold values from -6 to 6
- cotangent: bfloat16 [2, 4096, 768], P(None, 'seq'), may hold values from -6 to 6
- lengths: int32 [2], replicated, may hold values from 512 to 4096, as said below
- query_index: int32 [2, 512], P(None, 'seq'), may hold values from -1 to 4095, as said below
- key_index: int32 [2, 512], P(None, 'seq'), may hold values from -1 to 4095, as said below
- gain_attn: bfloat16 [768], replicated, may hold values from 0.5 to 1.5
- router_query: bfloat16 [768], replicated, may hold values from -0.15625 to 0.15625
- router_key: bfloat16 [768], replicated, may hold values from -0.15625 to 0.15625
- wq_light: bfloat16 [768, 512], P(None, 'branch'), may hold values from -0.21875 to 0.21875
- wk_light: bfloat16 [768, 512], P(None, 'branch'), may hold values from -0.21875 to 0.21875
- wv_light: bfloat16 [768, 512], P(None, 'branch'), may hold values from -0.21875 to 0.21875
- wo_light: bfloat16 [768, 512], P(None, 'branch'), may hold values from -0.75 to 0.75
- wq_heavy: bfloat16 [768, 768], P(None, 'branch'), may hold values from -0.21875 to 0.21875
- wk_heavy: bfloat16 [768, 768], P(None, 'branch'), may hold values from -0.21875 to 0.21875
- wv_heavy: bfloat16 [768, 768], P(None, 'branch'), may hold values from -0.21875 to 0.21875
- wo_heavy: bfloat16 [768, 768], P(None, 'branch'), may hold values from -0.875 to 0.875
- gain_ffn: bfloat16 [768], replicated, may hold values from 0.5 to 1.5
- router_ffn: bfloat16 [768], replicated, may hold values from -0.15625 to 0.15625
- gate_light: bfloat16 [768, 1024], P(None, 'branch'), may hold values from -0.21875 to 0.21875
- up_light: bfloat16 [768, 1024], P(None, 'branch'), may hold values from -0.21875 to 0.21875
- down_light: bfloat16 [768, 1024], P(None, 'branch'), may hold values from -0.1875 to 0.1875
- gate_heavy: bfloat16 [768, 4096], P(None, 'branch'), may hold values from -0.21875 to 0.21875
- up_heavy: bfloat16 [768, 4096], P(None, 'branch'), may hold values from -0.21875 to 0.21875
- down_heavy: bfloat16 [768, 4096], P(None, 'branch'), may hold values from -0.09375 to 0.09375
Outputs:
- mixed: float32 [2, 4096, 768], P(None, 'seq', 'branch')
- grad_tokens: float32 [2, 4096, 768], P(None, 'seq')
- grad_gain_attn: float32 [768], P('seq')
- grad_router_query: float32 [768], P('seq')
- grad_router_key: float32 [768], P('seq')
- grad_wq_light: float32 [768, 512], P('seq', 'branch')
- grad_wk_light: float32 [768, 512], P('seq', 'branch')
- grad_wv_light: float32 [768, 512], P('seq', 'branch')
- grad_wo_light: float32 [768, 512], P('seq', 'branch')
- grad_wq_heavy: float32 [768, 768], P('seq', 'branch')
- grad_wk_heavy: float32 [768, 768], P('seq', 'branch')
- grad_wv_heavy: float32 [768, 768], P('seq', 'branch')
- grad_wo_heavy: float32 [768, 768], P('seq', 'branch')
- grad_gain_ffn: float32 [768], P('seq')
- grad_router_ffn: float32 [768], P('seq')
- grad_gate_light: float32 [768, 1024], P('seq', 'branch')
- grad_up_light: float32 [768, 1024], P('seq', 'branch')
- grad_down_light: float32 [768, 1024], P('seq', 'branch')
- grad_gate_heavy: float32 [768, 4096], P('seq', 'branch')
- grad_up_heavy: float32 [768, 4096], P('seq', 'branch')
- grad_down_heavy: float32 [768, 4096], P('seq', 'branch')
Inputs may be any that keep to these rules, and one draw needn't show every extreme that they name: `lengths`: one document, a different one from seed to seed, has exactly 4096 tokens; every other one has at most 3584. `query_index`: slots k * 64 to (k + 1) * 64 - 1 of a document hold distinct positions from k * 512 to (k + 1) * 512 - 1 that are below the document's length, as many as one eighth of that range's positions below the length, rounded up, always including the last such position; the other slots hold -1. `key_index`: built as query_index, drawn independently.
All inputs are finite; a program needn't handle non-finite values.
Results may differ from a plain program's by a relative error of at most 0.02.
Values may be sent and summed in bfloat16 or wider, within the bound.
A program may use at most 192 MiB of HBM per device.

v0:
```python
import math

import jax
import jax.numpy as jnp
from jax import lax
from jax.sharding import PartitionSpec as P

HD = 64
WINDOW = 128


highest = lax.Precision.HIGHEST
masked_value = -1000000000.0
epsilon = 1e-06


def with_halo(cells, sides, width):
    for axis, dim in sides:
        count = lax.axis_size(axis)
        ends = count - 1
        head = lax.slice_in_dim(cells, 0, width, axis=dim)
        tail = lax.slice_in_dim(cells, cells.shape[dim] - width, cells.shape[dim], axis=dim)
        cells = jnp.concatenate(
            [
                lax.ppermute(tail, axis, [(i, (i + 1) % count) for i in range(ends)]),
                cells,
                lax.ppermute(head, axis, [((i + 1) % count, i) for i in range(ends)]),
            ],
            axis=dim,
        )
    return cells


def project(operand, matrix):
    return jnp.einsum("dsc,ch->dsh", operand, matrix, preferred_element_type=jnp.float32)


def unproject(operand, matrix):
    return jnp.einsum("dsh,ch->dsc", operand, matrix, preferred_element_type=jnp.float32)


def weight_grad(operand, gradient):
    return jnp.einsum("dsc,dsh->ch", operand, gradient, preferred_element_type=jnp.float32)


def pick_rows(selector, values):
    return jnp.einsum("drs,dsc->drc", selector, values, precision=highest)


def put_rows(selector, values):
    return jnp.einsum("drs,drc->dsc", selector, values, precision=highest)


def pick_scalar(selector, values):
    return jnp.einsum("drs,ds->dr", selector, values, precision=highest)


def put_scalar(selector, values):
    return jnp.einsum("drs,dr->ds", selector, values, precision=highest)


def split_heads(values):
    return values.reshape(values.shape[0], values.shape[1], -1, HD)


def attention_scores(queries, keys, mask_bias):
    raw_scores = jnp.einsum("dqhe,dkhe->dhqk", queries, keys, preferred_element_type=jnp.float32)
    return raw_scores * HD ** (-0.5) + mask_bias


def forward_attention(queries, keys, values, mask_bias):
    scores = attention_scores(queries, keys, mask_bias)
    highest_score = jnp.max(scores, axis=-1, keepdims=True)
    exponent = jnp.exp(scores - highest_score)
    totals = jnp.sum(exponent, axis=-1, keepdims=True)
    probs_low = (exponent / totals).astype(jnp.bfloat16)
    result = jnp.einsum("dhqk,dkhe->dqhe", probs_low, values, preferred_element_type=jnp.float32)
    result = result.reshape(result.shape[0], result.shape[1], -1).astype(jnp.bfloat16)
    return (result, highest_score + jnp.log(totals))


def score_grads(queries, keys, values, mask_bias, logsum, grad_out, row_delta):
    probs = jnp.exp(attention_scores(queries, keys, mask_bias) - logsum)
    grad_probs = jnp.einsum("dqhe,dkhe->dhqk", grad_out, values, preferred_element_type=jnp.float32)
    row_delta = jnp.sum(grad_probs * probs, axis=-1, keepdims=True)
    grad_raw = (probs * (grad_probs - row_delta) * HD ** (-0.5)).astype(jnp.bfloat16)
    return (grad_raw, probs.astype(jnp.bfloat16), row_delta)


def contract_query(grad_raw, keys):
    result = jnp.einsum("dhqk,dkhe->dqhe", grad_raw, keys, preferred_element_type=jnp.float32)
    return result.reshape(result.shape[0], result.shape[1], -1)


def contract_key(grad_raw, queries):
    result = jnp.einsum("dhqk,dqhe->dkhe", grad_raw, queries, preferred_element_type=jnp.float32)
    return result.reshape(result.shape[0], result.shape[1], -1)


def geglu_back(gate_vals, up_vals, grad_mid):
    activated, gelu_pull = jax.vjp(jax.nn.gelu, gate_vals.astype(jnp.float32))
    grad_gate = gelu_pull(grad_mid * up_vals.astype(jnp.float32))[0].astype(jnp.bfloat16)
    grad_up = (grad_mid * activated).astype(jnp.bfloat16)
    return (grad_gate, grad_up)


def geglu(gate_vals, up_vals):
    return (jax.nn.gelu(gate_vals.astype(jnp.float32)) * up_vals.astype(jnp.float32)).astype(
        jnp.bfloat16
    )


def shards(
    tokens,
    cotangent,
    lengths,
    query_index,
    key_index,
    gain_attn,
    router_query,
    router_key,
    wq_light,
    wk_light,
    wv_light,
    wo_light,
    wq_heavy,
    wk_heavy,
    wv_heavy,
    wo_heavy,
    gain_ffn,
    router_ffn,
    gate_light,
    up_light,
    down_light,
    gate_heavy,
    up_heavy,
    down_heavy,
):
    documents, local_len, model_width = tokens.shape
    radius = WINDOW // 2
    block_rows = math.gcd(local_len, 512)
    key_span = block_rows + 2 * radius
    offset = lax.axis_index("seq") * local_len
    positions = offset + jnp.arange(local_len, dtype=jnp.int32)
    valid_rows = (positions[None, :] < lengths[:, None]).astype(jnp.float32)[:, :, None]
    pick_query = (query_index[:, :, None] == positions[None, None, :]).astype(jnp.float32)
    pick_key = (key_index[:, :, None] == positions[None, None, :]).astype(jnp.float32)
    inputs = tokens.astype(jnp.float32)
    inv_attn = lax.rsqrt(jnp.mean(inputs * inputs, axis=-1, keepdims=True) + epsilon)
    unit_attn = inputs * inv_attn
    gain_attn_f = gain_attn.astype(jnp.float32)
    normed = unit_attn * gain_attn_f
    normed_low = normed.astype(jnp.bfloat16)
    light_q = project(normed_low, wq_light).astype(jnp.bfloat16)
    light_k = project(normed_low, wk_light).astype(jnp.bfloat16)
    light_v = project(normed_low, wv_light).astype(jnp.bfloat16)
    light_width = light_q.shape[2]
    rim_block = with_halo(jnp.concatenate([light_k, light_v], axis=2), (("seq", 1),), radius)
    wide_k = split_heads(rim_block[:, :, :light_width])
    wide_v = split_heads(rim_block[:, :, light_width:])
    heads_q = split_heads(light_q)
    key_pos = offset - radius + jnp.arange(local_len + 2 * radius, dtype=jnp.int32)
    in_window = (jnp.abs(positions[:, None] - key_pos[None, :]) <= radius)[None]
    in_window = (
        in_window
        & (key_pos[None, None, :] >= 0)
        & (key_pos[None, None, :] < lengths[:, None, None])
    )
    light_bias = jnp.where(in_window, 0.0, masked_value)[:, None]
    piece_out, piece_lse = forward_attention(heads_q, wide_k, wide_v, light_bias)
    router_query_f = router_query.astype(jnp.float32)
    router_key_f = router_key.astype(jnp.float32)
    score_query = pick_scalar(
        pick_query,
        jax.nn.sigmoid(jnp.einsum("dsc,c->ds", normed, router_query_f, precision=highest)),
    )
    score_key = pick_scalar(
        pick_key, jax.nn.sigmoid(jnp.einsum("dsc,c->ds", normed, router_key_f, precision=highest))
    )
    heavy_in = pick_rows(pick_query, normed).astype(jnp.bfloat16)
    key_rows = pick_rows(pick_key, normed)
    key_in = key_rows.astype(jnp.bfloat16)
    scaled_in = (key_rows * score_key[:, :, None]).astype(jnp.bfloat16)
    heavy_q = project(heavy_in, wq_heavy).astype(jnp.bfloat16)
    heavy_k = project(key_in, wk_heavy).astype(jnp.bfloat16)
    heavy_v = project(scaled_in, wv_heavy).astype(jnp.bfloat16)
    heavy_width = heavy_q.shape[2]
    key_alive = (key_index >= 0).astype(jnp.bfloat16)
    routed_kv, alive_all = (
        lax.all_gather(jnp.concatenate([heavy_k, heavy_v], axis=2), "seq", axis=1, tiled=True),
        lax.all_gather(key_alive, "seq", axis=1, tiled=True),
    )
    all_k = routed_kv[:, :, :heavy_width]
    all_v = routed_kv[:, :, heavy_width:]
    heavy_bias = jnp.where(alive_all > 0, 0.0, masked_value)[:, None, None, :]
    heavy_out, heavy_lse = forward_attention(
        split_heads(heavy_q), split_heads(all_k), split_heads(all_v), heavy_bias
    )
    heavy_proj = unproject(heavy_out, wo_heavy)
    light_attn = unproject(piece_out, wo_light) * valid_rows
    heavy_attn = put_rows(pick_query, heavy_proj * score_query[:, :, None])
    attn_total = lax.psum((light_attn + heavy_attn).astype(jnp.bfloat16), "branch").astype(
        jnp.float32
    )
    hidden = inputs + attn_total
    inv_ffn = lax.rsqrt(jnp.mean(hidden * hidden, axis=-1, keepdims=True) + epsilon)
    unit_ffn = hidden * inv_ffn
    gain_ffn_f = gain_ffn.astype(jnp.float32)
    normed_ffn = unit_ffn * gain_ffn_f
    ffn_low = normed_ffn.astype(jnp.bfloat16)
    gate_l = project(ffn_low, gate_light).astype(jnp.bfloat16)
    up_l = project(ffn_low, up_light).astype(jnp.bfloat16)
    middle_l = geglu(gate_l, up_l)
    light_ffn = unproject(middle_l, down_light) * valid_rows
    router_ffn_f = router_ffn.astype(jnp.float32)
    score_ffn = pick_scalar(
        pick_query,
        jax.nn.sigmoid(jnp.einsum("dsc,c->ds", normed_ffn, router_ffn_f, precision=highest)),
    )
    ffn_rows = pick_rows(pick_query, normed_ffn).astype(jnp.bfloat16)
    gate_h = project(ffn_rows, gate_heavy).astype(jnp.bfloat16)
    up_h = project(ffn_rows, up_heavy).astype(jnp.bfloat16)
    middle_h = geglu(gate_h, up_h)
    heavy_fproj = unproject(middle_h, down_heavy)
    heavy_ffn = put_rows(pick_query, heavy_fproj * score_ffn[:, :, None])
    share = model_width // lax.axis_size("branch")
    own_cols = lax.axis_index("branch") * share
    mixed = lax.dynamic_slice_in_dim(hidden, own_cols, share, 2) + lax.psum_scatter(
        (light_ffn + heavy_ffn).astype(jnp.bfloat16), "branch", scatter_dimension=2, tiled=True
    ).astype(jnp.float32)
    grad_out = cotangent.astype(jnp.float32)
    grad_light = (grad_out * valid_rows).astype(jnp.bfloat16)
    grad_down_light = weight_grad(grad_light, middle_l)
    grad_gate_l, grad_up_l = geglu_back(gate_l, up_l, project(grad_light, down_light))
    grad_gate_light = weight_grad(ffn_low, grad_gate_l)
    grad_up_light = weight_grad(ffn_low, grad_up_l)
    grad_rows = pick_rows(pick_query, grad_out)
    grad_heavy = (grad_rows * score_ffn[:, :, None]).astype(jnp.bfloat16)
    score_ffn_part = jnp.sum(grad_rows * heavy_fproj, axis=-1)
    grad_down_heavy = weight_grad(grad_heavy, middle_h)
    grad_gate_h, grad_up_h = geglu_back(gate_h, up_h, project(grad_heavy, down_heavy))
    grad_gate_heavy = weight_grad(ffn_rows, grad_gate_h)
    grad_up_heavy = weight_grad(ffn_rows, grad_up_h)
    heavy_ffn_rows = unproject(grad_gate_h, gate_heavy) + unproject(grad_up_h, up_heavy)
    ffn_part = (
        unproject(grad_gate_l, gate_light)
        + unproject(grad_up_l, up_light)
        + put_rows(pick_query, heavy_ffn_rows)
    )
    grad_normed_ffn, grad_score_ffn = (
        lax.psum(ffn_part.astype(jnp.bfloat16), "branch").astype(jnp.float32),
        lax.psum(score_ffn_part.astype(jnp.bfloat16), "branch").astype(jnp.float32),
    )
    pre_ffn = put_scalar(pick_query, grad_score_ffn * score_ffn * (1.0 - score_ffn))
    grad_normed_ffn = grad_normed_ffn + pre_ffn[:, :, None] * router_ffn_f
    grad_router_ffn = jnp.einsum("ds,dsc->c", pre_ffn, normed_ffn, precision=highest)
    grad_gain_ffn = jnp.sum(grad_normed_ffn * unit_ffn, axis=(0, 1))
    grad_unit_f = grad_normed_ffn * gain_ffn_f
    grad_hidden = grad_out + inv_ffn * (
        grad_unit_f - unit_ffn * jnp.mean(grad_unit_f * unit_ffn, axis=-1, keepdims=True)
    )
    grad_light_attn = (grad_hidden * valid_rows).astype(jnp.bfloat16)
    grad_wo_light = weight_grad(grad_light_attn, piece_out)
    grad_light_out = split_heads(project(grad_light_attn, wo_light).astype(jnp.bfloat16))
    wide_grad = jnp.zeros((documents, local_len + 2 * radius, 2 * light_width), jnp.float32)
    light_raw, light_plow, unused_delta = score_grads(
        heads_q, wide_k, wide_v, light_bias, piece_lse, grad_light_out, None
    )
    query_pieces = contract_query(light_raw, wide_k)
    key_terms = jnp.concatenate(
        [contract_key(light_raw, heads_q), contract_key(light_plow, grad_light_out)], axis=2
    )
    wide_grad = wide_grad.at[:, 0:key_span].add(key_terms)
    grad_light_q = query_pieces.astype(jnp.bfloat16)
    outer_rims = jnp.concatenate(
        [wide_grad[:, :radius], wide_grad[:, radius + local_len :]], axis=1
    )
    returned = with_halo(outer_rims.astype(jnp.bfloat16), (("seq", 1),), radius).astype(
        outer_rims.dtype
    )
    inner = wide_grad[:, radius : radius + local_len]
    inner = inner + jnp.pad(returned[:, :radius], ((0, 0), (0, local_len - radius), (0, 0)))
    inner = inner + jnp.pad(returned[:, 3 * radius :], ((0, 0), (local_len - radius, 0), (0, 0)))
    grad_light_k = inner[:, :, :light_width].astype(jnp.bfloat16)
    grad_light_v = inner[:, :, light_width:].astype(jnp.bfloat16)
    grad_wq_light = weight_grad(normed_low, grad_light_q)
    grad_wk_light = weight_grad(normed_low, grad_light_k)
    grad_wv_light = weight_grad(normed_low, grad_light_v)
    light_part = (
        unproject(grad_light_q, wq_light)
        + unproject(grad_light_k, wk_light)
        + unproject(grad_light_v, wv_light)
    )
    grad_hrows = pick_rows(pick_query, grad_hidden)
    grad_heavy_attn = (grad_hrows * score_query[:, :, None]).astype(jnp.bfloat16)
    score_query_part = jnp.sum(grad_hrows * heavy_proj, axis=-1)
    grad_wo_heavy = weight_grad(grad_heavy_attn, heavy_out)
    grad_heavy_out = project(grad_heavy_attn, wo_heavy).astype(jnp.bfloat16)
    heavy_raw, heavy_plow, heavy_delta = score_grads(
        split_heads(heavy_q),
        split_heads(all_k),
        split_heads(all_v),
        heavy_bias,
        heavy_lse,
        split_heads(grad_heavy_out),
        None,
    )
    grad_heavy_q = contract_query(heavy_raw, split_heads(all_k)).astype(jnp.bfloat16)
    every_kv = jnp.concatenate(
        [
            contract_key(heavy_raw, split_heads(heavy_q)),
            contract_key(heavy_plow, split_heads(grad_heavy_out)),
        ],
        axis=2,
    )
    own_kv = lax.psum_scatter(every_kv, "seq", scatter_dimension=1, tiled=True)
    grad_heavy_k = own_kv[:, :, :heavy_width].astype(jnp.bfloat16)
    grad_heavy_v = own_kv[:, :, heavy_width:].astype(jnp.bfloat16)
    grad_scaled = unproject(grad_heavy_v, wv_heavy)
    score_key_part = jnp.sum(grad_scaled * key_rows, axis=-1)
    grad_key_rows = unproject(grad_heavy_k, wk_heavy) + grad_scaled * score_key[:, :, None]
    grad_wq_heavy = weight_grad(heavy_in, grad_heavy_q)
    grad_wk_heavy = weight_grad(key_in, grad_heavy_k)
    grad_wv_heavy = weight_grad(scaled_in, grad_heavy_v)
    attn_part = (
        light_part
        + put_rows(pick_query, unproject(grad_heavy_q, wq_heavy))
        + put_rows(pick_key, grad_key_rows)
    )
    grad_normed, grad_score_query, grad_score_key = (
        lax.psum(attn_part.astype(jnp.bfloat16), "branch").astype(jnp.float32),
        lax.psum(score_query_part.astype(jnp.bfloat16), "branch").astype(jnp.float32),
        lax.psum(score_key_part.astype(jnp.bfloat16), "branch").astype(jnp.float32),
    )
    pre_query = put_scalar(pick_query, grad_score_query * score_query * (1.0 - score_query))
    pre_key = put_scalar(pick_key, grad_score_key * score_key * (1.0 - score_key))
    grad_normed = (
        grad_normed + pre_query[:, :, None] * router_query_f + pre_key[:, :, None] * router_key_f
    )
    grad_router_query = jnp.einsum("ds,dsc->c", pre_query, normed, precision=highest)
    grad_router_key = jnp.einsum("ds,dsc->c", pre_key, normed, precision=highest)
    grad_gain_attn = jnp.sum(grad_normed * unit_attn, axis=(0, 1))
    grad_unit_a = grad_normed * gain_attn_f
    grad_tokens = grad_hidden + inv_attn * (
        grad_unit_a - unit_attn * jnp.mean(grad_unit_a * unit_attn, axis=-1, keepdims=True)
    )
    (
        grad_gain_attn,
        grad_router_query,
        grad_router_key,
        grad_wq_light,
        grad_wk_light,
        grad_wv_light,
        grad_wo_light,
        grad_wq_heavy,
        grad_wk_heavy,
        grad_wv_heavy,
        grad_wo_heavy,
        grad_gain_ffn,
        grad_router_ffn,
        grad_gate_light,
        grad_up_light,
        grad_down_light,
        grad_gate_heavy,
        grad_up_heavy,
        grad_down_heavy,
    ) = (
        lax.psum_scatter(grad_gain_attn, "seq", scatter_dimension=0, tiled=True),
        lax.psum_scatter(grad_router_query, "seq", scatter_dimension=0, tiled=True),
        lax.psum_scatter(grad_router_key, "seq", scatter_dimension=0, tiled=True),
        lax.psum_scatter(grad_wq_light, "seq", scatter_dimension=0, tiled=True),
        lax.psum_scatter(grad_wk_light, "seq", scatter_dimension=0, tiled=True),
        lax.psum_scatter(grad_wv_light, "seq", scatter_dimension=0, tiled=True),
        lax.psum_scatter(grad_wo_light, "seq", scatter_dimension=0, tiled=True),
        lax.psum_scatter(grad_wq_heavy, "seq", scatter_dimension=0, tiled=True),
        lax.psum_scatter(grad_wk_heavy, "seq", scatter_dimension=0, tiled=True),
        lax.psum_scatter(grad_wv_heavy, "seq", scatter_dimension=0, tiled=True),
        lax.psum_scatter(grad_wo_heavy, "seq", scatter_dimension=0, tiled=True),
        lax.psum_scatter(grad_gain_ffn, "seq", scatter_dimension=0, tiled=True),
        lax.psum_scatter(grad_router_ffn, "seq", scatter_dimension=0, tiled=True),
        lax.psum_scatter(grad_gate_light, "seq", scatter_dimension=0, tiled=True),
        lax.psum_scatter(grad_up_light, "seq", scatter_dimension=0, tiled=True),
        lax.psum_scatter(grad_down_light, "seq", scatter_dimension=0, tiled=True),
        lax.psum_scatter(grad_gate_heavy, "seq", scatter_dimension=0, tiled=True),
        lax.psum_scatter(grad_up_heavy, "seq", scatter_dimension=0, tiled=True),
        lax.psum_scatter(grad_down_heavy, "seq", scatter_dimension=0, tiled=True),
    )
    return (
        mixed,
        grad_tokens,
        grad_gain_attn,
        grad_router_query,
        grad_router_key,
        grad_wq_light,
        grad_wk_light,
        grad_wv_light,
        grad_wo_light,
        grad_wq_heavy,
        grad_wk_heavy,
        grad_wv_heavy,
        grad_wo_heavy,
        grad_gain_ffn,
        grad_router_ffn,
        grad_gate_light,
        grad_up_light,
        grad_down_light,
        grad_gate_heavy,
        grad_up_heavy,
        grad_down_heavy,
    )


def solution(mesh):
    return jax.shard_map(
        shards,
        mesh=mesh,
        in_specs=(
            P(None, "seq", None),
            P(None, "seq", None),
            P(),
            P(None, "seq"),
            P(None, "seq"),
            P(),
            P(),
            P(),
            P(None, "branch"),
            P(None, "branch"),
            P(None, "branch"),
            P(None, "branch"),
            P(None, "branch"),
            P(None, "branch"),
            P(None, "branch"),
            P(None, "branch"),
            P(),
            P(),
            P(None, "branch"),
            P(None, "branch"),
            P(None, "branch"),
            P(None, "branch"),
            P(None, "branch"),
            P(None, "branch"),
        ),
        out_specs=(
            P(None, "seq", "branch"),
            P(None, "seq", None),
            P("seq"),
            P("seq"),
            P("seq"),
            P("seq", "branch"),
            P("seq", "branch"),
            P("seq", "branch"),
            P("seq", "branch"),
            P("seq", "branch"),
            P("seq", "branch"),
            P("seq", "branch"),
            P("seq", "branch"),
            P("seq"),
            P("seq"),
            P("seq", "branch"),
            P("seq", "branch"),
            P("seq", "branch"),
            P("seq", "branch"),
            P("seq", "branch"),
            P("seq", "branch"),
        ),
        check_vma=False,
    )
```

profile of v0, /device:TPU:0, one launch (start us, length us, event | category | flops | bytes accessed | tf_op | source)
XLA Modules:
  0.0 921.0 jit_solution(9394069685457355142)
XLA Ops:
  13.8 3.0 collective-permute-start
  19.3 14.6 %all-gather = bf16[8,64,2]{1,2,0:T(2,128)(2,1)S(1)} all-gather(bf16[1,64,2]{1,2,0:T(2,128)(2,1)S(1)} %fusion.295), channel_id=1, replica_groups=mesh['branch'=4,'seq'=8] {'seq'}, dimensions={0}, use_global_device_ids=true | all-gather | bytes 2304 | tf_op jit(solution)/shard_map/all_gather | solution.py:191
  52.9 16.4 %all_gather.6 = bf16[2,512,384]{2,1,0:T(8,128)(2,1)S(1)} all-gather(bf16[2,64,384]{2,1,0:T(8,128)(2,1)S(1)} %pad_maximum_fusion.5), channel_id=1, replica_groups=mesh['branch'=4,'seq'=8] {'seq'}, dimensions={1}, use_global_device_ids=true | all-gather | bytes 884736 | tf_op jit(solution)/shard_map/all_gather | solution.py:190
  86.0 3.0 add_convert_fusion.3
  94.6 2.6 fusion.165
  97.2 3.1 fusion.91
  100.3 48.1 %all-reduce.15.cloned.1.call-done = bf16[2,512,768]{2,1,0:T(8,128)(2,1)} async-done(((bf16[2,512,768]{2,1,0:T(8,128)(2,1)}), bf16[2,512,768]{2,1,0:T(8,128)(2,1)}) %all-reduce.15.cloned.1.call-update) | async-done | bytes 1572880 | tf_op jit(solution)/shard_map/psum | solution.py:202
  170.1 9.2 psum.44
  184.0 3.5 add_convert_fusion.2
  187.5 4.9 copy.122
  192.5 35.0 %all-reduce.17.cloned.1.call-done = bf16[2,512,768]{2,1,0:T(8,128)(2,1)} async-done(((bf16[2,512,768]{2,1,0:T(8,128)(2,1)}), bf16[2,512,768]{2,1,0:T(8,128)(2,1)}) %all-reduce.17.cloned.1.call-update) | async-done | bytes 1572880 | tf_op jit(solution)/shard_map/psum | solution.py:251
  227.6 4.7 multiply_reduce_fusion.1
  244.3 4.7 fusion.150
  254.0 3.0 pad_maximum_fusion
  257.1 4.4 fusion.39
  263.7 4.3 fusion.317
  268.0 19.9 %fusion.25 = f32[2,2,64,640]{3,2,1,0:T(8,128)} fusion(bf16[2,512,2,64]{1,3,2,0:T(8,128)(2,1)} %bitcast.302, f32[2,2,512,640]{3,2,1,0:T(8,128)} %fusion.317, f32[2,2,512,640]{3,2,1,0:T(8,128)} %copy-done.4, f32[2,2,512]{2,1,0:T(2,128)} %log_add_fusion), kind=kOutput, calls=%fused_computation.27 | convolution fusion | flops 176949888 | bytes 11411456 | tf_op jit(solution)/shard_map/dhqk,dqhe->dkhe/dot_general | solution.py:96
  296.0 4.5 convolution_convert_fusion.6
  300.5 16.0 %fusion.116 = bf16[2,2,64,512]{3,2,1,0:T(8,128)(2,1)} fusion(bf16[2,640,2,64]{1,3,2,0:T(8,128)(2,1)} %bitcast.287, f32[2,2,512,640]{3,2,1,0:T(8,128)} %fusion.317, f32[2,2,512,640]{3,2,1,0:T(8,128)} %copy-done.4, f32[2,2,512]{2,1,0:T(2,128)} %log_add_fusion), kind=kOutput, calls=%fused_computation.145 | convolution fusion | flops 177080960 | bytes 11083776 | tf_op jit(solution)/shard_map/dhqk,dkhe->dqhe/dot_general | solution.py:91
  317.7 3.4 fusion.229
  321.1 3.2 fusion.157
  333.8 7.8 add_convert_fusion
  341.6 3.5 convolution_bitcast_fusion.3
  345.2 3.1 convolution_bitcast_fusion.4
  348.3 4.4 fusion.98
  352.8 3.5 convolution_bitcast_fusion.9
  356.7 2.6 convolution_bitcast_fusion.12
  373.6 3.4 convolution_bitcast_fusion
  377.1 3.2 convolution_bitcast_fusion.2
  380.4 3.3 convolution_bitcast_fusion.1
  388.5 9.1 all-reduce.9
  402.0 29.2 %all-reduce.19.cloned.1.call-done = (bf16[2,512,768]{1,0,2:T(2,128)(2,1)}, bf16[2,512,768]{2,1,0:T(8,128)(2,1)}) async-done(((bf16[2,512,768]{1,0,2:T(2,128)(2,1)}, bf16[2,512,768]{2,1,0:T(8,128)(2,1)}), (bf16[2,512,768]{1,0,2:T(2,128)(2,1)}, bf16[2,512,768]{2,1,0:T(8,128)(2,1)})) %all-reduce.19.cloned.1.call-update) | async-done | bytes 3145744
  431.2 2.9 fusion.35
  434.2 28.8 %all-reduce.8 = (f32[768]{0:T(1024)S(1)}, f32[768]{0:T(1024)S(1)}, f32[768]{0:T(1024)S(1)}, f32[768]{0:T(1024)S(1)}, f32[768]{0:T(1024)S(1)}) all-reduce(f32[768]{0:T(1024)S(1)} %get-tuple-element.106, f32[768]{0:T(1024)S(1)} %fusion.131, f32[768]{0:T(1024)S(1)} %fusion.134, ...), channel_id=4, replica_groups=mesh['branch'=4,'seq'=8] {'seq'}, use_global_device_ids=true, to_apply=%region_22.23.clone | all-reduce | flops 3840 | bytes 30720
  470.6 4.4 fusion.34
  475.0 23.1 %reduce-scatter.34.cloned.1.call-done = f32[96,256]{1,0:T(8,128)} async-done(((f32[768,256]{1,0:T(8,128)}), f32[96,256]{1,0:T(8,128)}) %reduce-scatter.34.cloned.1.call-update) | async-done | bytes 98320 | tf_op jit(solution)/shard_map/reduce_scatter | solution.py:381
  498.1 32.7 %reduce-scatter.38.cloned.1.call-done = f32[96,256]{1,0:T(8,128)} async-done(((f32[768,256]{1,0:T(8,128)}), f32[96,256]{1,0:T(8,128)}) %reduce-scatter.38.cloned.1.call-update) | async-done | bytes 98320 | tf_op jit(solution)/shard_map/reduce_scatter | solution.py:383
  530.8 31.8 %reduce-scatter.24.cloned.1.call-done = f32[96,128]{1,0:T(8,128)} async-done(((f32[768,128]{1,0:T(8,128)}), f32[96,128]{1,0:T(8,128)}) %reduce-scatter.24.cloned.1.call-update) | async-done | bytes 49168 | tf_op jit(solution)/shard_map/reduce_scatter | solution.py:374
  562.7 31.8 %reduce-scatter.18.cloned.1.call-done = f32[96,128]{1,0:T(8,128)} async-done(((f32[768,128]{1,0:T(8,128)}), f32[96,128]{1,0:T(8,128)}) %reduce-scatter.18.cloned.1.call-update) | async-done | bytes 49168 | tf_op jit(solution)/shard_map/reduce_scatter | solution.py:371
  594.5 31.5 %reduce-scatter.20.cloned.1.call-done = f32[96,128]{1,0:T(8,128)} async-done(((f32[768,128]{1,0:T(8,128)}), f32[96,128]{1,0:T(8,128)}) %reduce-scatter.20.cloned.1.call-update) | async-done | bytes 49168 | tf_op jit(solution)/shard_map/reduce_scatter | solution.py:372
  626.0 31.8 %reduce-scatter.22.cloned.1.call-done = f32[96,128]{1,0:T(8,128)} async-done(((f32[768,128]{1,0:T(8,128)}), f32[96,128]{1,0:T(8,128)}) %reduce-scatter.22.cloned.1.call-update) | async-done | bytes 49168 | tf_op jit(solution)/shard_map/reduce_scatter | solution.py:373
  657.8 32.5 %reduce-scatter.32.cloned.1.call-done = f32[96,192]{1,0:T(8,128)} async-done(((f32[768,192]{1,0:T(8,128)}), f32[96,192]{1,0:T(8,128)}) %reduce-scatter.32.cloned.1.call-update) | async-done | bytes 73744 | tf_op jit(solution)/shard_map/reduce_scatter | solution.py:378
  690.3 32.7 %reduce-scatter.26.cloned.1.call-done = f32[96,192]{1,0:T(8,128)} async-done(((f32[768,192]{1,0:T(8,128)}), f32[96,192]{1,0:T(8,128)}) %reduce-scatter.26.cloned.1.call-update) | async-done | bytes 73744 | tf_op jit(solution)/shard_map/reduce_scatter | solution.py:375
  723.0 32.5 %reduce-scatter.30.cloned.1.call-done = f32[96,192]{1,0:T(8,128)} async-done(((f32[768,192]{1,0:T(8,128)}), f32[96,192]{1,0:T(8,128)}) %reduce-scatter.30.cloned.1.call-update) | async-done | bytes 73744 | tf_op jit(solution)/shard_map/reduce_scatter | solution.py:377
  755.5 32.6 %reduce-scatter.28.cloned.1.call-done = f32[96,192]{1,0:T(8,128)} async-done(((f32[768,192]{1,0:T(8,128)}), f32[96,192]{1,0:T(8,128)}) %reduce-scatter.28.cloned.1.call-update) | async-done | bytes 73744 | tf_op jit(solution)/shard_map/reduce_scatter | solution.py:376
  788.1 41.4 %reduce-scatter.44.cloned.1.call-done = f32[96,1024]{1,0:T(8,128)} async-done(((f32[768,1024]{1,0:T(8,128)}), f32[96,1024]{1,0:T(8,128)}) %reduce-scatter.44.cloned.1.call-update) | async-done | bytes 393232 | tf_op jit(solution)/shard_map/reduce_scatter | solution.py:386
  829.5 42.2 %reduce-scatter.40.cloned.1.call-done = f32[96,1024]{1,0:T(8,128)} async-done(((f32[768,1024]{1,0:T(8,128)}), f32[96,1024]{1,0:T(8,128)}) %reduce-scatter.40.cloned.1.call-update) | async-done | bytes 393232 | tf_op jit(solution)/shard_map/reduce_scatter | solution.py:384
  871.7 42.2 %reduce-scatter.42.cloned.1.call-done = f32[96,1024]{1,0:T(8,128)} async-done(((f32[768,1024]{1,0:T(8,128)}), f32[96,1024]{1,0:T(8,128)}) %reduce-scatter.42.cloned.1.call-update) | async-done | bytes 393232 | tf_op jit(solution)/shard_map/reduce_scatter | solution.py:385
  (358 shorter events, 144.3 us)
Async XLA Ops:
  7.2 148.5 %copy-start = (bf16[768,1024]{1,0:T(8,128)(2,1)S(1)}, bf16[768,1024]{1,0:T(8,128)(2,1)}, u32[]{:S(2)}) copy-start(bf16[768,1024]{1,0:T(8,128)(2,1)} %param.49) | copy-start | bytes 4718596
  7.2 141.2 %all-reduce.15.cloned.1.call-start = ((), (), s32[]{:S(2)}) async-start(), calls=%async_computation.15 | async-start | bytes 3145728 | tf_op jit(solution)/shard_map/psum | solution.py:202
  8.1 39.1 %copy-start.57 = (f32[768]{0:T(1024)}, f32[768]{0:T(1024)S(1)}, u32[]{:S(2)}) copy-start(f32[768]{0:T(1024)S(1)} %convert_element_type.242) | copy-start | bytes 9220
  10.0 37.2 %copy-start.59 = (f32[2,512]{1,0:T(2,128)}, f32[2,512]{1,0:T(2,128)S(1)}, u32[]{:S(2)}) copy-start(f32[2,512]{1,0:T(2,128)S(1)} %add_rsqrt_fusion.1) | copy-start | bytes 12292
  10.0 8.7 copy-start.88
  10.0 8.7 copy-start.81
  10.0 8.7 copy-start.83
  13.8 65.3 %collective-permute-start = (bf16[2,64,256]{1,2,0:T(8,128)(2,1)}, bf16[2,64,256]{1,2,0:T(8,128)(2,1)}, u32[]{:S(2)}, u32[]{:S(2)}) collective-permute-start(bf16[2,64,256]{1,2,0:T(8,128)(2,1)} %get-tuple-element.127), channel_id=1, source_target_pairs={{0,1},{1,2},{2,3},{3,4},{4,5},{5,6},{6,7},{8,9},{9,10},{10,11},{11... | collective-permute-start | bytes 196616 | tf_op jit(solution)/shard_map/ppermute | solution.py:25
  16.8 62.3 %collective-permute-start.1 = (bf16[2,64,256]{1,2,0:T(8,128)(2,1)}, bf16[2,64,256]{1,2,0:T(8,128)(2,1)}, u32[]{:S(2)}, u32[]{:S(2)}) collective-permute-start(bf16[2,64,256]{1,2,0:T(8,128)(2,1)} %get-tuple-element.128), channel_id=1, source_target_pairs={{1,0},{2,1},{3,2},{4,3},{5,4},{6,5},{7,6},{9,8},{10,9},{11,10},{12... | collective-permute-start | bytes 196616 | tf_op jit(solution)/shard_map/ppermute | solution.py:27
  36.5 5.5 copy-start.85
  38.8 6.0 copy-start.30
  47.2 5.3 copy-start.31
  47.2 5.3 copy-start.78
  52.2 22.2 %copy-start.74 = (f32[512,2]{0,1:T(2,128)S(1)}, f32[512,2]{0,1:T(2,128)}, u32[]{:S(2)}) copy-start(f32[512,2]{0,1:T(2,128)} %reshape.333) | copy-start | bytes 12292
  78.6 7.4 copy-start.16
  89.0 138.5 %all-reduce.17.cloned.1.call-start = ((), (), s32[]{:S(2)}) async-start(), calls=%async_computation.16 | async-start | bytes 3145728 | tf_op jit(solution)/shard_map/psum | solution.py:251
  150.6 7.9 copy-start.55
  166.3 163.5 %reduce-scatter.16.cloned.1.call-start = ((), (), s32[]{:S(2)}) async-start(), calls=%async_computation.17 | async-start | bytes 1769472 | tf_op jit(solution)/shard_map/reduce_scatter | solution.py:316
  184.0 43.5 %copy-start.6 = (bf16[2,512,768]{2,1,0:T(8,128)(2,1)S(1)}, bf16[2,512,768]{2,1,0:T(8,128)(2,1)}, u32[]{:S(2)}) copy-start(bf16[2,512,768]{2,1,0:T(8,128)(2,1)} %all-reduce.15.cloned.1.call-done) | copy-start | bytes 4718596
  184.0 43.5 %copy-start.54 = (f32[768]{0:T(1024)S(1)}, f32[768]{0:T(1024)}, u32[]{:S(2)}) copy-start(f32[768]{0:T(1024)} %convert_element_type.265) | copy-start | bytes 9220
  184.0 43.5 %copy-start.56 = (f32[2,512]{1,0:T(2,128)S(1)}, f32[2,512]{1,0:T(2,128)}, u32[]{:S(2)}) copy-start(f32[2,512]{1,0:T(2,128)} %copy-done.55) | copy-start | bytes 12292
  257.0 174.2 %all-reduce.19.cloned.1.call-start = ((), (), s32[]{:S(2)}) async-start(), calls=%async_computation.32 | async-start | bytes 6291456
  292.1 32.2 %collective-permute-start.2 = (bf16[2,64,256]{2,1,0:T(8,128)(2,1)}, bf16[2,64,256]{2,1,0:T(8,128)(2,1)}, u32[]{:S(2)}, u32[]{:S(2)}) collective-permute-start(bf16[2,64,256]{2,1,0:T(8,128)(2,1)} %get-tuple-element.123), channel_id=1, source_target_pairs={{0,1},{1,2},{2,3},{3,4},{4,5},{5,6},{6,7},{8,9},{9,10},{10,11},{11... | collective-permute-start | bytes 196616 | tf_op jit(solution)/shard_map/ppermute | solution.py:25
  294.5 29.8 %collective-permute-start.3 = (bf16[2,64,256]{2,1,0:T(8,128)(2,1)}, bf16[2,64,256]{2,1,0:T(8,128)(2,1)}, u32[]{:S(2)}, u32[]{:S(2)}) collective-permute-start(bf16[2,64,256]{2,1,0:T(8,128)(2,1)} %get-tuple-element.124), channel_id=1, source_target_pairs={{1,0},{2,1},{3,2},{4,3},{5,4},{6,5},{7,6},{9,8},{10,9},{11,10},{12... | collective-permute-start | bytes 196616 | tf_op jit(solution)/shard_map/ppermute | solution.py:27
  317.7 7.5 copy-start.14
  317.7 7.5 copy-start.15
  341.6 133.4 %reduce-scatter.36.cloned.1.call-start = ((), (), s32[]{:S(2)}) async-start(), calls=%async_computation.27 | async-start | bytes 884736 | tf_op jit(solution)/shard_map/reduce_scatter | solution.py:382
  345.2 153.0 %reduce-scatter.34.cloned.1.call-start = ((), (), s32[]{:S(2)}) async-start(), calls=%async_computation.26 | async-start | bytes 884736 | tf_op jit(solution)/shard_map/reduce_scatter | solution.py:381
  348.3 182.6 %reduce-scatter.38.cloned.1.call-start = ((), (), s32[]{:S(2)}) async-start(), calls=%async_computation.28 | async-start | bytes 884736 | tf_op jit(solution)/shard_map/reduce_scatter | solution.py:383
  352.7 209.9 %reduce-scatter.24.cloned.1.call-start = ((), (), s32[]{:S(2)}) async-start(), calls=%async_computation.21 | async-start | bytes 442368 | tf_op jit(solution)/shard_map/reduce_scatter | solution.py:374
  356.3 238.2 %reduce-scatter.18.cloned.1.call-start = ((), (), s32[]{:S(2)}) async-start(), calls=%async_computation.18 | async-start | bytes 442368 | tf_op jit(solution)/shard_map/reduce_scatter | solution.py:371
  359.3 266.7 %reduce-scatter.20.cloned.1.call-start = ((), (), s32[]{:S(2)}) async-start(), calls=%async_computation.19 | async-start | bytes 442368 | tf_op jit(solution)/shard_map/reduce_scatter | solution.py:372
  362.0 295.8 %reduce-scatter.22.cloned.1.call-start = ((), (), s32[]{:S(2)}) async-start(), calls=%async_computation.20 | async-start | bytes 442368 | tf_op jit(solution)/shard_map/reduce_scatter | solution.py:373
  364.6 325.7 %reduce-scatter.32.cloned.1.call-start = ((), (), s32[]{:S(2)}) async-start(), calls=%async_computation.25 | async-start | bytes 884736 | tf_op jit(solution)/shard_map/reduce_scatter | solution.py:378
  367.0 356.0 %reduce-scatter.26.cloned.1.call-start = ((), (), s32[]{:S(2)}) async-start(), calls=%async_computation.22 | async-start | bytes 884736 | tf_op jit(solution)/shard_map/reduce_scatter | solution.py:375
  369.2 386.3 %reduce-scatter.30.cloned.1.call-start = ((), (), s32[]{:S(2)}) async-start(), calls=%async_computation.24 | async-start | bytes 884736 | tf_op jit(solution)/shard_map/reduce_scatter | solution.py:377
  371.5 416.7 %reduce-scatter.28.cloned.1.call-start = ((), (), s32[]{:S(2)}) async-start(), calls=%async_computation.23 | async-start | bytes 884736 | tf_op jit(solution)/shard_map/reduce_scatter | solution.py:376
  373.6 456.0 %reduce-scatter.44.cloned.1.call-start = ((), (), s32[]{:S(2)}) async-start(), calls=%async_computation.31 | async-start | bytes 3538944 | tf_op jit(solution)/shard_map/reduce_scatter | solution.py:386
  377.0 494.7 %reduce-scatter.40.cloned.1.call-start = ((), (), s32[]{:S(2)}) async-start(), calls=%async_computation.29 | async-start | bytes 3538944 | tf_op jit(solution)/shard_map/reduce_scatter | solution.py:384
  380.4 5.9 copy-start.63
  380.4 533.5 %reduce-scatter.42.cloned.1.call-start = ((), (), s32[]{:S(2)}) async-start(), calls=%async_computation.30 | async-start | bytes 3538944 | tf_op jit(solution)/shard_map/reduce_scatter | solution.py:385
  383.7 13.8 %copy-start.77 = (f32[2,1,64]{2,1,0:T(1,128)S(1)}, f32[2,1,64]{2,1,0:T(1,128)}, u32[]{:S(2)}) copy-start(f32[2,1,64]{2,1,0:T(1,128)} %fusion.173) | copy-start | bytes 1540
  383.7 13.8 %copy-start.79 = (f32[2,1,64]{2,1,0:T(1,128)S(1)}, f32[2,1,64]{2,1,0:T(1,128)}, u32[]{:S(2)}) copy-start(f32[2,1,64]{2,1,0:T(1,128)} %fusion.188) | copy-start | bytes 1540
  383.7 13.9 %copy-start.90 = (s32[2,64]{1,0:T(2,128)S(1)}, s32[2,64]{1,0:T(2,128)}, u32[]{:S(2)}) copy-start(s32[2,64]{1,0:T(2,128)} %param.32) | copy-start | bytes 1540
  383.7 14.1 %copy-start.70 = (s32[2,64]{1,0:T(2,128)S(1)}, s32[2,64]{1,0:T(2,128)}, u32[]{:S(2)}) copy-start(s32[2,64]{1,0:T(2,128)} %param.31) | copy-start | bytes 1540
  383.7 14.4 %copy-start.60 = (f32[2,512]{1,0:T(2,128)S(1)}, f32[2,512]{1,0:T(2,128)}, u32[]{:S(2)}) copy-start(f32[2,512]{1,0:T(2,128)} %copy-done.59) | copy-start | bytes 12292
  400.1 34.1 %copy-start.72 = (f32[768]{0:T(1024)S(1)}, f32[768]{0:T(1024)}, u32[]{:S(2)}) copy-start(f32[768]{0:T(1024)} %get-tuple-element.104) | copy-start | bytes 9220
  470.6 443.3 %copy-start.1 = (bf16[768,1024]{1,0:T(8,128)(2,1)S(1)}, bf16[768,1024]{1,0:T(8,128)(2,1)}, u32[]{:S(2)}) copy-start(bf16[768,1024]{1,0:T(8,128)(2,1)} %param.49) | copy-start | bytes 4718596
  (69 other events, 194.3 us)
Sparse Core Ops, SparseCore 0:
  89.1 59.2 all-reduce.14
  166.4 61.0 all-reduce.16
  257.2 34.1 reduce-scatter.15
  341.7 89.4 all-reduce.18
  434.0 31.7 reduce-scatter.35
  468.5 29.5 reduce-scatter.33
  501.1 29.7 reduce-scatter.37
  533.7 28.9 reduce-scatter.23
  565.6 28.8 reduce-scatter.17
  597.1 28.8 reduce-scatter.19
  628.9 28.8 reduce-scatter.21
  660.5 29.7 reduce-scatter.31
  693.2 29.7 reduce-scatter.25
  725.7 29.7 reduce-scatter.29
  758.3 29.7 reduce-scatter.27
  790.9 38.6 reduce-scatter.43
  832.3 39.4 reduce-scatter.39
  874.4 39.4 reduce-scatter.41
where the time goes:
time: 931 us; the launch traced here: 921 us
  waiting for transfers between devices  552 us (59%)
  matrix products  188 us (20%)
  blocking collectives  78.2 us (8%)
  other arithmetic  40.2 us (4%)
  local copies, waits for them, and re-layouts  36.1 us (4%)
  between operations  17.2 us (2%)
  starting transfers between devices  9.7 us (1%)
    psum x1, waiting for transfers between devices, shards(): lax.psum((light_attn + heavy_attn).astype(jnp.bfloat16), 'branch')  48.1 us
    reduce_scatter x1, waiting for transfers between devices, shards(): lax.psum_scatter(grad_up_heavy, 'seq', scatter_dimension=0, tiled=True)  42.2 us
    reduce_scatter x1, waiting for transfers between devices, shards(): lax.psum_scatter(grad_gate_heavy, 'seq', scatter_dimension=0, tiled=True)  42.2 us
    reduce_scatter x1, waiting for transfers between devices, shards(): lax.psum_scatter(grad_down_heavy, 'seq', scatter_dimension=0, tiled=True)  41.4 us
    dot_general x14, matrix products, weight_grad(): jnp.einsum('dsc,dsh->ch', operand, gradient, preferred_element_type=jnp.f...  40.6 us
    psum x1, waiting for transfers between devices, shards(): lax.psum(ffn_part.astype(jnp.bfloat16), 'branch').astype(jnp.float32)  35 us
    reduce_scatter x1, waiting for transfers between devices, shards(): lax.psum_scatter(grad_wq_heavy, 'seq', scatter_dimension=0, tiled=True)  32.7 us
    reduce_scatter x1, waiting for transfers between devices, shards(): lax.psum_scatter(grad_down_light, 'seq', scatter_dimension=0, tiled=True)  32.7 us
  transfers between devices with their start and end apart: 22, of which 16 were waited for; matrix products, arithmetic and copies ran while one was open for 20% of the time, Pallas kernels for 0%

commit v1 on v0

--- a/solution.py
+++ b/solution.py
@@ -344,47 +344,28 @@
     grad_tokens = grad_hidden + inv_attn * (
         grad_unit_a - unit_attn * jnp.mean(grad_unit_a * unit_attn, axis=-1, keepdims=True)
     )
+    names = (
+        grad_wq_light, grad_wk_light, grad_wv_light, grad_wo_light,
+        grad_wq_heavy, grad_wk_heavy, grad_wv_heavy, grad_wo_heavy,
+        grad_gate_light, grad_up_light, grad_down_light,
+        grad_gate_heavy, grad_up_heavy, grad_down_heavy,
+    )
+    vectors = jnp.stack(
+        [grad_gain_attn, grad_router_query, grad_router_key, grad_gain_ffn, grad_router_ffn], axis=1
+    )
+    packed = jnp.concatenate([g.astype(jnp.bfloat16) for g in names + (vectors,)], axis=1)
+    summed = lax.psum_scatter(packed, "seq", scatter_dimension=0, tiled=True).astype(jnp.float32)
+    widths = [g.shape[1] for g in names]
+    cuts = [sum(widths[:i]) for i in range(len(widths) + 1)]
     (
-        grad_gain_attn,
-        grad_router_query,
-        grad_router_key,
-        grad_wq_light,
-        grad_wk_light,
-        grad_wv_light,
-        grad_wo_light,
-        grad_wq_heavy,
-        grad_wk_heavy,
-        grad_wv_heavy,
-        grad_wo_heavy,
-        grad_gain_ffn,
-        grad_router_ffn,
-        grad_gate_light,
-        grad_up_light,
-        grad_down_light,
-        grad_gate_heavy,
-        grad_up_heavy,
-        grad_down_heavy,
-    ) = (
-        lax.psum_scatter(grad_gain_attn, "seq", scatter_dimension=0, tiled=True),
-        lax.psum_scatter(grad_router_query, "seq", scatter_dimension=0, tiled=True),
-        lax.psum_scatter(grad_router_key, "seq", scatter_dimension=0, tiled=True),
-        lax.psum_scatter(grad_wq_light, "seq", scatter_dimension=0, tiled=True),
-        lax.psum_scatter(grad_wk_light, "seq", scatter_dimension=0, tiled=True),
-        lax.psum_scatter(grad_wv_light, "seq", scatter_dimension=0, tiled=True),
-        lax.psum_scatter(grad_wo_light, "seq", scatter_dimension=0, tiled=True),
-        lax.psum_scatter(grad_wq_heavy, "seq", scatter_dimension=0, tiled=True),
-        lax.psum_scatter(grad_wk_heavy, "seq", scatter_dimension=0, tiled=True),
-        lax.psum_scatter(grad_wv_heavy, "seq", scatter_dimension=0, tiled=True),
-        lax.psum_scatter(grad_wo_heavy, "seq", scatter_dimension=0, tiled=True),
-        lax.psum_scatter(grad_gain_ffn, "seq", scatter_dimension=0, tiled=True),
-        lax.psum_scatter(grad_router_ffn, "seq", scatter_dimension=0, tiled=True),
-        lax.psum_scatter(grad_gate_light, "seq", scatter_dimension=0, tiled=True),
-        lax.psum_scatter(grad_up_light, "seq", scatter_dimension=0, tiled=True),
-        lax.psum_scatter(grad_down_light, "seq", scatter_dimension=0, tiled=True),
-        lax.psum_scatter(grad_gate_heavy, "seq", scatter_dimension=0, tiled=True),
-        lax.psum_scatter(grad_up_heavy, "seq", scatter_dimension=0, tiled=True),
-        lax.psum_scatter(grad_down_heavy, "seq", scatter_dimension=0, tiled=True),
-    )
+        grad_wq_light, grad_wk_light, grad_wv_light, grad_wo_light,
+        grad_wq_heavy, grad_wk_heavy, grad_wv_heavy, grad_wo_heavy,
+        grad_gate_light, grad_up_light, grad_down_light,
+        grad_gate_heavy, grad_up_heavy, grad_down_heavy,
+    ) = [summed[:, cuts[i] : cuts[i + 1]] for i in range(len(widths))]
+    grad_gain_attn, grad_router_query, grad_router_key, grad_gain_ffn, grad_router_ffn = [
+        summed[:, cuts[-1] + i] for i in range(5)
+    ]
     return (
         mixed,
         grad_tokens,

time: 931 us -> 572 us (0.61)
  waiting for transfers between devices: 552 us -> 207 us
  local copies, waits for them, and re-layouts: 36.1 us -> 74.6 us
  blocking collectives: 78.2 us -> 49.8 us
  matrix products: 188 us -> 163 us
    reduce_scatter x14 -> x1, waiting for transfers between devices: 439 us -> 75.6 us  [shards(): lax.psum_scatter(packed, 'seq', scatter_dimension=0, tiled=True)]
    unnamed x1 -> x0, blocking collectives: 28.8 us -> none
    unnamed x19 -> x6, waiting for transfers between devices: 29.5 us -> 57.8 us
    convert_element_type x0 -> x11, local copies, waits for them, and re-layouts: none -> 16.7 us  [shards(): g.astype(jnp.bfloat16)]
    dot_general x14, matrix products: 40.6 us -> 25.6 us  [weight_grad(): jnp.einsum('dsc,dsh->ch', operand, gradient, preferred_element_type=jnp.f...]
    concatenate x0 -> x1, local copies, waits for them, and re-layouts: none -> 14.6 us  [shards(): jnp.concatenate([g.astype(jnp.bfloat16) for g in names + (vectors,)], axi...]
  transfers between devices with their start and end apart: 22 -> 9, of which waited for: 16 -> 4; matrix products, arithmetic and copies ran while one was open for 20% -> 31% of each run, Pallas kernels for 0% -> 0%
where the time goes in v1:
time: 572 us; the launch traced here: 563 us
  waiting for transfers between devices  207 us (36%)
  matrix products  163 us (28%)
  local copies, waits for them, and re-layouts  74.6 us (13%)
  blocking collectives  49.8 us (9%)
  other arithmetic  43.8 us (8%)
  between operations  16.4 us (3%)
  starting transfers between devices  8.62 us (2%)
    reduce_scatter x1, waiting for transfers between devices, shards(): lax.psum_scatter(packed, 'seq', scatter_dimension=0, tiled=True)  75.6 us
    unnamed x6, waiting for transfers between devices  57.8 us
    psum x1, waiting for transfers between devices, shards(): lax.psum((light_attn + heavy_attn).astype(jnp.bfloat16), 'branch')  45 us
    psum x1, waiting for transfers between devices, shards(): lax.psum(ffn_part.astype(jnp.bfloat16), 'branch').astype(jnp.float32)  28.4 us
    dot_general x4, matrix products, contract_key(): jnp.einsum('dhqk,dqhe->dkhe', grad_raw, queries, preferred_element_type=j...  26.5 us
    dot_general x14, matrix products, weight_grad(): jnp.einsum('dsc,dsh->ch', operand, gradient, preferred_element_type=jnp.f...  25.6 us
    dot_general x14, matrix products, unproject(): jnp.einsum('dsh,ch->dsc', operand, matrix, preferred_element_type=jnp.flo...  21.3 us
    dot_general x2, matrix products, contract_query(): jnp.einsum('dhqk,dkhe->dqhe', grad_raw, keys, preferred_element_type=jnp....  19.4 us
  transfers between devices with their start and end apart: 9, of which 4 were waited for; matrix products, arithmetic and copies ran while one was open for 31% of the time, Pallas kernels for 0%

profile of v1, /device:TPU:0, one launch (start us, length us, event | category | flops | bytes accessed | tf_op | source)
XLA Modules:
  0.0 562.9 jit_solution(10502082173037440570)
XLA Ops:
  9.9 2.2 convolution_convert_fusion.4
  13.7 3.0 collective-permute-start
  19.1 2.3 fusion.17
  26.6 18.5 %all_gather.6 = bf16[2,512,384]{2,1,0:T(8,128)(2,1)S(1)} all-gather(bf16[2,64,384]{2,1,0:T(8,128)(2,1)S(1)} %pad_maximum_fusion.5), channel_id=1, replica_groups=mesh['branch'=4,'seq'=8] {'seq'}, dimensions={1}, use_global_device_ids=true | all-gather | bytes 884736 | tf_op jit(solution)/shard_map/all_gather | solution.py:190
  48.2 2.3 fusion.138
  54.6 12.2 %all-gather = bf16[8,64,2]{1,2,0:T(2,128)(2,1)S(1)} all-gather(bf16[1,64,2]{1,2,0:T(2,128)(2,1)} %fusion.308), channel_id=1, replica_groups=mesh['branch'=4,'seq'=8] {'seq'}, dimensions={0}, use_global_device_ids=true | all-gather | bytes 2304 | tf_op jit(solution)/shard_map/all_gather | solution.py:191
  86.4 3.0 add_convert_fusion.3
  97.3 2.6 fusion.178
  99.9 3.1 fusion.91
  103.6 45.0 %all-reduce.9.cloned.1.call-done = bf16[2,512,768]{2,1,0:T(8,128)(2,1)} async-done(((bf16[2,512,768]{2,1,0:T(8,128)(2,1)}), bf16[2,512,768]{2,1,0:T(8,128)(2,1)}) %all-reduce.9.cloned.1.call-update) | async-done | bytes 1572880 | tf_op jit(solution)/shard_map/psum | solution.py:202
  150.8 2.8 fusion.51
  160.1 10.0 %psum.44 = bf16[2,64]{1,0:T(2,128)(2,1)} all-reduce(bf16[2,64]{1,0:T(2,128)(2,1)} %get-tuple-element.157), channel_id=1, replica_groups=mesh['branch'=4,'seq'=8] {'branch'}, use_global_device_ids=true, to_apply=%region_10.11 | all-reduce | flops 128 | bytes 512 | tf_op jit(solution)/shard_map/psum | solution.py:252
  172.3 2.1 fusion.62
  176.2 2.2 fusion.176
  183.6 2.1 add_convert_fusion.1
  187.4 3.3 add_convert_fusion.2
  193.7 5.0 copy.141
  200.7 3.4 fusion.104
  206.1 2.9 fusion.102
  210.9 2.9 bitcast_convert_fusion.1
  213.8 2.8 bitcast_convert_fusion.2
  218.4 28.4 %all-reduce.11.cloned.1.call-done = bf16[2,512,768]{2,1,0:T(8,128)(2,1)} async-done(((bf16[2,512,768]{2,1,0:T(8,128)(2,1)}), bf16[2,512,768]{2,1,0:T(8,128)(2,1)}) %all-reduce.11.cloned.1.call-update) | async-done | bytes 1572880 | tf_op jit(solution)/shard_map/psum | solution.py:251
  246.8 4.6 multiply_reduce_fusion.1
  257.7 2.2 fusion.335
  261.1 4.3 fusion.163
  265.4 2.4 copy.150
  267.8 2.5 copy.151
  270.4 3.1 pad_maximum_fusion
  273.6 3.3 fusion.334
  276.9 4.4 fusion.39
  281.3 16.6 %fusion.25 = f32[2,2,64,640]{3,2,1,0:T(8,128)} fusion(bf16[2,512,2,64]{1,3,2,0:T(8,128)(2,1)S(1)} %bitcast.324, f32[2,2,512,640]{3,2,1,0:T(8,128)} %fusion.334, f32[2,2,512,640]{3,2,1,0:T(8,128)} %copy-done.4, f32[2,2,512]{2,1,0:T(2,128)S(1)} %copy-done.91), kind=kOutput, calls=%fused_computation.27 | convolution fusion | flops 176949888 | bytes 11411456 | tf_op jit(solution)/shard_map/dhqk,dqhe->dkhe/dot_general | solution.py:96
  299.2 2.2 copy.145
  303.2 2.4 collective-permute-start.2
  306.9 3.4 convolution_convert_fusion.6
  310.3 16.0 %fusion.125 = bf16[2,2,64,512]{3,2,1,0:T(8,128)(2,1)} fusion(bf16[2,640,2,64]{1,3,2,0:T(8,128)(2,1)} %bitcast.308, f32[2,2,512,640]{3,2,1,0:T(8,128)} %fusion.334, f32[2,2,512,640]{3,2,1,0:T(8,128)} %copy-done.4, f32[2,2,512]{2,1,0:T(2,128)S(1)} %copy-done.91), kind=kOutput, calls=%fused_computation.152 | convolution fusion | flops 177080960 | bytes 11083776 | tf_op jit(solution)/shard_map/dhqk,dkhe->dqhe/dot_general | solution.py:91
  326.6 2.3 fusion.133
  329.0 3.2 fusion.170
  332.1 2.3 fusion.242
  340.1 3.4 fusion.234
  343.5 2.2 fusion.237
  347.3 7.8 %add_convert_fusion = bf16[2,512,768]{2,1,0:T(8,128)(2,1)} fusion(f32[2,512,768]{2,1,0:T(8,128)} %fusion.170, f32[2,512,768]{2,1,0:T(8,128)} %fusion.234, f32[2,512,768]{2,1,0:T(8,128)} %fusion.242, f32[2,512,768]{2,1,0:T(8,128)} %fusion.237, f32[2,64,768]{2,1,0:T(8,128)S(1)} %convolution_add_fusion, s32[2,64]{1,0:T(2,128)S(1)} %copy-done.110, ...), kind=kOutput, calls=%fused_computation.42 | convolution fusion | flops 607977472 | bytes 14551552 | tf_op jit(solution)/shard_map/drs,drc->dsc/dot_general | solution.py:51
  356.1 2.4 fusion.134
  364.4 9.2 %all-reduce.3 = (bf16[2,64]{1,0:T(2,128)(2,1)S(1)}, bf16[2,64]{1,0:T(2,128)(2,1)S(1)}) all-reduce(bf16[2,64]{1,0:T(2,128)(2,1)S(1)} %get-tuple-element.159, bf16[2,64]{1,0:T(2,128)(2,1)S(1)} %copy-done.111), channel_id=1, replica_groups=mesh['branch'=4,'seq'=8] {'branch'}, use_global_device_ids=true, to_apply=%region_19.20 | all-reduce | flops 256 | bytes 1024 | tf_op jit(solution)/shard_map/psum | solution.py:333
  387.0 57.7 %all-reduce.13.cloned.1.call-done = (bf16[2,512,768]{1,0,2:T(2,128)(2,1)}, bf16[2,512,768]{2,1,0:T(8,128)(2,1)}) async-done(((bf16[2,512,768]{1,0,2:T(2,128)(2,1)}, bf16[2,512,768]{2,1,0:T(8,128)(2,1)}), (bf16[2,512,768]{1,0,2:T(2,128)(2,1)}, bf16[2,512,768]{2,1,0:T(8,128)(2,1)})) %all-reduce.13.cloned.1.call-update) | async-done | bytes 3145744
  444.8 3.6 fusion.35
  449.2 14.6 %concatenate.33 = bf16[768,5125]{1,0:T(8,128)(2,1)} concatenate(bf16[768,128]{1,0:T(8,128)(2,1)} %copy.159, bf16[768,128]{1,0:T(8,128)(2,1)} %copy.160, bf16[768,128]{1,0:T(8,128)(2,1)} %copy.161, bf16[768,128]{1,0:T(8,128)(2,1)} %copy.162, bf16[768,192]{1,0:T(8,128)(2,1)} %copy.163, bf16[768,192]{1,0:T(8,128)(2,1)} %copy.164, bf16[768,192]{1,0:T(8,128)(2,1)} %copy.165, ...), dimensions={1} | concatenate | bytes 15744000 | tf_op jit(solution)/shard_map/concatenate | solution.py:356
  470.4 4.4 fusion.34
  474.8 75.6 %reduce-scatter.5.cloned.1.call-done = bf16[96,5125]{1,0:T(8,128)(2,1)} async-done(((bf16[768,5125]{1,0:T(8,128)(2,1)}), bf16[96,5125]{1,0:T(8,128)(2,1)}) %reduce-scatter.5.cloned.1.call-update) | async-done | bytes 984016 | tf_op jit(solution)/shard_map/reduce_scatter | solution.py:357
  (371 shorter events, 128.2 us)
Async XLA Ops:
  7.2 149.5 %copy-start = (bf16[768,1024]{1,0:T(8,128)(2,1)S(1)}, bf16[768,1024]{1,0:T(8,128)(2,1)}, u32[]{:S(2)}) copy-start(bf16[768,1024]{1,0:T(8,128)(2,1)} %param.49) | copy-start | bytes 4718596
  7.2 141.4 %all-reduce.9.cloned.1.call-start = ((), (), s32[]{:S(2)}) async-start(), calls=%async_computation.2 | async-start | bytes 3145728 | tf_op jit(solution)/shard_map/psum | solution.py:202
  9.2 66.0 %copy-start.73 = (f32[2,512]{1,0:T(2,128)}, f32[2,512]{1,0:T(2,128)S(1)}, u32[]{:S(2)}) copy-start(f32[2,512]{1,0:T(2,128)S(1)} %add_rsqrt_fusion.1) | copy-start | bytes 12292
  9.9 65.3 %copy-start.75 = (f32[768]{0:T(1024)}, f32[768]{0:T(1024)S(1)}, u32[]{:S(2)}) copy-start(f32[768]{0:T(1024)S(1)} %convert_element_type.288) | copy-start | bytes 9220
  9.9 8.7 %copy-start.109 = (s32[2,64]{1,0:T(2,128)S(1)}, s32[2,64]{1,0:T(2,128)}, u32[]{:S(2)}) copy-start(s32[2,64]{1,0:T(2,128)} %param.32) | copy-start | bytes 1540
  13.7 65.7 %collective-permute-start = (bf16[2,64,256]{1,2,0:T(8,128)(2,1)}, bf16[2,64,256]{1,2,0:T(8,128)(2,1)}, u32[]{:S(2)}, u32[]{:S(2)}) collective-permute-start(bf16[2,64,256]{1,2,0:T(8,128)(2,1)} %get-tuple-element.141), channel_id=1, source_target_pairs={{0,1},{1,2},{2,3},{3,4},{4,5},{5,6},{6,7},{8,9},{9,10},{10,11},{11... | collective-permute-start | bytes 196616 | tf_op jit(solution)/shard_map/ppermute | solution.py:25
  16.7 62.7 %collective-permute-start.1 = (bf16[2,64,256]{1,2,0:T(8,128)(2,1)}, bf16[2,64,256]{1,2,0:T(8,128)(2,1)}, u32[]{:S(2)}, u32[]{:S(2)}) collective-permute-start(bf16[2,64,256]{1,2,0:T(8,128)(2,1)} %get-tuple-element.142), channel_id=1, source_target_pairs={{1,0},{2,1},{3,2},{4,3},{5,4},{6,5},{7,6},{9,8},{10,9},{11,10},{12... | collective-permute-start | bytes 196616 | tf_op jit(solution)/shard_map/ppermute | solution.py:27
  19.1 7.1 %copy-start.41 = (bf16[768,192]{0,1:T(8,128)(2,1)S(1)}, bf16[768,192]{0,1:T(8,128)(2,1)}, u32[]{:S(2)}) copy-start(bf16[768,192]{0,1:T(8,128)(2,1)} %param.42) | copy-start | bytes 884740
  70.8 6.3 %copy-start.85 = (s32[2,64]{1,0:T(2,128)S(1)}, s32[2,64]{1,0:T(2,128)}, u32[]{:S(2)}) copy-start(s32[2,64]{1,0:T(2,128)} %param.31) | copy-start | bytes 1540
  71.9 5.5 copy-start.64
  74.4 6.4 %copy-start.66 = (bf16[2,512,128]{1,2,0:T(8,128)(2,1)}, bf16[2,512,128]{1,2,0:T(8,128)(2,1)S(1)}, u32[]{:S(2)}) copy-start(bf16[2,512,128]{1,2,0:T(8,128)(2,1)S(1)} %convolution_convert_fusion.3) | copy-start | bytes 786436
  77.4 8.9 %copy-start.94 = (f32[2,1,64]{2,1,0:T(1,128)}, f32[2,1,64]{2,1,0:T(1,128)S(1)}, u32[]{:S(2)}) copy-start(f32[2,1,64]{2,1,0:T(1,128)S(1)} %fusion.186) | copy-start | bytes 1540
  79.0 7.4 %copy-start.19 = (f32[2,64,768]{2,1,0:T(8,128)}, f32[2,64,768]{2,1,0:T(8,128)S(1)}, u32[]{:S(2)}) copy-start(f32[2,64,768]{2,1,0:T(8,128)S(1)} %fusion.223) | copy-start | bytes 1179652
  89.3 157.4 %all-reduce.11.cloned.1.call-start = ((), (), s32[]{:S(2)}) async-start(), calls=%async_computation.3 | async-start | bytes 3145728 | tf_op jit(solution)/shard_map/psum | solution.py:251
  89.6 13.4 %copy-start.93 = (f32[2,2,512]{2,1,0:T(2,128)S(1)}, f32[2,2,512]{2,1,0:T(2,128)}, u32[]{:S(2)}) copy-start(f32[2,2,512]{2,1,0:T(2,128)} %copy-done.92) | copy-start | bytes 24580
  103.6 50.3 %copy-start.72 = (f32[768]{0:T(1024)S(1)}, f32[768]{0:T(1024)}, u32[]{:S(2)}) copy-start(f32[768]{0:T(1024)} %convert_element_type.311) | copy-start | bytes 9220
  185.7 160.0 %reduce-scatter.3.cloned.1.call-start = ((), (), s32[]{:S(2)}) async-start(), calls=%async_computation.4 | async-start | bytes 1769472 | tf_op jit(solution)/shard_map/reduce_scatter | solution.py:316
  210.9 5.7 %copy-start.15 = (f32[2,64,768]{2,1,0:T(8,128)S(1)}, f32[2,64,768]{2,1,0:T(8,128)}, u32[]{:S(2)}) copy-start(f32[2,64,768]{2,1,0:T(8,128)} %fusion.178) | copy-start | bytes 1179652
  210.9 5.7 %copy-start.52 = (bf16[2,64,1024]{2,1,0:T(8,128)(2,1)S(1)}, bf16[2,64,1024]{2,1,0:T(8,128)(2,1)}, u32[]{:S(2)}) copy-start(bf16[2,64,1024]{2,1,0:T(8,128)(2,1)} %copy-done.51) | copy-start | bytes 786436
  210.9 5.7 %copy-start.106 = (f32[2,1,64]{2,1,0:T(1,128)S(1)}, f32[2,1,64]{2,1,0:T(1,128)}, u32[]{:S(2)}) copy-start(f32[2,1,64]{2,1,0:T(1,128)} %copy-done.104) | copy-start | bytes 1540
  255.0 6.1 %copy-start.21 = (f32[2,64,768]{2,1,0:T(8,128)}, f32[2,64,768]{2,1,0:T(8,128)S(1)}, u32[]{:S(2)}) copy-start(f32[2,64,768]{2,1,0:T(8,128)S(1)} %get-tuple-element.162) | copy-start | bytes 1179652
  267.8 5.7 %copy-start.37 = (bf16[2,640,128]{1,2,0:T(8,128)(2,1)S(1)}, bf16[2,640,128]{1,2,0:T(8,128)(2,1)}, u32[]{:S(2)}) copy-start(bf16[2,640,128]{1,2,0:T(8,128)(2,1)} %copy-done.36) | copy-start | bytes 983044
  273.5 171.3 %all-reduce.13.cloned.1.call-start = ((), (), s32[]{:S(2)}) async-start(), calls=%async_computation.6 | async-start | bytes 6291456
  303.2 35.9 %collective-permute-start.2 = (bf16[2,64,256]{2,1,0:T(8,128)(2,1)}, bf16[2,64,256]{2,1,0:T(8,128)(2,1)}, u32[]{:S(2)}, u32[]{:S(2)}) collective-permute-start(bf16[2,64,256]{2,1,0:T(8,128)(2,1)} %get-tuple-element.137), channel_id=1, source_target_pairs={{0,1},{1,2},{2,3},{3,4},{4,5},{5,6},{6,7},{8,9},{9,10},{10,11},{11... | collective-permute-start | bytes 196616 | tf_op jit(solution)/shard_map/ppermute | solution.py:25
  305.6 33.5 %collective-permute-start.3 = (bf16[2,64,256]{2,1,0:T(8,128)(2,1)}, bf16[2,64,256]{2,1,0:T(8,128)(2,1)}, u32[]{:S(2)}, u32[]{:S(2)}) collective-permute-start(bf16[2,64,256]{2,1,0:T(8,128)(2,1)} %get-tuple-element.138), channel_id=1, source_target_pairs={{1,0},{2,1},{3,2},{4,3},{5,4},{6,5},{7,6},{9,8},{10,9},{11,10},{12... | collective-permute-start | bytes 196616 | tf_op jit(solution)/shard_map/ppermute | solution.py:27
  310.3 16.1 %copy-start.62 = (bf16[2,3,64,64]{3,2,1,0:T(8,128)(2,1)}, bf16[2,3,64,64]{3,2,1,0:T(8,128)(2,1)S(1)}, u32[]{:S(2)}) copy-start(bf16[2,3,64,64]{3,2,1,0:T(8,128)(2,1)S(1)} %convolution_convert_fusion.6) | copy-start | bytes 147460
  310.3 16.1 %copy-start.40 = (bf16[768,192]{0,1:T(8,128)(2,1)S(1)}, bf16[768,192]{0,1:T(8,128)(2,1)}, u32[]{:S(2)}) copy-start(bf16[768,192]{0,1:T(8,128)(2,1)} %param.40) | copy-start | bytes 884740
  310.3 16.3 %copy-start.74 = (f32[2,512]{1,0:T(2,128)S(1)}, f32[2,512]{1,0:T(2,128)}, u32[]{:S(2)}) copy-start(f32[2,512]{1,0:T(2,128)} %copy-done.73) | copy-start | bytes 12292
  310.3 16.3 %copy-start.76 = (f32[768]{0:T(1024)S(1)}, f32[768]{0:T(1024)}, u32[]{:S(2)}) copy-start(f32[768]{0:T(1024)} %copy-done.75) | copy-start | bytes 9220
  326.6 5.5 copy-start.68
  326.6 5.5 copy-start.69
  332.1 7.9 %copy-start.18 = (f32[2,640,128]{2,1,0:T(8,128)S(1)}, f32[2,640,128]{2,1,0:T(8,128)}, u32[]{:S(2)}) copy-start(f32[2,640,128]{2,1,0:T(8,128)} %copy.145) | copy-start | bytes 1966084
  340.1 6.6 %copy-start.42 = (bf16[768,192]{0,1:T(8,128)(2,1)S(1)}, bf16[768,192]{0,1:T(8,128)(2,1)}, u32[]{:S(2)}) copy-start(bf16[768,192]{0,1:T(8,128)(2,1)} %param.42) | copy-start | bytes 884740
  346.7 8.4 %copy-start.33 = (bf16[2,64,384]{2,1,0:T(8,128)(2,1)}, bf16[2,64,384]{2,1,0:T(8,128)(2,1)S(1)}, u32[]{:S(2)}) copy-start(bf16[2,64,384]{2,1,0:T(8,128)(2,1)S(1)} %convert.36) | copy-start | bytes 294916
  355.2 6.2 %copy-start.24 = (bf16[2,512,256]{2,1,0:T(8,128)(2,1)S(1)}, bf16[2,512,256]{2,1,0:T(8,128)(2,1)}, u32[]{:S(2)}) copy-start(bf16[2,512,256]{2,1,0:T(8,128)(2,1)} %copy-done.23) | copy-start | bytes 1572868
  355.2 195.3 %reduce-scatter.5.cloned.1.call-start = ((), (), s32[]{:S(2)}) async-start(), calls=%async_computation.5 | async-start | bytes 9068544 | tf_op jit(solution)/shard_map/reduce_scatter | solution.py:357
  362.0 11.5 %copy-start.96 = (f32[2,1,64]{2,1,0:T(1,128)S(1)}, f32[2,1,64]{2,1,0:T(1,128)}, u32[]{:S(2)}) copy-start(f32[2,1,64]{2,1,0:T(1,128)} %copy-done.94) | copy-start | bytes 1540
  362.0 11.5 %copy-start.90 = (s32[2,64]{1,0:T(2,128)S(1)}, s32[2,64]{1,0:T(2,128)}, u32[]{:S(2)}) copy-start(s32[2,64]{1,0:T(2,128)} %param.31) | copy-start | bytes 1540
  374.7 5.7 %copy-start.34 = (bf16[2,64,384]{2,1,0:T(8,128)(2,1)S(1)}, bf16[2,64,384]{2,1,0:T(8,128)(2,1)}, u32[]{:S(2)}) copy-start(bf16[2,64,384]{2,1,0:T(8,128)(2,1)} %copy-done.33) | copy-start | bytes 294916
  374.7 5.7 %copy-start.103 = (f32[2,1,64]{2,1,0:T(1,128)S(1)}, f32[2,1,64]{2,1,0:T(1,128)}, u32[]{:S(2)}) copy-start(f32[2,1,64]{2,1,0:T(1,128)} %copy-done.101) | copy-start | bytes 1540
  376.6 68.2 %copy-start.77 = (f32[768]{0:T(1024)S(1)}, f32[768]{0:T(1024)}, u32[]{:S(2)}) copy-start(f32[768]{0:T(1024)} %convert_element_type.357) | copy-start | bytes 9220
  376.6 68.1 %copy-start.78 = (f32[768]{0:T(1024)S(1)}, f32[768]{0:T(1024)}, u32[]{:S(2)}) copy-start(f32[768]{0:T(1024)} %convert_element_type.360) | copy-start | bytes 9220
  380.3 68.9 %copy-start.13 = (bf16[768,1024]{1,0:T(8,128)(2,1)S(1)}, bf16[768,1024]{1,0:T(8,128)(2,1)}, u32[]{:S(2)}) copy-start(bf16[768,1024]{1,0:T(8,128)(2,1)} %bitcast_convert_fusion.1) | copy-start | bytes 4718596
  385.1 64.1 %copy-start.32 = (bf16[768,256]{1,0:T(8,128)(2,1)S(1)}, bf16[768,256]{1,0:T(8,128)(2,1)}, u32[]{:S(2)}) copy-start(bf16[768,256]{1,0:T(8,128)(2,1)} %copy.168) | copy-start | bytes 1179652
  463.8 6.6 %copy-start.100 = (f32[2,512]{1,0:T(2,128)S(1)}, f32[2,512]{1,0:T(2,128)}, u32[]{:S(2)}) copy-start(f32[2,512]{1,0:T(2,128)} %get-tuple-element.107) | copy-start | bytes 12292
  463.8 6.6 %copy-start.79 = (f32[2,512]{1,0:T(2,128)S(1)}, f32[2,512]{1,0:T(2,128)}, u32[]{:S(2)}) copy-start(f32[2,512]{1,0:T(2,128)} %get-tuple-element.148) | copy-start | bytes 12292
  463.8 6.6 %copy-start.80 = (f32[2,512]{1,0:T(2,128)S(1)}, f32[2,512]{1,0:T(2,128)}, u32[]{:S(2)}) copy-start(f32[2,512]{1,0:T(2,128)} %get-tuple-element.163) | copy-start | bytes 12292
  470.4 85.5 %copy-start.1 = (bf16[768,1024]{1,0:T(8,128)(2,1)S(1)}, bf16[768,1024]{1,0:T(8,128)(2,1)}, u32[]{:S(2)}) copy-start(bf16[768,1024]{1,0:T(8,128)(2,1)} %param.49) | copy-start | bytes 4718596
  (74 other events, 205.0 us)
Sparse Core Ops, SparseCore 0:
  89.5 59.1 all-reduce.8
  185.8 60.8 all-reduce.10
  273.6 34.0 reduce-scatter.2
  355.3 89.4 all-reduce.12
  463.9 86.5 reduce-scatter.4

commit v2 on v1

--- a/solution.py
+++ b/solution.py
@@ -1,8 +1,11 @@
+import functools
 import math
 
 import jax
 import jax.numpy as jnp
 from jax import lax
+from jax.experimental import pallas as pl
+from jax.experimental.pallas import tpu as pltpu
 from jax.sharding import PartitionSpec as P
 
 HD = 64
@@ -110,7 +113,7 @@
     )
 
 
-def shards(
+def plain_shards(
     tokens,
     cotangent,
     lengths,
@@ -391,9 +394,958 @@
     )
 
 
+BF = jnp.bfloat16
+F32 = jnp.float32
+MESH = pl.DeviceIdType.MESH
+
+
+def mm(a, b):
+    return jnp.dot(a, b, preferred_element_type=F32)
+
+
+def mmt(a, b):
+    return lax.dot_general(a, b, (((1,), (1,)), ((), ())), preferred_element_type=F32)
+
+
+def tmm(a, b):
+    return lax.dot_general(a, b, (((0,), (0,)), ((), ())), preferred_element_type=F32)
+
+
+def row_sum(values):
+    return jnp.sum(values, axis=-1, keepdims=True)
+
+
+def gelu_parts(v):
+    c = math.sqrt(2.0 / math.pi)
+    square = v * v
+    t = jnp.tanh(c * v * (1.0 + 0.044715 * square))
+    act = 0.5 * v * (1.0 + t)
+    slope = 0.5 * (1.0 + t) + (0.5 * c) * v * (1.0 - t * t) * (1.0 + 0.134145 * square)
+    return act, slope
+
+
+def layer_kernel(dims, *refs):
+    docs, rows, width, slots, n_seq, wl, wh, fl_n, fh_n = dims
+    nz = n_seq // 2
+    chunk = width // n_seq
+    half = rows // 2
+    quarter = rows // 4
+    eighth = rows // 8
+    radius = WINDOW // 2
+    share = width // 4
+    it = iter(refs)
+
+    def take(count):
+        return [next(it) for _ in range(count)]
+
+    lens, vec, idxc, idxr = take(4)
+    (tok_h, cot_h, wql_h, wkl_h, wvl_h, wol_h, wqh_h, wkh_h, wvh_h, woh_h,
+     gl_h, ul_h, dl_h, gh_h, uh_h, dh_h) = take(16)
+    gt_o, mix_o, tot_o, pack_o = take(4)
+    (tok, cot, wqkv, wol, whq, whk, whv, who, wgul, wdl, wguh, wdh) = take(12)
+    (nl, inva, hin, kin, sin, qbuf, kvw, pbuf, lo, hqx, kvall, ph, hox) = take(13)
+    (pqk, pqkt, parts, tot1, tot2, r1, r2, cols) = take(8)
+    (dm, dmh, grow, fl, invf, mid, dgu, frow, ghr, midh, dguh) = take(11)
+    (mixb, mixr, ghf, ghb, dol, dox, gah, dqh, dkvw, rims, rimr, dqkv) = take(12)
+    (hb, h1, h2, dkvh, gains) = take(5)
+    (g_h, g_l, ra_h, ra_l, ra_a, rb_h, rb_l, rb_a, packed, vbuf, vr) = take(11)
+    g_a = wguh
+    (load_s, ar_s, ar_r, ag_s, ag_r, fw_s, fw_r, halo_s, halo_r, rim_s, rim_r, ha_s, ha_r, hz_s, hz_r,
+     mx_s, mx_r, wa_s, wa_r, wz_s, wz_r, v_s, v_r, out_s) = take(24)
+
+    b = lax.axis_index("branch")
+    s = lax.axis_index("seq")
+    bit_x = b % 2
+    bit_y = b // 2
+    core = s % 2
+    z = s // 2
+    offset = s * rows
+    dev_x = (b + 1 - 2 * bit_x, s)
+    dev_y = (b + 2 - 4 * bit_y, s)
+    sibling = (b, s + 1 - 2 * core)
+
+    def zpeer(k):
+        return (z + k) % nz
+
+    def same_core(k):
+        return (b, 2 * zpeer(k) + core)
+
+    late = []
+
+    def send(src, dst, ssem, rsem, dev, when=None):
+        copy = pltpu.make_async_remote_copy(
+            src_ref=src, dst_ref=dst, send_sem=ssem, recv_sem=rsem, device_id=dev, device_id_type=MESH
+        )
+        if when is None:
+            copy.start()
+        else:
+            pl.when(when)(copy.start)
+        return copy
+
+    def arrived(dst, ssem, rsem, dev):
+        pltpu.make_async_remote_copy(
+            src_ref=dst, dst_ref=dst, send_sem=ssem, recv_sem=rsem, device_id=dev, device_id_type=MESH
+        ).wait_recv()
+
+    loads = {}
+
+    def load(name, src, dst, i):
+        copy = pltpu.make_async_copy(src, dst, load_s.at[i])
+        copy.start()
+        loads[name] = copy
+
+    load("tok", tok_h, tok, 0)
+    load("whq", wqh_h, whq, 1)
+    load("whk", wkh_h, whk, 2)
+    load("whv", wvh_h, whv, 3)
+    load("wq", wql_h, wqkv.at[:, 0:wl], 4)
+    load("wk", wkl_h, wqkv.at[:, wl : 2 * wl], 5)
+    load("wv", wvl_h, wqkv.at[:, 2 * wl : 3 * wl], 6)
+    load("wol", wol_h, wol, 7)
+    load("who", woh_h, who, 8)
+    load("cot", cot_h, cot, 9)
+    load("wdl", dl_h, wdl, 10)
+    load("wdh", dh_h, wdh, 11)
+    load("gl", gl_h, wgul.at[:, 0:fl_n], 12)
+    load("ul", ul_h, wgul.at[:, fl_n : 2 * fl_n], 13)
+    load("gh", gh_h, wguh.at[:, 0:fh_n], 14)
+    load("uh", uh_h, wguh.at[:, fh_n : 2 * fh_n], 15)
+
+    barrier = pltpu.get_barrier_semaphore()
+    for k in range(1, 4):
+        pl.semaphore_signal(barrier, inc=1, device_id=((b + k) % 4, s), device_id_type=MESH)
+
+    def greet(k, carry):
+        pl.semaphore_signal(barrier, inc=1, device_id=(b, (s + k) % n_seq), device_id_type=MESH)
+        return carry
+
+    lax.fori_loop(1, n_seq, greet, 0)
+    pl.semaphore_wait(barrier, 3 + n_seq - 1)
+
+    gain_a = vec[0:1, :]
+    router_q = vec[1:2, :]
+    router_k = vec[2:3, :]
+    gain_f = vec[3:4, :]
+    router_f = vec[4:5, :]
+
+    def valid_rows(d, first, count):
+        at = lax.broadcasted_iota(jnp.int32, (count, 1), 0) + (offset + first)
+        return jnp.where(at < lens[d], 1.0, 0.0).astype(F32)
+
+    def tiles(count, size, body):
+        def step(t, carry):
+            body(pl.multiple_of(t * size, size))
+            return carry
+
+        lax.fori_loop(0, count // size, step, 0)
+
+    def geometry(h):
+        first, second = ((dev_x, bit_x), (dev_y, bit_y))[:: 1 if h == 0 else -1]
+        base = half * h
+        keep1 = base + quarter * first[1]
+        send1 = base + quarter * (1 - first[1])
+        keep2 = keep1 + eighth * second[1]
+        send2 = keep1 + eighth * (1 - second[1])
+        return (first[0], second[0]) + tuple(pl.multiple_of(v, eighth) for v in (keep1, send1, keep2, send2))
+
+    flights = {}
+
+    def ar_start(a, d, h):
+        first, second, keep1, send1, keep2, send2 = geometry(h)
+        flights[a, d, h, 0] = send(
+            parts.at[d, pl.ds(send1, quarter)], r1.at[d, h], ar_s.at[a, d, h, 0], ar_r.at[a, d, h, 0], first
+        )
+
+    def add_rows(d, at, buf, base, total):
+        def body(t, carry):
+            r = pl.multiple_of(t * 32, 32)
+            here = pl.ds(pl.multiple_of(at + r, 32), 32)
+            value = parts[d, here, :].astype(F32) + buf[pl.ds(base + r, 32), :].astype(F32)
+            total[d, here, :] = value.astype(BF)
+            return carry
+
+        lax.fori_loop(0, eighth // 32, body, 0)
+
+    def ar_step(a, d, step, total):
+        for h in range(2):
+            first, second, keep1, send1, keep2, send2 = geometry(h)
+            at = (a, d, h)
+            if step == 1:
+                arrived(r1.at[d, h], ar_s.at[a, d, h, 0], ar_r.at[a, d, h, 0], first)
+                add_rows(d, send2, r1.at[d, h], pl.multiple_of(send2 - keep1, eighth), parts)
+                flights[at + (1,)] = send(
+                    parts.at[d, pl.ds(send2, eighth)], r2.at[d, h], ar_s.at[a, d, h, 1], ar_r.at[a, d, h, 1], second
+                )
+                add_rows(d, keep2, r1.at[d, h], pl.multiple_of(keep2 - keep1, eighth), parts)
+            elif step == 2:
+                arrived(r2.at[d, h], ar_s.at[a, d, h, 1], ar_r.at[a, d, h, 1], second)
+                add_rows(d, keep2, r2.at[d, h], 0, total)
+                own = total.at[d, pl.ds(keep2, eighth)]
+                flights[at + (2,)] = send(own, own, ar_s.at[a, d, h, 2], ar_r.at[a, d, h, 2], second)
+            elif step == 3:
+                arrived(total.at[d, pl.ds(send2, eighth)], ar_s.at[a, d, h, 2], ar_r.at[a, d, h, 2], second)
+                own = total.at[d, pl.ds(keep1, quarter)]
+                flights[at + (3,)] = send(own, own, ar_s.at[a, d, h, 3], ar_r.at[a, d, h, 3], first)
+            else:
+                arrived(total.at[d, pl.ds(send1, quarter)], ar_s.at[a, d, h, 3], ar_r.at[a, d, h, 3], first)
+                flights[at + (0,)].wait_send()
+                flights[at + (1,)].wait_send()
+
+    def ar_sent(a, d):
+        for h in range(2):
+            flights[a, d, h, 2].wait_send()
+            flights[a, d, h, 3].wait_send()
+
+    loads["tok"].wait()
+    for d in range(docs):
+
+        def norm_body(t, d=d):
+            r = pl.ds(t, 32)
+            x = tok[d, r, :].astype(F32)
+            inv = lax.rsqrt(row_sum(x * x) * (1.0 / width) + epsilon)
+            inva[d, r, :] = inv
+            nl[d, r, :] = (x * inv * gain_a).astype(BF)
+
+        tiles(rows, 32, norm_body)
+
+    for d in range(docs):
+        lane_pos = lax.broadcasted_iota(jnp.int32, (2 * slots, rows), 1) + offset
+        pqk[d] = jnp.where(idxc[:, d : d + 1] == lane_pos, 1.0, 0.0).astype(BF)
+        sub_pos = lax.broadcasted_iota(jnp.int32, (rows, 2 * slots), 0) + offset
+        pqkt[d] = jnp.where(idxr[d : d + 1, :] == sub_pos, 1.0, 0.0).astype(BF)
+
+    SQ, SK, SF, PREQ, PREF, PREK = range(6)
+
+    def mine(d):
+        return slice(d * slots, (d + 1) * slots)
+
+    for d in range(docs):
+        live = jnp.where(idxc[:, d : d + 1] >= 0, 1.0, 0.0).astype(F32)
+        picked = mm(pqk[d], nl[d])
+        score_q = jax.nn.sigmoid(row_sum(picked[:slots] * router_q)) * live[:slots]
+        score_k = jax.nn.sigmoid(row_sum(picked[slots:] * router_k)) * live[slots:]
+        cols[SQ, mine(d), :] = score_q
+        cols[SK, mine(d), :] = score_k
+        hin[mine(d), :] = picked[:slots].astype(BF)
+        kin[mine(d), :] = picked[slots:].astype(BF)
+        sin[mine(d), :] = (picked[slots:] * score_k).astype(BF)
+        pad_lane = lax.broadcasted_iota(jnp.int32, (slots, 256 - wh), 1)
+        kvall[s, mine(d), wh:256] = jnp.where(
+            pad_lane == 0, (1.0 - live[slots:]) * masked_value, 0.0
+        ).astype(BF)
+        kvall[s, mine(d), 256 + wh : 512] = jnp.zeros((slots, 256 - wh), BF)
+    loads["whk"].wait()
+    kvall[s, :, 0:wh] = mm(kin[...], whk[...]).astype(BF)
+    loads["whv"].wait()
+    kvall[s, :, 256 : 256 + wh] = mm(sin[...], whv[...]).astype(BF)
+
+    own_block = kvall.at[s]
+    late.append(send(own_block, own_block, ag_s.at[0], ag_r.at[0], sibling))
+    for k in range(1, nz):
+        late.append(send(own_block, own_block, ag_s.at[k], ag_r.at[k], same_core(k)))
+
+    loads["whq"].wait()
+    hqx[:, 0:wh] = mm(hin[...], whq[...]).astype(BF)
+    pad_lane = lax.broadcasted_iota(jnp.int32, (docs * slots, 256 - wh), 1)
+    hqx[:, wh:256] = jnp.where(pad_lane == 0, 8.0, 0.0).astype(BF)
+
+    for name in ("wq", "wk", "wv"):
+        loads[name].wait()
+    last = n_seq - 1
+    left = (b, (s + last) % n_seq)
+    right = (b, (s + 1) % n_seq)
+    for d in range(docs):
+
+        def qkv_body(t, d=d):
+            r = mm(nl[d, pl.ds(t, half), :], wqkv[...]).astype(BF)
+            qbuf[d, pl.ds(t, half), :] = r[:, 0:wl]
+            kvw[d, pl.ds(pl.multiple_of(t + radius, 32), half), :] = r[:, wl : 3 * wl]
+
+        tiles(rows, half, qkv_body)
+
+        @pl.when(s == 0)
+        def _(d=d):
+            kvw[d, 0:radius, :] = jnp.zeros((radius, 2 * wl), BF)
+
+        @pl.when(s == last)
+        def _(d=d):
+            kvw[d, rows + radius : rows + 2 * radius, :] = jnp.zeros((radius, 2 * wl), BF)
+
+        late.append((s > 0, send(
+            kvw.at[d, pl.ds(radius, radius)], kvw.at[d, pl.ds(rows + radius, radius)],
+            halo_s.at[d, 0], halo_r.at[d, 0], left, s > 0,
+        )))
+        late.append((s < last, send(
+            kvw.at[d, pl.ds(rows, radius)], kvw.at[d, pl.ds(0, radius)],
+            halo_s.at[d, 1], halo_r.at[d, 1], right, s < last,
+        )))
+
+    def halo_wait(d):
+        @pl.when(s < last)
+        def _():
+            arrived(kvw.at[d, pl.ds(rows + radius, radius)], halo_s.at[d, 0], halo_r.at[d, 0], right)
+
+        @pl.when(s > 0)
+        def _():
+            arrived(kvw.at[d, pl.ds(0, radius)], halo_s.at[d, 1], halo_r.at[d, 1], left)
+
+    blk = WINDOW
+    span = 2 * WINDOW
+    n_blk = rows // blk
+
+    def two_heads(v):
+        lane = lax.broadcasted_iota(jnp.int32, v.shape, 1)
+        zero = jnp.zeros_like(v)
+        return jnp.concatenate([jnp.where(lane < HD, v, zero), jnp.where(lane < HD, zero, v)], axis=0)
+
+    def one_of_two(v):
+        lane = lax.broadcasted_iota(jnp.int32, (blk, 2 * HD), 1)
+        return jnp.where(lane < HD, v[:blk], v[blk:])
+
+    def light_attention(d):
+        def body(i, carry):
+            at = pl.multiple_of(i * blk, blk)
+            q2 = two_heads(qbuf[d, pl.ds(at, blk), :])
+            k = kvw[d, pl.ds(at, span), 0:wl]
+            v = kvw[d, pl.ds(at, span), wl : 2 * wl]
+            row = lax.broadcasted_iota(jnp.int32, (2 * blk, span), 0) % blk
+            col = lax.broadcasted_iota(jnp.int32, (2 * blk, span), 1)
+            pos = col + (offset + at - radius)
+            seen = (col >= row) & (col <= row + WINDOW) & (pos >= 0) & (pos < lens[d])
+            scores = jnp.where(seen, mmt(q2, k) * HD ** (-0.5), masked_value)
+            e = jnp.exp(scores - jnp.max(scores, axis=-1, keepdims=True))
+            p = (e * (1.0 / row_sum(e))).astype(BF)
+            pbuf[d * n_blk + i] = p
+            out = one_of_two(mm(p, v))
+            lo[d, pl.ds(at, blk), :] = (out * valid_rows(d, at, blk)).astype(BF)
+            return carry
+
+        lax.fori_loop(0, n_blk, body, 0)
+
+    def three_heads(v):
+        lane = lax.broadcasted_iota(jnp.int32, v.shape, 1)
+        zero = jnp.zeros_like(v)
+        return jnp.concatenate(
+            [jnp.where((lane // HD == h) | (lane >= wh), v, zero) for h in range(wh // HD)], axis=0
+        )
+
+    def one_of_three(v):
+        lane = lax.broadcasted_iota(jnp.int32, (slots, 256), 1)
+        total = jnp.zeros((slots, 256), F32)
+        for h in range(wh // HD):
+            total = jnp.where(lane // HD == h, v[h * slots : (h + 1) * slots], total)
+        return total
+
+    def keys_of(d, at):
+        return kvall[:, mine(d), at : at + 256].reshape(n_seq * slots, 256)
+
+    def heavy_attention(d):
+        q3 = three_heads(hqx[mine(d), :])
+        scores = mmt(q3, keys_of(d, 0)) * HD ** (-0.5)
+        e = jnp.exp(scores - jnp.max(scores, axis=-1, keepdims=True))
+        p = (e * (1.0 / row_sum(e))).astype(BF)
+        ph[d] = p
+        hox[mine(d), :] = one_of_three(mm(p, keys_of(d, 256))).astype(BF)
+
+    halo_wait(0)
+    light_attention(0)
+    forwards = []
+    for k in range(1, nz):
+        block = kvall.at[2 * zpeer(nz - k) + core]
+        arrived(block, ag_s.at[k], ag_r.at[k], same_core(nz - k))
+        late.append(send(block, block, fw_s.at[k], fw_r.at[k], sibling))
+    halo_wait(1)
+    light_attention(1)
+    arrived(kvall.at[s + 1 - 2 * core], ag_s.at[0], ag_r.at[0], sibling)
+    for k in range(1, nz):
+        block = kvall.at[2 * zpeer(nz - k) + 1 - core]
+        arrived(block, fw_s.at[k], fw_r.at[k], sibling)
+
+    loads["who"].wait()
+    loads["wol"].wait()
+
+    def attention_terms(d):
+        heavy_attention(d)
+        proj = (mmt(hox[mine(d), 0:wh], who[...]) * cols[SQ, mine(d), :]).astype(BF)
+        for h in range(2):
+            r = pl.ds(h * half, half)
+            value = mmt(lo[d, r, :], wol[...]) + mm(pqkt[d, r, 0:slots], proj)
+            parts[d, r, :] = value.astype(BF)
+            ar_start(0, d, h)
+
+    attention_terms(0)
+    attention_terms(1)
+    ar_step(0, 0, 1, tot1)
+
+    for name in ("cot", "wdl", "wdh"):
+        loads[name].wait()
+
+    def light_pre(d):
+        def body(t):
+            r = pl.ds(t, half)
+            dm[d, r, :] = mm(cot[d, r, :], wdl[...]) * valid_rows(d, t, half)
+
+        tiles(rows, half, body)
+        grow[mine(d), :] = mm(pqk[d, 0:slots, :], cot[d]).astype(BF)
+
+    light_pre(0)
+    ar_step(0, 0, 2, tot1)
+    ar_step(0, 1, 1, tot1)
+    light_pre(1)
+    dmh[...] = mm(grow[...], wdh[...])
+    ar_step(0, 0, 3, tot1)
+    ar_step(0, 1, 2, tot1)
+    for name in ("gl", "ul", "gh", "uh"):
+        loads[name].wait()
+
+    gains[...] = jnp.zeros(gains.shape, F32)
+
+    def hidden_rows(d, r):
+        return tok[d, r, :].astype(F32) + tot1[d, r, :].astype(F32)
+
+    def ffn_norm(d):
+        def body(t):
+            r = pl.ds(t, 32)
+            hidden = hidden_rows(d, r)
+            inv = lax.rsqrt(row_sum(hidden * hidden) * (1.0 / width) + epsilon)
+            invf[d, r, :] = inv
+            fl[d, r, :] = (hidden * inv * gain_f).astype(BF)
+
+        tiles(rows, 32, body)
+
+    def ffn_heavy(d):
+        live = jnp.where(idxc[0:slots, d : d + 1] >= 0, 1.0, 0.0).astype(F32)
+        rowsf = mm(pqk[d, 0:slots, :], fl[d])
+        score = jax.nn.sigmoid(row_sum(rowsf * router_f)) * live
+        cols[SF, mine(d), :] = score
+        frow[mine(d), :] = rowsf.astype(BF)
+        ghr[mine(d), :] = (grow[mine(d), :].astype(F32) * score).astype(BF)
+        step = 256
+
+        def body(t, dscore):
+            c = pl.ds(pl.multiple_of(t * step, step), step)
+            c2 = pl.ds(pl.multiple_of(fh_n + t * step, step), step)
+            gate = mm(frow[mine(d), :], wguh[:, c]).astype(BF).astype(F32)
+            up = mm(frow[mine(d), :], wguh[:, c2]).astype(BF).astype(F32)
+            act, slope = gelu_parts(gate)
+            middle = (act * up).astype(BF)
+            raw = dmh[mine(d), c]
+            grad_mid = raw * score
+            midh[mine(d), c] = middle
+            dguh[mine(d), c] = (grad_mid * up * slope).astype(BF)
+            dguh[mine(d), c2] = (grad_mid * act).astype(BF)
+            return dscore + row_sum(middle.astype(F32) * raw)
+
+        dscore = lax.fori_loop(0, fh_n // step, body, jnp.zeros((slots, 1), F32))
+        pre = dscore * score * (1.0 - score)
+        cols[PREF, mine(d), :] = pre
+        return (mmt(dguh[mine(d), :], wguh[...]) + pre * router_f).astype(BF)
+
+    def add_gain(which, values):
+        count = values.shape[0]
+        gains[which] += jnp.sum(values.reshape(count // 8, 8, width), axis=0)
+
+    def ffn_light(d, back_rows, between):
+        for h in range(2):
+            r = pl.ds(h * half, half)
+            gu = mm(fl[d, r, :], wgul[...]).astype(BF)
+            gate = gu[:, 0:fl_n].astype(F32)
+            up = gu[:, fl_n : 2 * fl_n].astype(F32)
+            act, slope = gelu_parts(gate)
+            mid[d, r, :] = (act * up * valid_rows(d, h * half, half)).astype(BF)
+            grad_mid = dm[d, r, :]
+            dgu[d, r, 0:fl_n] = (grad_mid * up * slope).astype(BF)
+            dgu[d, r, fl_n : 2 * fl_n] = (grad_mid * act).astype(BF)
+            value = mmt(dgu[d, r, :], wgul[...]) + mm(pqkt[d, r, 0:slots], back_rows)
+            parts[d, r, :] = value.astype(BF)
+            ar_start(1, d, h)
+
+            def gain_body(t, d=d, h=h):
+                rr = pl.ds(pl.multiple_of(h * half + t, 32), 32)
+                unit = hidden_rows(d, rr) * invf[d, rr, :]
+                add_gain(1, parts[d, rr, :].astype(F32) * unit)
+
+            tiles(half, 32, gain_body)
+            if h == 0:
+                between()
+
+    def nothing():
+        pass
+
+    ar_step(0, 0, 4, tot1)
+    ffn_norm(0)
+    back0 = ffn_heavy(0)
+    ar_step(0, 1, 3, tot1)
+    ffn_light(0, back0, nothing)
+    ar_step(0, 1, 4, tot1)
+    ffn_norm(1)
+    back1 = ffn_heavy(1)
+    ar_step(1, 0, 1, tot2)
+    ffn_light(1, back1, nothing)
+    ar_step(1, 0, 2, tot2)
+    tot_copy = pltpu.make_async_copy(tot1, tot_o, out_s.at[0])
+    tot_copy.start()
+
+    grads = ((g_h, ra_h, rb_h), (g_l, ra_l, rb_l), (g_a, ra_a, rb_a))
+    packed_at = (0, g_h.shape[1], g_h.shape[1] + g_l.shape[1])
+
+    def chunk_rows(zz, cc):
+        return pl.ds(pl.multiple_of(chunk * (2 * zz + cc), chunk), chunk)
+
+    def rs_start(p):
+        grad, ra, rb = grads[p]
+        for zz in range(nz):
+            late.append(send(
+                grad.at[chunk_rows(zz, 1 - core), pl.ds(0, ra.shape[2])], ra.at[zz],
+                wa_s.at[p, zz], wa_r.at[p, zz], sibling,
+            ))
+
+    def rs_middle(p):
+        grad, ra, rb = grads[p]
+        cut = ra.shape[2]
+        for k in range(1, nz + 1):
+            zz = zpeer(k)
+            arrived(ra.at[zz], wa_s.at[p, zz], wa_r.at[p, zz], sibling)
+
+            def add_body(t, carry):
+                r = pl.ds(pl.multiple_of(chunk * (2 * zz + core) + 16 * t, 16), 16)
+                value = grad[r, 0:cut].astype(F32) + ra[zz, pl.ds(pl.multiple_of(16 * t, 16), 16), :].astype(F32)
+                grad[r, 0:cut] = value.astype(BF)
+                return carry
+
+            lax.fori_loop(0, chunk // 16, add_body, 0)
+            if k < nz:
+                late.append(send(
+                    grad.at[chunk_rows(zz, core), pl.ds(0, cut)], rb.at[k - 1],
+                    wz_s.at[p, k - 1], wz_r.at[p, k - 1], same_core(k),
+                ))
+
+    def rs_end(p):
+        grad, ra, rb = grads[p]
+        cut = ra.shape[2]
+        for k in range(1, nz):
+            arrived(rb.at[k - 1], wz_s.at[p, k - 1], wz_r.at[p, k - 1], same_core(nz - k))
+
+        def add_body(t, carry):
+            r = pl.ds(pl.multiple_of(16 * t, 16), 16)
+            value = grad[pl.ds(pl.multiple_of(chunk * s + 16 * t, 16), 16), 0:cut].astype(F32)
+            for k in range(1, nz):
+                value = value + rb[k - 1, r, :].astype(F32)
+            packed[r, packed_at[p] : packed_at[p] + cut] = value
+            return carry
+
+        lax.fori_loop(0, chunk // 16, add_body, 0)
+
+    def heavy_ffn_grads():
+        step = 512
+        for src, gr, base, total in ((frow, dguh, 0, 2 * fh_n), (ghr, midh, 2 * fh_n, fh_n)):
+            for t in range(2):
+                f = slice(t * (width // 2), (t + 1) * (width // 2))
+                left_t = src[:, f].T
+
+                def body(i, carry, gr=gr, f=f, base=base, left_t=left_t):
+                    c = pl.ds(pl.multiple_of(i * step, step), step)
+                    o = pl.ds(pl.multiple_of(base + i * step, step), step)
+                    g_h[f, o] = mm(left_t, gr[:, c]).astype(BF)
+                    return carry
+
+                lax.fori_loop(0, total // step, body, 0)
+
+    def all_rows(ref, f):
+        return ref[:, :, f].reshape(docs * rows, ref[:, :, f].shape[2])
+
+    def light_grad(src, gr, ref, base):
+        for t in range(2):
+            f = slice(t * (width // 2), (t + 1) * (width // 2))
+            right_side = gr[...].reshape(docs * rows, gr.shape[2])
+            ref[f, base : base + gr.shape[2]] = tmm(all_rows(src, f), right_side).astype(BF)
+
+    heavy_ffn_grads()
+    rs_start(0)
+    ar_step(1, 1, 1, tot2)
+    ar_step(1, 0, 3, tot2)
+    light_grad(fl, dgu, g_l, 0)
+    light_grad(cot, mid, g_l, 2 * fl_n)
+    rs_start(1)
+    rs_middle(0)
+    ar_step(1, 1, 2, tot2)
+
+    def mixed_terms(d):
+        def body(j, carry):
+            w = pl.ds(pl.multiple_of(j * share, share), share)
+            heavy = (mmt(midh[mine(d), :], wdh[w, :]) * cols[SF, mine(d), :]).astype(BF)
+            for h in range(2):
+                r = pl.ds(h * half, half)
+                value = mmt(mid[d, r, :], wdl[w, :]) + mm(pqkt[d, r, 0:slots], heavy)
+                mixb[j, d, r, :] = value.astype(BF)
+            return carry
+
+        lax.fori_loop(0, 4, body, 0)
+
+    mixed_terms(0)
+    mixed_terms(1)
+    rs_middle(1)
+
+    def hidden_grad(d):
+        def body(t):
+            r = pl.ds(t, 32)
+            unit = hidden_rows(d, r) * invf[d, r, :]
+            w = tot2[d, r, :].astype(F32) * gain_f
+            inner = row_sum(w * unit) * (1.0 / width)
+            value = cot[d, r, :].astype(F32) + invf[d, r, :] * (w - unit * inner)
+            ghf[d, r, :] = value
+            ghb[d, r, :] = value.astype(BF)
+
+        tiles(rows, 32, body)
+
+    def heavy_back(d):
+        picked = mm(pqk[d, 0:slots, :], ghb[d])
+        score = cols[SQ, mine(d), :]
+        gah[mine(d), :] = (picked * score).astype(BF)
+        raw = mm(picked.astype(BF), who[...])
+        pre = row_sum(hox[mine(d), 0:wh].astype(F32) * raw) * score * (1.0 - score)
+        cols[PREQ, mine(d), :] = pre
+        dox[mine(d), 0:wh] = (raw * score).astype(BF)
+        dox[mine(d), wh:256] = jnp.zeros((slots, 256 - wh), BF)
+        do3 = three_heads(dox[mine(d), :])
+        q3 = three_heads(hqx[mine(d), :])
+        p = ph[d]
+        pf = p.astype(F32)
+        dp = mmt(do3, keys_of(d, 256))
+        ds = (pf * (dp - row_sum(dp * pf)) * HD ** (-0.5)).astype(BF)
+        dqh[mine(d), :] = one_of_three(mm(ds, keys_of(d, 0))).astype(BF)
+        dk = tmm(ds, q3).astype(BF).reshape(nz, 2, slots, 256)
+        dv = tmm(p, do3).astype(BF).reshape(nz, 2, slots, 256)
+        for c in range(2):
+            for zz in range(nz):
+                hb[d, c, zz, :, 0:256] = dk[zz, c]
+                hb[d, c, zz, :, 256:512] = dv[zz, c]
+        late.append(send(hb.at[d, 1 - core], h1.at[d], ha_s.at[d], ha_r.at[d], sibling))
+
+    def heavy_back_middle(d):
+        arrived(h1.at[d], ha_s.at[d], ha_r.at[d], sibling)
+        for k in range(1, nz + 1):
+            zz = zpeer(k)
+            value = hb[d, core, zz].astype(F32) + h1[d, zz].astype(F32)
+            hb[d, core, zz] = value.astype(BF)
+            if k < nz:
+                late.append(send(
+                    hb.at[d, core, zz], h2.at[d, k - 1], hz_s.at[d, k - 1], hz_r.at[d, k - 1], same_core(k)
+                ))
+
+    def heavy_back_end(d):
+        for k in range(1, nz):
+            arrived(h2.at[d, k - 1], hz_s.at[d, k - 1], hz_r.at[d, k - 1], same_core(nz - k))
+        value = hb[d, core, z].astype(F32)
+        for k in range(1, nz):
+            value = value + h2[d, k - 1].astype(F32)
+        dkvh[mine(d), :] = value.astype(BF)
+
+    def light_back(d):
+        dkvw[d] = jnp.zeros((rows + 2 * radius, 2 * wl), F32)
+
+        def dol_body(t):
+            r = pl.ds(t, half)
+            dol[d, r, :] = (mm(ghb[d, r, :], wol[...]) * valid_rows(d, t, half)).astype(BF)
+
+        tiles(rows, half, dol_body)
+
+        def body(i, carry):
+            at = pl.multiple_of(i * blk, blk)
+            q2 = two_heads(qbuf[d, pl.ds(at, blk), :])
+            do2 = two_heads(dol[d, pl.ds(at, blk), :])
+            k = kvw[d, pl.ds(at, span), 0:wl]
+            v = kvw[d, pl.ds(at, span), wl : 2 * wl]
+            p = pbuf[d * n_blk + i]
+            pf = p.astype(F32)
+            dp = mmt(do2, v)
+            ds = (pf * (dp - row_sum(dp * pf)) * HD ** (-0.5)).astype(BF)
+            dqkv[d, pl.ds(at, blk), 0:wl] = one_of_two(mm(ds, k)).astype(BF)
+            dkvw[d, pl.ds(at, span), 0:wl] += tmm(ds, q2)
+            dkvw[d, pl.ds(at, span), wl : 2 * wl] += tmm(p, do2)
+            return carry
+
+        lax.fori_loop(0, n_blk, body, 0)
+        rims[d, 0] = dkvw[d, 0:radius, :].astype(BF)
+        rims[d, 1] = dkvw[d, rows + radius : rows + 2 * radius, :].astype(BF)
+
+        @pl.when(s == 0)
+        def _():
+            rimr[d, 0] = jnp.zeros((radius, 2 * wl), BF)
+
+        @pl.when(s == last)
+        def _():
+            rimr[d, 1] = jnp.zeros((radius, 2 * wl), BF)
+
+        late.append((s > 0, send(rims.at[d, 0], rimr.at[d, 1], rim_s.at[d, 0], rim_r.at[d, 0], left, s > 0)))
+        late.append((s < last, send(rims.at[d, 1], rimr.at[d, 0], rim_s.at[d, 1], rim_r.at[d, 1], right, s < last)))
+
+    def rim_wait(d):
+        @pl.when(s < last)
+        def _():
+            arrived(rimr.at[d, 1], rim_s.at[d, 0], rim_r.at[d, 0], right)
+
+        @pl.when(s > 0)
+        def _():
+            arrived(rimr.at[d, 0], rim_s.at[d, 1], rim_r.at[d, 1], left)
+
+    def attention_back_terms(d):
+        heavy_back_end(d)
+        ds_in = mmt(dkvh[mine(d), 256 : 256 + wh], whv[...])
+        score = cols[SK, mine(d), :]
+        pre_k = row_sum(ds_in * kin[mine(d), :].astype(F32)) * score * (1.0 - score)
+        cols[PREK, mine(d), :] = pre_k
+        key_rows = mmt(dkvh[mine(d), 0:wh], whk[...]) + ds_in * score + pre_k * router_k
+        query_rows = mmt(dqh[mine(d), 0:wh], whq[...]) + cols[PREQ, mine(d), :] * router_q
+        both = jnp.concatenate([query_rows, key_rows], axis=0).astype(BF)
+        rim_wait(d)
+        dkvw[d, radius : 2 * radius, :] += rimr[d, 0].astype(F32)
+        dkvw[d, rows : rows + radius, :] += rimr[d, 1].astype(F32)
+        for h in range(2):
+            r = pl.ds(h * half, half)
+            dqkv[d, r, wl : 3 * wl] = dkvw[d, pl.ds(h * half + radius, half), :].astype(BF)
+            value = mmt(dqkv[d, r, :], wqkv[...]) + mm(pqkt[d, r, :], both)
+            parts[d, r, :] = value.astype(BF)
+            ar_start(2, d, h)
+
+            def gain_body(t, d=d, h=h):
+                rr = pl.ds(pl.multiple_of(h * half + t, 32), 32)
+                unit = tok[d, rr, :].astype(F32) * inva[d, rr, :]
+                add_gain(0, parts[d, rr, :].astype(F32) * unit)
+
+            tiles(half, 32, gain_body)
+
+    def token_grad(d):
+        def body(t):
+            r = pl.ds(t, 32)
+            inv = inva[d, r, :]
+            unit = tok[d, r, :].astype(F32) * inv
+            w = tot2[d, r, :].astype(F32) * gain_a
+            inner = row_sum(w * unit) * (1.0 / width)
+            ghf[d, r, :] = ghf[d, r, :] + inv * (w - unit * inner)
+
+        tiles(rows, 32, body)
+        copy = pltpu.make_async_copy(ghf.at[d], gt_o.at[d], out_s.at[1 + d])
+        copy.start()
+        return copy
+
+    ar_step(1, 0, 4, tot2)
+    hidden_grad(0)
+    heavy_back(0)
+    ar_step(1, 1, 3, tot2)
+    light_back(0)
+    heavy_back_middle(0)
+    ar_step(1, 1, 4, tot2)
+    for k in range(1, 4):
+        to = (b + k) % 4
+        late.append(send(mixb.at[to], mixr.at[k - 1], mx_s.at[k - 1], mx_r.at[k - 1], (to, s)))
+    hidden_grad(1)
+    heavy_back(1)
+    ar_sent(1, 0)
+    attention_back_terms(0)
+    light_back(1)
+    heavy_back_middle(1)
+    ar_step(2, 0, 1, tot2)
+    ar_sent(1, 1)
+    attention_back_terms(1)
+    ar_step(2, 0, 2, tot2)
+    ar_step(2, 1, 1, tot2)
+
+    light_grad(nl, dqkv, g_a, 0)
+    light_grad(ghb, lo, g_a, 3 * wl)
+    at = 4 * wl
+    for src, gr in (
+        (hin, dqh[:, 0:wh]), (kin, dkvh[:, 0:wh]), (sin, dkvh[:, 256 : 256 + wh]), (gah, hox[:, 0:wh])
+    ):
+        g_a[:, at : at + wh] = tmm(src[...], gr).astype(BF)
+        at += 256
+    vector_lane = lax.broadcasted_iota(jnp.int32, (width, 128), 1)
+    lane = lax.broadcasted_iota(jnp.int32, (docs * slots, 128), 1)
+    vectors = jnp.zeros((width, 128), F32)
+    for src, which, at_lane in ((hin, PREQ, 1), (kin, PREK, 2), (frow, PREF, 4)):
+        vectors = vectors + tmm(src[...], jnp.where(lane == at_lane, cols[which], 0.0).astype(BF))
+    for which, at_lane in ((0, 0), (1, 3)):
+        vectors = jnp.where(vector_lane == at_lane, row_sum(gains[which].T), vectors)
+    g_a[:, at : at + 128] = vectors.astype(BF)
+    rs_start(2)
+    ar_step(2, 0, 3, tot2)
+    ar_step(2, 1, 2, tot2)
+    rs_end(0)
+    rs_middle(2)
+    ar_step(2, 0, 4, tot2)
+    out_copies = [tot_copy, token_grad(0)]
+    ar_step(2, 1, 3, tot2)
+    rs_end(1)
+
+    for k in range(1, 4):
+        frm = (b + 4 - k) % 4
+        arrived(mixr.at[k - 1], mx_s.at[k - 1], mx_r.at[k - 1], (frm, s))
+    for d in range(docs):
+
+        def mix_body(t, d=d):
+            r = pl.ds(t, 64)
+            value = mixb[b, d, r, :].astype(F32)
+            for k in range(3):
+                value = value + mixr[k, d, r, :].astype(F32)
+            dm[d, r, 0:share] = value
+
+        tiles(rows, 64, mix_body)
+    mix_copy = pltpu.make_async_copy(dm, mix_o, out_s.at[3])
+    mix_copy.start()
+    out_copies.append(mix_copy)
+    ar_step(2, 1, 4, tot2)
+    out_copies.append(token_grad(1))
+    rs_end(2)
+    va = packed.shape[1] - 128
+    vbuf[...] = packed[:, va : va + 128]
+    for k in range(1, 4):
+        late.append(send(vbuf, vr.at[k - 1], v_s.at[k - 1], v_r.at[k - 1], ((b + k) % 4, s)))
+    for k in range(1, 4):
+        arrived(vr.at[k - 1], v_s.at[k - 1], v_r.at[k - 1], ((b + 4 - k) % 4, s))
+    packed[:, va : va + 128] = vbuf[...] + vr[0] + vr[1] + vr[2]
+    pack_copy = pltpu.make_async_copy(packed, pack_o, out_s.at[4])
+    pack_copy.start()
+    out_copies.append(pack_copy)
+
+    for entry in late:
+        if isinstance(entry, tuple):
+            pl.when(entry[0])(entry[1].wait_send)
+        else:
+            entry.wait_send()
+    for d in range(docs):
+        ar_sent(0, d)
+        ar_sent(2, d)
+    for copy in out_copies:
+        copy.wait()
+
+
+def kernel_scratch(docs, rows, width, slots, n_seq, wl, wh, fl_n, fh_n):
+    nz = n_seq // 2
+    chunk = width // n_seq
+    routed = docs * slots
+    keys = n_seq * slots
+    pad = -(-wh // 256) * 256
+    ga_n = 4 * wl + 4 * pad + 128
+    h_n, l_n = 3 * fh_n, 3 * fl_n
+    radius = WINDOW // 2
+    span = rows + 2 * radius
+    vmem = [
+        ((docs, rows, width), BF), ((docs, rows, width), BF), ((width, 3 * wl), BF), ((width, wl), BF),
+        ((width, wh), BF), ((width, wh), BF), ((width, wh), BF), ((width, wh), BF),
+        ((width, 2 * fl_n), BF), ((width, fl_n), BF), ((width, 2 * fh_n), BF), ((width, fh_n), BF),
+        ((docs, rows, width), BF), ((docs, rows, 1), F32), ((routed, width), BF), ((routed, width), BF),
+        ((routed, width), BF), ((docs, rows, wl), BF), ((docs, span, 2 * wl), BF),
+        ((docs * rows // WINDOW, 2 * WINDOW, 2 * WINDOW), BF), ((docs, rows, wl), BF), ((routed, pad), BF),
+        ((n_seq, routed, 2 * pad), BF), ((docs, wh // HD * slots, keys), BF), ((routed, pad), BF),
+        ((docs, 2 * slots, rows), BF), ((docs, rows, 2 * slots), BF), ((docs, rows, width), BF),
+        ((docs, rows, width), BF), ((docs, rows, width), BF), ((docs, 2, rows // 4, width), BF),
+        ((docs, 2, rows // 8, width), BF), ((6, routed, 1), F32),
+        ((docs, rows, fl_n), F32), ((routed, fh_n), F32), ((routed, width), BF), ((docs, rows, width), BF),
+        ((docs, rows, 1), F32), ((docs, rows, fl_n), BF), ((docs, rows, 2 * fl_n), BF), ((routed, width), BF),
+        ((routed, width), BF), ((routed, fh_n), BF), ((routed, 2 * fh_n), BF),
+        ((4, docs, rows, width // 4), BF), ((3, docs, rows, width // 4), BF), ((docs, rows, width), F32),
+        ((docs, rows, width), BF), ((docs, rows, wl), BF), ((routed, pad), BF), ((routed, width), BF),
+        ((routed, pad), BF), ((docs, span, 2 * wl), F32), ((docs, 2, radius, 2 * wl), BF),
+        ((docs, 2, radius, 2 * wl), BF), ((docs, rows, 3 * wl), BF),
+        ((docs, 2, nz, slots, 2 * pad), BF), ((docs, nz, slots, 2 * pad), BF),
+        ((docs, nz - 1, slots, 2 * pad), BF), ((routed, 2 * pad), BF), ((2, 8, width), F32),
+        ((width, h_n), BF), ((width, l_n), BF),
+        ((nz, chunk, h_n), BF), ((nz, chunk, l_n), BF), ((nz, chunk, ga_n), BF),
+        ((nz - 1, chunk, h_n), BF), ((nz - 1, chunk, l_n), BF), ((nz - 1, chunk, ga_n), BF),
+        ((chunk, h_n + l_n + ga_n), F32), ((chunk, 128), F32), ((3, chunk, 128), F32),
+    ]
+    sems = [
+        (16,), (3, docs, 2, 4), (3, docs, 2, 4), (nz,), (nz,), (nz,), (nz,), (docs, 2), (docs, 2),
+        (docs, 2), (docs, 2), (docs,), (docs,), (docs, nz - 1), (docs, nz - 1), (3,), (3,),
+        (3, nz), (3, nz), (3, nz - 1), (3, nz - 1), (3,), (3,), (5,),
+    ]
+    total = 0
+    for shape, kind in vmem:
+        lanes = -(-shape[-1] // 128) * 128
+        total += math.prod(shape[:-1]) * lanes * jnp.dtype(kind).itemsize
+    return vmem, sems, total
+
+
+def shards(sizes, *args):
+    (tokens, cotangent, lengths, query_index, key_index, gain_attn, router_query, router_key, wq_light,
+     wk_light, wv_light, wo_light, wq_heavy, wk_heavy, wv_heavy, wo_heavy, gain_ffn, router_ffn,
+     gate_light, up_light, down_light, gate_heavy, up_heavy, down_heavy) = args
+    n_seq = sizes["seq"]
+    docs, rows, width = tokens.shape
+    slots = query_index.shape[1]
+    wl, wh = wq_light.shape[1], wq_heavy.shape[1]
+    fl_n, fh_n = gate_light.shape[1], gate_heavy.shape[1]
+    dims = (docs, rows, width, slots, n_seq, wl, wh, fl_n, fh_n)
+    vmem, sems, total = kernel_scratch(*dims)
+    fits = (
+        total <= 60 * 2**20
+        and sizes["branch"] == 4
+        and n_seq % 2 == 0
+        and width % (16 * n_seq) == 0
+        and wl == 2 * HD
+        and wh == 3 * HD
+        and slots % 16 == 0
+        and rows % 256 == 0
+    )
+    if not fits:
+        return plain_shards(*args)
+    share = width // 4
+    chunk = width // n_seq
+    ga_n = 4 * wl + 4 * 256 + 128
+    pack_n = 3 * fh_n + 3 * fl_n + ga_n
+    idx_rows = jnp.concatenate([query_index, key_index], axis=1)
+    vec = jnp.stack(
+        [gain_attn, router_query, router_key, gain_ffn, router_ffn, gain_ffn, gain_ffn, gain_ffn]
+    ).astype(F32)
+    in_hbm = [
+        tokens, cotangent, wq_light, wk_light, wv_light, wo_light, wq_heavy, wk_heavy, wv_heavy, wo_heavy,
+        gate_light, up_light, down_light, gate_heavy, up_heavy, down_heavy,
+    ]
+    whole = pl.BlockSpec(memory_space=pltpu.VMEM)
+    outside = pl.BlockSpec(memory_space=pl.ANY)
+    grad_tokens, mix, attn_total, packed = pl.pallas_call(
+        functools.partial(layer_kernel, dims),
+        out_shape=[
+            jax.ShapeDtypeStruct((docs, rows, width), F32),
+            jax.ShapeDtypeStruct((docs, rows, fl_n), F32),
+            jax.ShapeDtypeStruct((docs, rows, width), BF),
+            jax.ShapeDtypeStruct((chunk, pack_n), F32),
+        ],
+        in_specs=[pl.BlockSpec(memory_space=pltpu.SMEM), whole, whole, whole] + [outside] * 16,
+        out_specs=[outside] * 4,
+        scratch_shapes=[pltpu.VMEM(shape, kind) for shape, kind in vmem]
+        + [pltpu.SemaphoreType.DMA(shape) for shape in sems],
+        compiler_params=pltpu.CompilerParams(
+            collective_id=0, has_side_effects=True, vmem_limit_bytes=64 * 2**20 - 2**16
+        ),
+    )(lengths, vec, idx_rows.T, idx_rows, *in_hbm)
+    own = lax.axis_index("branch") * share
+    mixed = mix[:, :, :share] + (
+        lax.dynamic_slice_in_dim(tokens, own, share, 2).astype(F32)
+        + lax.dynamic_slice_in_dim(attn_total, own, share, 2).astype(F32)
+    )
+
+    def part(at, wide):
+        return packed[:, at : at + wide]
+
+    l_at = 3 * fh_n
+    a_at = l_at + 3 * fl_n
+    h_at = a_at + 4 * wl
+    v_at = h_at + 4 * 256
+    return (
+        mixed, grad_tokens,
+        packed[:, v_at], packed[:, v_at + 1], packed[:, v_at + 2],
+        part(a_at, wl), part(a_at + wl, wl), part(a_at + 2 * wl, wl), part(a_at + 3 * wl, wl),
+        part(h_at, wh), part(h_at + 256, wh), part(h_at + 512, wh), part(h_at + 768, wh),
+        packed[:, v_at + 3], packed[:, v_at + 4],
+        part(l_at, fl_n), part(l_at + fl_n, fl_n), part(l_at + 2 * fl_n, fl_n),
+        part(0, fh_n), part(fh_n, fh_n), part(2 * fh_n, fh_n),
+    )
+
+
 def solution(mesh):
     return jax.shard_map(
-        shards,
+        functools.partial(shards, dict(mesh.shape)),
         mesh=mesh,
         in_specs=(
             P(None, "seq", None),

time: 572 us -> 235 us (0.41)
  the two profiles are of different devices: /device:TPU:0 before, /device:TPU:26 now
where the time goes in v2:
time: 235 us; the launch traced here: 234 us
  Pallas kernels  211 us (90%)
  local copies, waits for them, and re-layouts  17.6 us (7%)
  other arithmetic  4.97 us (2%)
    pallas_call x1, Pallas kernels, shards(): pl.pallas_call(functools.partial(layer_kernel, dims), out_shape=[jax.Shap...  211 us
    unnamed x12, local copies, waits for them, and re-layouts  9.43 us

profile of v2, /device:TPU:26, one launch (start us, length us, event | category | flops | bytes accessed | tf_op | source)
XLA Modules:
  0.0 234.4 jit_solution(12020262942496431074)
XLA Ops:
  0.7 0.0 copy-start.2
  0.7 0.7 stack.21
  1.4 0.7 stack.22
  2.1 0.7 stack.23
  2.8 0.7 stack.24
  3.5 0.7 stack.25
  4.2 0.6 convert_element_type.9.refs_1_
  4.8 0.8 fusion.4
  5.6 0.7 copy.51.refs_2_
  6.3 1.3 pad_add_fusion.refs_3_
  7.6 1.9 copy.52.refs_10_
  9.5 1.9 copy.53.refs_11_
  11.4 1.9 copy.54.refs_12_
  13.3 0.0 copy-done.2
  13.3 0.9 copy.55.refs_13_
  14.2 211.1 %shard_map.391 = (f32[2,512,768]{2,1,0:T(8,128)}, f32[2,512,256]{2,1,0:T(8,128)}, bf16[2,512,768]{2,1,0:T(8,128)(2,1)}, f32[96,5504]{1,0:T(8,128)}) custom-call(s32[2]{0:T(128)} %refs_0_.1, f32[8,768]{1,0:T(8,128)} %convert_element_type.9.refs_1_, s32[128,2]{1,0:T(8,128)} %copy.51.refs_2_, s32[2,128]{1,0:T(2,128)} %pad_add_fusion.refs_3_, ...), custom_call_target="tpu_custom_call" | custom-call | tf_op jit(solution)/shard_map/pallas_call | solution.py:1306
  225.3 0.0 copy-start.1
  225.3 2.3 add_add_fusion
  227.6 1.2 copy.56
  228.8 0.0 copy-done.1
  228.8 0.8 slice_reduce_fusion
  229.5 0.0 copy-start
  229.5 0.7 fusion.3
  230.2 0.7 fusion.2
  231.0 0.7 fusion.1
  231.7 1.0 fusion
  232.7 0.0 copy-done
  232.7 1.7 copy.58
  (1 shorter events, 0.0 us)
Async XLA Ops:
  0.7 12.6 %copy-start.2 = (bf16[768,192]{0,1:T(8,128)(2,1)S(1)}, bf16[768,192]{0,1:T(8,128)(2,1)}, u32[]{:S(2)}) copy-start(bf16[768,192]{0,1:T(8,128)(2,1)} %param.39) | copy-start | bytes 884740
  225.3 3.5 %copy-start.1 = (f32[96,5504]{1,0:T(8,128)S(1)}, f32[96,5504]{1,0:T(8,128)}, u32[]{:S(2)}) copy-start(f32[96,5504]{1,0:T(8,128)} %get-tuple-element.28) | copy-start | bytes 6340612
  229.5 3.2 %copy-start = (f32[2,512,768]{2,1,0:T(8,128)S(1)}, f32[2,512,768]{2,1,0:T(8,128)}, u32[]{:S(2)}) copy-start(f32[2,512,768]{2,1,0:T(8,128)} %get-tuple-element.112) | copy-start | bytes 9437188

commit v3 on v2

--- a/solution.py
+++ b/solution.py
@@ -438,20 +438,19 @@
     def take(count):
         return [next(it) for _ in range(count)]
 
-    lens, vec, idxc, idxr = take(4)
+    lens, qi, ki, ga_v, rq_v, rk_v, gf_v, rf_v = take(8)
     (tok_h, cot_h, wql_h, wkl_h, wvl_h, wol_h, wqh_h, wkh_h, wvh_h, woh_h,
      gl_h, ul_h, dl_h, gh_h, uh_h, dh_h) = take(16)
-    gt_o, mix_o, tot_o, pack_o = take(4)
-    (tok, cot, wqkv, wol, whq, whk, whv, who, wgul, wdl, wguh, wdh) = take(12)
-    (nl, inva, hin, kin, sin, qbuf, kvw, pbuf, lo, hqx, kvall, ph, hox) = take(13)
+    gt_o, mix_o, pack_o, vec_o = take(4)
+    (tok, cot, wqkv, wol, whq, whk, whv, who, wgul, wdl, wguh, wdh, wkeep) = take(13)
+    (nl, inva, hin, kin, sin, qbuf, kvw, pbuf, lo, hqx, kvall, ph, hox, qall, doall) = take(15)
     (pqk, pqkt, parts, tot1, tot2, r1, r2, cols) = take(8)
     (dm, dmh, grow, fl, invf, mid, dgu, frow, ghr, midh, dguh) = take(11)
-    (mixb, mixr, ghf, ghb, dol, dox, gah, dqh, dkvw, rims, rimr, dqkv) = take(12)
-    (hb, h1, h2, dkvh, gains) = take(5)
-    (g_h, g_l, ra_h, ra_l, ra_a, rb_h, rb_l, rb_a, packed, vbuf, vr) = take(11)
+    (mixb, mixr, mixa, ghf, ghb, dol, dox, gah, dqh, dkvw, rims, rimr, dqkv, dkvh) = take(14)
+    (g_h, g_l, ra_h, ra_l, ra_a, rb_h, rb_l, rb_a, rl_h, rl_l, rl_a, packed, vbuf, vr, vect) = take(15)
     g_a = wguh
-    (load_s, ar_s, ar_r, ag_s, ag_r, fw_s, fw_r, halo_s, halo_r, rim_s, rim_r, ha_s, ha_r, hz_s, hz_r,
-     mx_s, mx_r, wa_s, wa_r, wz_s, wz_r, v_s, v_r, out_s) = take(24)
+    (load_s, ar_s, ar_r, ag_s, ag_r, fw_s, fw_r, halo_s, halo_r, rim_s, rim_r,
+     mx_s, mx_r, wa_s, wa_r, wz_s, wz_r, rl_s, rl_r, v_s, v_r, out_s) = take(22)
 
     b = lax.axis_index("branch")
     s = lax.axis_index("seq")
@@ -510,6 +509,9 @@
     load("ul", ul_h, wgul.at[:, fl_n : 2 * fl_n], 13)
     load("gh", gh_h, wguh.at[:, 0:fh_n], 14)
     load("uh", uh_h, wguh.at[:, fh_n : 2 * fh_n], 15)
+    own_rows = pl.ds(pl.multiple_of(chunk * s, chunk), chunk)
+    load("gk", gh_h.at[own_rows], wkeep.at[:, 0:fh_n], 16)
+    load("uk", uh_h.at[own_rows], wkeep.at[:, fh_n : 2 * fh_n], 17)
 
     barrier = pltpu.get_barrier_semaphore()
     for k in range(1, 4):
@@ -522,15 +524,24 @@
     lax.fori_loop(1, n_seq, greet, 0)
     pl.semaphore_wait(barrier, 3 + n_seq - 1)
 
-    gain_a = vec[0:1, :]
-    router_q = vec[1:2, :]
-    router_k = vec[2:3, :]
-    gain_f = vec[3:4, :]
-    router_f = vec[4:5, :]
+    gain_a, router_q, router_k, gain_f, router_f = [
+        ref[...].astype(F32).reshape(1, width) for ref in (ga_v, rq_v, rk_v, gf_v, rf_v)
+    ]
+
+    def as_column(row):
+        count = row.shape[1]
+        square = lax.broadcasted_iota(jnp.int32, (count, count), 0)
+        same = square == lax.broadcasted_iota(jnp.int32, (count, count), 1)
+        return row_sum(jnp.where(same, row.astype(F32), 0.0)).astype(jnp.int32)
+
+    idx_row = [[ref[d : d + 1, :] for ref in (qi, ki)] for d in range(docs)]
+    idx_col = [[as_column(row) for row in idx_row[d]] for d in range(docs)]
 
     def valid_rows(d, first, count):
         at = lax.broadcasted_iota(jnp.int32, (count, 1), 0) + (offset + first)
         return jnp.where(at < lens[d], 1.0, 0.0).astype(F32)
+
+    big = 64
 
     def tiles(count, size, body):
         def step(t, carry):
@@ -600,19 +611,24 @@
     for d in range(docs):
 
         def norm_body(t, d=d):
-            r = pl.ds(t, 32)
+            r = pl.ds(t, big)
             x = tok[d, r, :].astype(F32)
             inv = lax.rsqrt(row_sum(x * x) * (1.0 / width) + epsilon)
             inva[d, r, :] = inv
             nl[d, r, :] = (x * inv * gain_a).astype(BF)
 
-        tiles(rows, 32, norm_body)
+        tiles(rows, big, norm_body)
 
     for d in range(docs):
-        lane_pos = lax.broadcasted_iota(jnp.int32, (2 * slots, rows), 1) + offset
-        pqk[d] = jnp.where(idxc[:, d : d + 1] == lane_pos, 1.0, 0.0).astype(BF)
-        sub_pos = lax.broadcasted_iota(jnp.int32, (rows, 2 * slots), 0) + offset
-        pqkt[d] = jnp.where(idxr[d : d + 1, :] == sub_pos, 1.0, 0.0).astype(BF)
+        lane_pos = lax.broadcasted_iota(jnp.int32, (slots, rows), 1) + offset
+        sub_pos = lax.broadcasted_iota(jnp.int32, (rows, slots), 0) + offset
+        for i in range(2):
+            here = slice(i * slots, (i + 1) * slots)
+            pqk[d, here, :] = jnp.where(idx_col[d][i] == lane_pos, 1.0, 0.0).astype(BF)
+            pqkt[d, :, here] = jnp.where(idx_row[d][i] == sub_pos, 1.0, 0.0).astype(BF)
+
+    def alive(d, i):
+        return jnp.where(idx_col[d][i] >= 0, 1.0, 0.0).astype(F32)
 
     SQ, SK, SF, PREQ, PREF, PREK = range(6)
 
@@ -620,10 +636,9 @@
         return slice(d * slots, (d + 1) * slots)
 
     for d in range(docs):
-        live = jnp.where(idxc[:, d : d + 1] >= 0, 1.0, 0.0).astype(F32)
         picked = mm(pqk[d], nl[d])
-        score_q = jax.nn.sigmoid(row_sum(picked[:slots] * router_q)) * live[:slots]
-        score_k = jax.nn.sigmoid(row_sum(picked[slots:] * router_k)) * live[slots:]
+        score_q = jax.nn.sigmoid(row_sum(picked[:slots] * router_q)) * alive(d, 0)
+        score_k = jax.nn.sigmoid(row_sum(picked[slots:] * router_k)) * alive(d, 1)
         cols[SQ, mine(d), :] = score_q
         cols[SK, mine(d), :] = score_k
         hin[mine(d), :] = picked[:slots].astype(BF)
@@ -631,21 +646,40 @@
         sin[mine(d), :] = (picked[slots:] * score_k).astype(BF)
         pad_lane = lax.broadcasted_iota(jnp.int32, (slots, 256 - wh), 1)
         kvall[s, mine(d), wh:256] = jnp.where(
-            pad_lane == 0, (1.0 - live[slots:]) * masked_value, 0.0
+            pad_lane == 0, (1.0 - alive(d, 1)) * masked_value, 0.0
         ).astype(BF)
         kvall[s, mine(d), 256 + wh : 512] = jnp.zeros((slots, 256 - wh), BF)
     loads["whk"].wait()
-    kvall[s, :, 0:wh] = mm(kin[...], whk[...]).astype(BF)
+    kvall[s, :, 0:wh] = mmt(kin[...], whk[...]).astype(BF)
     loads["whv"].wait()
-    kvall[s, :, 256 : 256 + wh] = mm(sin[...], whv[...]).astype(BF)
-
-    own_block = kvall.at[s]
-    late.append(send(own_block, own_block, ag_s.at[0], ag_r.at[0], sibling))
-    for k in range(1, nz):
-        late.append(send(own_block, own_block, ag_s.at[k], ag_r.at[k], same_core(k)))
+    kvall[s, :, 256 : 256 + wh] = mmt(sin[...], whv[...]).astype(BF)
+
+    def gather_start(g, ref, part):
+        block = ref.at[s, part]
+        late.append(send(block, block, ag_s.at[g, 0], ag_r.at[g, 0], sibling))
+        for k in range(1, nz):
+            late.append(send(block, block, ag_s.at[g, k], ag_r.at[g, k], same_core(k)))
+
+    def gather_pass(g, ref, part):
+        for k in range(1, nz):
+            block = ref.at[2 * zpeer(nz - k) + core, part]
+            arrived(block, ag_s.at[g, k], ag_r.at[g, k], same_core(nz - k))
+            late.append(send(block, block, fw_s.at[g, k], fw_r.at[g, k], sibling))
+
+    def gather_end(g, ref, part):
+        arrived(ref.at[s + 1 - 2 * core, part], ag_s.at[g, 0], ag_r.at[g, 0], sibling)
+        for k in range(1, nz):
+            block = ref.at[2 * zpeer(nz - k) + 1 - core, part]
+            arrived(block, fw_s.at[g, k], fw_r.at[g, k], sibling)
+
+    def routed(d):
+        return pl.ds(d * slots, slots)
+
+    every = pl.ds(0, docs * slots)
+    gather_start(0, kvall, every)
 
     loads["whq"].wait()
-    hqx[:, 0:wh] = mm(hin[...], whq[...]).astype(BF)
+    hqx[:, 0:wh] = mmt(hin[...], whq[...]).astype(BF)
     pad_lane = lax.broadcasted_iota(jnp.int32, (docs * slots, 256 - wh), 1)
     hqx[:, wh:256] = jnp.where(pad_lane == 0, 8.0, 0.0).astype(BF)
 
@@ -739,34 +773,56 @@
     def keys_of(d, at):
         return kvall[:, mine(d), at : at + 256].reshape(n_seq * slots, 256)
 
+    def spread(column):
+        lane = lax.broadcasted_iota(jnp.int32, (slots, 256 - wh), 1)
+        out = jnp.zeros((slots, 256 - wh), F32)
+        for h in range(wh // HD):
+            value = column[h * slots : (h + 1) * slots]
+            high = value.astype(BF).astype(F32)
+            low = value - high
+            out = jnp.where(lane == 2 * h, high, jnp.where(lane == 2 * h + 1, low, out))
+        return out.astype(BF)
+
+    def own_keys(d, at):
+        v = kvall[s, mine(d), at : at + 256]
+        lane = lax.broadcasted_iota(jnp.int32, v.shape, 1)
+        zero = jnp.zeros_like(v)
+        one = jnp.ones_like(v)
+        return jnp.concatenate(
+            [
+                jnp.where(
+                    lane // HD == h, v, jnp.where((lane == wh + 2 * h) | (lane == wh + 2 * h + 1), one, zero)
+                )
+                for h in range(wh // HD)
+            ],
+            axis=0,
+        )
+
     def heavy_attention(d):
         q3 = three_heads(hqx[mine(d), :])
         scores = mmt(q3, keys_of(d, 0)) * HD ** (-0.5)
-        e = jnp.exp(scores - jnp.max(scores, axis=-1, keepdims=True))
-        p = (e * (1.0 / row_sum(e))).astype(BF)
+        top = jnp.max(scores, axis=-1, keepdims=True)
+        e = jnp.exp(scores - top)
+        sums = row_sum(e)
+        p = (e * (1.0 / sums)).astype(BF)
         ph[d] = p
+        qall[s, mine(d), 0:wh] = hqx[mine(d), 0:wh]
+        qall[s, mine(d), wh:256] = spread((top + jnp.log(sums)) * -(HD**0.5))
         hox[mine(d), :] = one_of_three(mm(p, keys_of(d, 256))).astype(BF)
 
     halo_wait(0)
     light_attention(0)
-    forwards = []
-    for k in range(1, nz):
-        block = kvall.at[2 * zpeer(nz - k) + core]
-        arrived(block, ag_s.at[k], ag_r.at[k], same_core(nz - k))
-        late.append(send(block, block, fw_s.at[k], fw_r.at[k], sibling))
+    gather_pass(0, kvall, every)
     halo_wait(1)
     light_attention(1)
-    arrived(kvall.at[s + 1 - 2 * core], ag_s.at[0], ag_r.at[0], sibling)
-    for k in range(1, nz):
-        block = kvall.at[2 * zpeer(nz - k) + 1 - core]
-        arrived(block, fw_s.at[k], fw_r.at[k], sibling)
+    gather_end(0, kvall, every)
 
     loads["who"].wait()
     loads["wol"].wait()
 
     def attention_terms(d):
         heavy_attention(d)
-        proj = (mmt(hox[mine(d), 0:wh], who[...]) * cols[SQ, mine(d), :]).astype(BF)
+        proj = (mm(hox[mine(d), 0:wh], who[...]) * cols[SQ, mine(d), :]).astype(BF)
         for h in range(2):
             r = pl.ds(h * half, half)
             value = mmt(lo[d, r, :], wol[...]) + mm(pqkt[d, r, 0:slots], proj)
@@ -775,6 +831,7 @@
 
     attention_terms(0)
     attention_terms(1)
+    gather_start(1, qall, every)
     ar_step(0, 0, 1, tot1)
 
     for name in ("cot", "wdl", "wdh"):
@@ -798,25 +855,22 @@
     for name in ("gl", "ul", "gh", "uh"):
         loads[name].wait()
 
-    gains[...] = jnp.zeros(gains.shape, F32)
-
     def hidden_rows(d, r):
         return tok[d, r, :].astype(F32) + tot1[d, r, :].astype(F32)
 
     def ffn_norm(d):
         def body(t):
-            r = pl.ds(t, 32)
+            r = pl.ds(t, big)
             hidden = hidden_rows(d, r)
             inv = lax.rsqrt(row_sum(hidden * hidden) * (1.0 / width) + epsilon)
             invf[d, r, :] = inv
             fl[d, r, :] = (hidden * inv * gain_f).astype(BF)
 
-        tiles(rows, 32, body)
+        tiles(rows, big, body)
 
     def ffn_heavy(d):
-        live = jnp.where(idxc[0:slots, d : d + 1] >= 0, 1.0, 0.0).astype(F32)
         rowsf = mm(pqk[d, 0:slots, :], fl[d])
-        score = jax.nn.sigmoid(row_sum(rowsf * router_f)) * live
+        score = jax.nn.sigmoid(row_sum(rowsf * router_f)) * alive(d, 0)
         cols[SF, mine(d), :] = score
         frow[mine(d), :] = rowsf.astype(BF)
         ghr[mine(d), :] = (grow[mine(d), :].astype(F32) * score).astype(BF)
@@ -841,11 +895,7 @@
         cols[PREF, mine(d), :] = pre
         return (mmt(dguh[mine(d), :], wguh[...]) + pre * router_f).astype(BF)
 
-    def add_gain(which, values):
-        count = values.shape[0]
-        gains[which] += jnp.sum(values.reshape(count // 8, 8, width), axis=0)
-
-    def ffn_light(d, back_rows, between):
+    def ffn_light(d, back_rows):
         for h in range(2):
             r = pl.ds(h * half, half)
             gu = mm(fl[d, r, :], wgul[...]).astype(BF)
@@ -860,71 +910,78 @@
             parts[d, r, :] = value.astype(BF)
             ar_start(1, d, h)
 
-            def gain_body(t, d=d, h=h):
-                rr = pl.ds(pl.multiple_of(h * half + t, 32), 32)
-                unit = hidden_rows(d, rr) * invf[d, rr, :]
-                add_gain(1, parts[d, rr, :].astype(F32) * unit)
-
-            tiles(half, 32, gain_body)
-            if h == 0:
-                between()
-
-    def nothing():
-        pass
-
-    ar_step(0, 0, 4, tot1)
-    ffn_norm(0)
-    back0 = ffn_heavy(0)
-    ar_step(0, 1, 3, tot1)
-    ffn_light(0, back0, nothing)
-    ar_step(0, 1, 4, tot1)
-    ffn_norm(1)
-    back1 = ffn_heavy(1)
-    ar_step(1, 0, 1, tot2)
-    ffn_light(1, back1, nothing)
-    ar_step(1, 0, 2, tot2)
-    tot_copy = pltpu.make_async_copy(tot1, tot_o, out_s.at[0])
-    tot_copy.start()
-
-    grads = ((g_h, ra_h, rb_h), (g_l, ra_l, rb_l), (g_a, ra_a, rb_a))
+    grads = ((g_h, ra_h, rb_h, rl_h), (g_l, ra_l, rb_l, rl_l), (g_a, ra_a, rb_a, rl_a))
     packed_at = (0, g_h.shape[1], g_h.shape[1] + g_l.shape[1])
+    at_end = (z == 0) | (z == nz - 1)
+    inner = (z > 0) & (z < nz - 1)
+    low_side = jnp.where(z < nz // 2, 1, 0)
 
     def chunk_rows(zz, cc):
         return pl.ds(pl.multiple_of(chunk * (2 * zz + cc), chunk), chunk)
 
     def rs_start(p):
-        grad, ra, rb = grads[p]
+        grad, ra, rb, rl = grads[p]
         for zz in range(nz):
             late.append(send(
                 grad.at[chunk_rows(zz, 1 - core), pl.ds(0, ra.shape[2])], ra.at[zz],
                 wa_s.at[p, zz], wa_r.at[p, zz], sibling,
             ))
 
+    def add_chunk(grad, zz, other):
+        cut = other.shape[1]
+
+        def add_body(t, carry):
+            r = pl.ds(pl.multiple_of(chunk * (2 * zz + core) + 16 * t, 16), 16)
+            value = grad[r, 0:cut].astype(F32) + other[pl.ds(pl.multiple_of(16 * t, 16), 16), :].astype(F32)
+            grad[r, 0:cut] = value.astype(BF)
+            return carry
+
+        lax.fori_loop(0, chunk // 16, add_body, 0)
+
+    def rs_direct(p, k, when):
+        grad, ra, rb, rl = grads[p]
+        late.append((when, send(
+            grad.at[chunk_rows(zpeer(k), core), pl.ds(0, ra.shape[2])], rb.at[k - 1],
+            wz_s.at[p, k - 1], wz_r.at[p, k - 1], same_core(k), when,
+        )))
+
     def rs_middle(p):
-        grad, ra, rb = grads[p]
-        cut = ra.shape[2]
-        for k in range(1, nz + 1):
+        grad, ra, rb, rl = grads[p]
+        for i in range(1, nz + 1):
+            k = low_side * (nz - i) + (1 - low_side) * i if i < nz else nz
             zz = zpeer(k)
             arrived(ra.at[zz], wa_s.at[p, zz], wa_r.at[p, zz], sibling)
-
-            def add_body(t, carry):
-                r = pl.ds(pl.multiple_of(chunk * (2 * zz + core) + 16 * t, 16), 16)
-                value = grad[r, 0:cut].astype(F32) + ra[zz, pl.ds(pl.multiple_of(16 * t, 16), 16), :].astype(F32)
-                grad[r, 0:cut] = value.astype(BF)
-                return carry
-
-            lax.fori_loop(0, chunk // 16, add_body, 0)
-            if k < nz:
-                late.append(send(
-                    grad.at[chunk_rows(zz, core), pl.ds(0, cut)], rb.at[k - 1],
-                    wz_s.at[p, k - 1], wz_r.at[p, k - 1], same_core(k),
-                ))
+            add_chunk(grad, zz, ra.at[zz])
+            if i == 1:
+                neighbour = (b, 2 * (z + 2 * low_side - 1) + core)
+                late.append((at_end, send(
+                    grad.at[chunk_rows(zz, core), pl.ds(0, ra.shape[2])], rl, rl_s.at[p], rl_r.at[p],
+                    neighbour, at_end,
+                )))
+                rs_direct(p, k, inner)
+            elif i == 2:
+                rs_direct(p, k, at_end)
+            elif i == 3:
+                rs_direct(p, k, z >= 0)
+
+    def rs_relay(p):
+        grad, ra, rb, rl = grads[p]
+
+        @pl.when(inner)
+        def _():
+            arrived(rl, rl_s.at[p], rl_r.at[p], same_core(1))
+            add_chunk(grad, zpeer(2), rl)
+
+        rs_direct(p, 2, inner)
 
     def rs_end(p):
-        grad, ra, rb = grads[p]
+        grad, ra, rb, rl = grads[p]
         cut = ra.shape[2]
-        for k in range(1, nz):
-            arrived(rb.at[k - 1], wz_s.at[p, k - 1], wz_r.at[p, k - 1], same_core(nz - k))
+        for k, when in ((1, z > 0), (2, z >= 0), (3, z < nz - 1)):
+
+            @pl.when(when)
+            def _(k=k):
+                arrived(rb.at[k - 1], wz_s.at[p, k - 1], wz_r.at[p, k - 1], same_core(nz - k))
 
         def add_body(t, carry):
             r = pl.ds(pl.multiple_of(16 * t, 16), 16)
@@ -936,6 +993,16 @@
 
         lax.fori_loop(0, chunk // 16, add_body, 0)
 
+    @pl.when(z == 0)
+    def _():
+        for grad, ra, rb, rl in grads:
+            rb[0] = jnp.zeros(rb.shape[1:], BF)
+
+    @pl.when(z == nz - 1)
+    def _():
+        for grad, ra, rb, rl in grads:
+            rb[2] = jnp.zeros(rb.shape[1:], BF)
+
     def heavy_ffn_grads():
         step = 512
         for src, gr, base, total in ((frow, dguh, 0, 2 * fh_n), (ghr, midh, 2 * fh_n, fh_n)):
@@ -960,35 +1027,24 @@
             right_side = gr[...].reshape(docs * rows, gr.shape[2])
             ref[f, base : base + gr.shape[2]] = tmm(all_rows(src, f), right_side).astype(BF)
 
-    heavy_ffn_grads()
-    rs_start(0)
-    ar_step(1, 1, 1, tot2)
-    ar_step(1, 0, 3, tot2)
-    light_grad(fl, dgu, g_l, 0)
-    light_grad(cot, mid, g_l, 2 * fl_n)
-    rs_start(1)
-    rs_middle(0)
-    ar_step(1, 1, 2, tot2)
-
     def mixed_terms(d):
         def body(j, carry):
             w = pl.ds(pl.multiple_of(j * share, share), share)
             heavy = (mmt(midh[mine(d), :], wdh[w, :]) * cols[SF, mine(d), :]).astype(BF)
-            for h in range(2):
-                r = pl.ds(h * half, half)
-                value = mmt(mid[d, r, :], wdl[w, :]) + mm(pqkt[d, r, 0:slots], heavy)
-                mixb[j, d, r, :] = value.astype(BF)
+            value = mmt(wdl[w, :], mid[d]) + tmm(heavy, pqk[d, 0:slots, :])
+            mixb[j, d] = value.astype(BF)
             return carry
 
         lax.fori_loop(0, 4, body, 0)
 
-    mixed_terms(0)
-    mixed_terms(1)
-    rs_middle(1)
+    def mixed_start(d):
+        column = lax.broadcasted_iota(jnp.int32, (share, width), 1) - b * share
+        own = jnp.where(column == lax.broadcasted_iota(jnp.int32, (share, width), 0), 1.0, 0.0).astype(BF)
+        mixa[d] = mmt(own, tok[d]) + mmt(own, tot1[d]) + mixb[b, d].astype(F32)
 
     def hidden_grad(d):
         def body(t):
-            r = pl.ds(t, 32)
+            r = pl.ds(t, big)
             unit = hidden_rows(d, r) * invf[d, r, :]
             w = tot2[d, r, :].astype(F32) * gain_f
             inner = row_sum(w * unit) * (1.0 / width)
@@ -996,50 +1052,35 @@
             ghf[d, r, :] = value
             ghb[d, r, :] = value.astype(BF)
 
-        tiles(rows, 32, body)
+        tiles(rows, big, body)
 
     def heavy_back(d):
         picked = mm(pqk[d, 0:slots, :], ghb[d])
         score = cols[SQ, mine(d), :]
         gah[mine(d), :] = (picked * score).astype(BF)
-        raw = mm(picked.astype(BF), who[...])
+        raw = mmt(picked.astype(BF), who[...])
         pre = row_sum(hox[mine(d), 0:wh].astype(F32) * raw) * score * (1.0 - score)
         cols[PREQ, mine(d), :] = pre
         dox[mine(d), 0:wh] = (raw * score).astype(BF)
         dox[mine(d), wh:256] = jnp.zeros((slots, 256 - wh), BF)
         do3 = three_heads(dox[mine(d), :])
-        q3 = three_heads(hqx[mine(d), :])
-        p = ph[d]
-        pf = p.astype(F32)
+        pf = ph[d].astype(F32)
         dp = mmt(do3, keys_of(d, 256))
-        ds = (pf * (dp - row_sum(dp * pf)) * HD ** (-0.5)).astype(BF)
+        delta = row_sum(dp * pf)
+        doall[s, mine(d), 0:wh] = dox[mine(d), 0:wh]
+        doall[s, mine(d), wh:256] = spread(-delta)
+        gather_start(2 + d, doall, routed(d))
+        ds = (pf * (dp - delta) * HD ** (-0.5)).astype(BF)
         dqh[mine(d), :] = one_of_three(mm(ds, keys_of(d, 0))).astype(BF)
-        dk = tmm(ds, q3).astype(BF).reshape(nz, 2, slots, 256)
-        dv = tmm(p, do3).astype(BF).reshape(nz, 2, slots, 256)
-        for c in range(2):
-            for zz in range(nz):
-                hb[d, c, zz, :, 0:256] = dk[zz, c]
-                hb[d, c, zz, :, 256:512] = dv[zz, c]
-        late.append(send(hb.at[d, 1 - core], h1.at[d], ha_s.at[d], ha_r.at[d], sibling))
-
-    def heavy_back_middle(d):
-        arrived(h1.at[d], ha_s.at[d], ha_r.at[d], sibling)
-        for k in range(1, nz + 1):
-            zz = zpeer(k)
-            value = hb[d, core, zz].astype(F32) + h1[d, zz].astype(F32)
-            hb[d, core, zz] = value.astype(BF)
-            if k < nz:
-                late.append(send(
-                    hb.at[d, core, zz], h2.at[d, k - 1], hz_s.at[d, k - 1], hz_r.at[d, k - 1], same_core(k)
-                ))
-
-    def heavy_back_end(d):
-        for k in range(1, nz):
-            arrived(h2.at[d, k - 1], hz_s.at[d, k - 1], hz_r.at[d, k - 1], same_core(nz - k))
-        value = hb[d, core, z].astype(F32)
-        for k in range(1, nz):
-            value = value + h2[d, k - 1].astype(F32)
-        dkvh[mine(d), :] = value.astype(BF)
+
+    def heavy_back_keys(d):
+        q = qall[:, mine(d), :].reshape(n_seq * slots, 256)
+        do = doall[:, mine(d), :].reshape(n_seq * slots, 256)
+        live = jnp.concatenate([alive(d, 1)] * (wh // HD), axis=0) > 0
+        p = jnp.exp(jnp.where(live, mmt(own_keys(d, 0), q) * HD ** (-0.5), masked_value))
+        ds = (p * mmt(own_keys(d, 256), do) * HD ** (-0.5)).astype(BF)
+        dkvh[mine(d), 0:256] = one_of_three(mm(ds, q)).astype(BF)
+        dkvh[mine(d), 256:512] = one_of_three(mm(p.astype(BF), do)).astype(BF)
 
     def light_back(d):
         dkvw[d] = jnp.zeros((rows + 2 * radius, 2 * wl), F32)
@@ -1090,13 +1131,13 @@
             arrived(rimr.at[d, 0], rim_s.at[d, 1], rim_r.at[d, 1], left)
 
     def attention_back_terms(d):
-        heavy_back_end(d)
-        ds_in = mmt(dkvh[mine(d), 256 : 256 + wh], whv[...])
+        heavy_back_keys(d)
+        ds_in = mm(dkvh[mine(d), 256 : 256 + wh], whv[...])
         score = cols[SK, mine(d), :]
         pre_k = row_sum(ds_in * kin[mine(d), :].astype(F32)) * score * (1.0 - score)
         cols[PREK, mine(d), :] = pre_k
-        key_rows = mmt(dkvh[mine(d), 0:wh], whk[...]) + ds_in * score + pre_k * router_k
-        query_rows = mmt(dqh[mine(d), 0:wh], whq[...]) + cols[PREQ, mine(d), :] * router_q
+        key_rows = mm(dkvh[mine(d), 0:wh], whk[...]) + ds_in * score + pre_k * router_k
+        query_rows = mm(dqh[mine(d), 0:wh], whq[...]) + cols[PREQ, mine(d), :] * router_q
         both = jnp.concatenate([query_rows, key_rows], axis=0).astype(BF)
         rim_wait(d)
         dkvw[d, radius : 2 * radius, :] += rimr[d, 0].astype(F32)
@@ -1108,48 +1149,70 @@
             parts[d, r, :] = value.astype(BF)
             ar_start(2, d, h)
 
-            def gain_body(t, d=d, h=h):
-                rr = pl.ds(pl.multiple_of(h * half + t, 32), 32)
-                unit = tok[d, rr, :].astype(F32) * inva[d, rr, :]
-                add_gain(0, parts[d, rr, :].astype(F32) * unit)
-
-            tiles(half, 32, gain_body)
-
     def token_grad(d):
         def body(t):
-            r = pl.ds(t, 32)
+            r = pl.ds(t, big)
             inv = inva[d, r, :]
             unit = tok[d, r, :].astype(F32) * inv
             w = tot2[d, r, :].astype(F32) * gain_a
             inner = row_sum(w * unit) * (1.0 / width)
             ghf[d, r, :] = ghf[d, r, :] + inv * (w - unit * inner)
 
-        tiles(rows, 32, body)
+        tiles(rows, big, body)
         copy = pltpu.make_async_copy(ghf.at[d], gt_o.at[d], out_s.at[1 + d])
         copy.start()
         return copy
 
+    gather_pass(1, qall, every)
+    ar_step(0, 0, 4, tot1)
+    ffn_norm(0)
+    back0 = ffn_heavy(0)
+    ar_step(0, 1, 3, tot1)
+    ffn_light(0, back0)
+    ar_step(0, 1, 4, tot1)
+    ffn_norm(1)
+    back1 = ffn_heavy(1)
+    ar_step(1, 0, 1, tot2)
+    heavy_ffn_grads()
+    rs_start(0)
+    ffn_light(1, back1)
+    ar_step(1, 0, 2, tot2)
+    rs_middle(0)
+    light_grad(fl, dgu, g_l, 0)
+    ar_step(1, 1, 1, tot2)
+    ar_step(1, 0, 3, tot2)
+    light_grad(cot, mid, g_l, 2 * fl_n)
+    rs_start(1)
+    ar_step(1, 1, 2, tot2)
+    mixed_terms(0)
     ar_step(1, 0, 4, tot2)
     hidden_grad(0)
     heavy_back(0)
     ar_step(1, 1, 3, tot2)
+    rs_middle(1)
     light_back(0)
-    heavy_back_middle(0)
+    mixed_terms(1)
     ar_step(1, 1, 4, tot2)
     for k in range(1, 4):
         to = (b + k) % 4
         late.append(send(mixb.at[to], mixr.at[k - 1], mx_s.at[k - 1], mx_r.at[k - 1], (to, s)))
     hidden_grad(1)
+    gather_end(1, qall, every)
+    gather_pass(2, doall, routed(0))
     heavy_back(1)
     ar_sent(1, 0)
+    gather_end(2, doall, routed(0))
     attention_back_terms(0)
+    rs_relay(0)
     light_back(1)
-    heavy_back_middle(1)
+    gather_pass(3, doall, routed(1))
     ar_step(2, 0, 1, tot2)
     ar_sent(1, 1)
+    gather_end(3, doall, routed(1))
     attention_back_terms(1)
     ar_step(2, 0, 2, tot2)
     ar_step(2, 1, 1, tot2)
+    rs_relay(1)
 
     light_grad(nl, dqkv, g_a, 0)
     light_grad(ghb, lo, g_a, 3 * wl)
@@ -1159,53 +1222,84 @@
     ):
         g_a[:, at : at + wh] = tmm(src[...], gr).astype(BF)
         at += 256
-    vector_lane = lax.broadcasted_iota(jnp.int32, (width, 128), 1)
     lane = lax.broadcasted_iota(jnp.int32, (docs * slots, 128), 1)
     vectors = jnp.zeros((width, 128), F32)
     for src, which, at_lane in ((hin, PREQ, 1), (kin, PREK, 2), (frow, PREF, 4)):
         vectors = vectors + tmm(src[...], jnp.where(lane == at_lane, cols[which], 0.0).astype(BF))
-    for which, at_lane in ((0, 0), (1, 3)):
-        vectors = jnp.where(vector_lane == at_lane, row_sum(gains[which].T), vectors)
     g_a[:, at : at + 128] = vectors.astype(BF)
     rs_start(2)
+    mixed_start(0)
+    mixed_start(1)
     ar_step(2, 0, 3, tot2)
     ar_step(2, 1, 2, tot2)
+    rs_middle(2)
     rs_end(0)
-    rs_middle(2)
     ar_step(2, 0, 4, tot2)
-    out_copies = [tot_copy, token_grad(0)]
+    out_copies = [token_grad(0)]
     ar_step(2, 1, 3, tot2)
     rs_end(1)
-
+    rs_relay(2)
+
+    for name in ("gk", "uk"):
+        loads[name].wait()
+    vlane = lax.broadcasted_iota(jnp.int32, (chunk, 128), 1)
+    eye = lax.broadcasted_iota(jnp.int32, (chunk, width), 1) - chunk * s
+    eye = eye == lax.broadcasted_iota(jnp.int32, (chunk, width), 0)
+
+    def own_column(row):
+        return row_sum(jnp.where(eye, row, 0.0))
+
+    gf_sum = row_sum(packed[:, 0 : 2 * fh_n] * wkeep[...].astype(F32))
+    gf_sum = gf_sum + row_sum(
+        packed[:, packed_at[1] : packed_at[1] + 2 * fl_n] * wgul[own_rows, :].astype(F32)
+    )
     for k in range(1, 4):
         frm = (b + 4 - k) % 4
         arrived(mixr.at[k - 1], mx_s.at[k - 1], mx_r.at[k - 1], (frm, s))
     for d in range(docs):
 
         def mix_body(t, d=d):
-            r = pl.ds(t, 64)
-            value = mixb[b, d, r, :].astype(F32)
+            r = pl.ds(t, 32)
+            value = mixa[d, r, :]
             for k in range(3):
                 value = value + mixr[k, d, r, :].astype(F32)
-            dm[d, r, 0:share] = value
-
-        tiles(rows, 64, mix_body)
-    mix_copy = pltpu.make_async_copy(dm, mix_o, out_s.at[3])
+            mixa[d, r, :] = value
+
+        tiles(share, 32, mix_body)
+    mix_copy = pltpu.make_async_copy(mixa, mix_o, out_s.at[3])
     mix_copy.start()
     out_copies.append(mix_copy)
     ar_step(2, 1, 4, tot2)
     out_copies.append(token_grad(1))
     rs_end(2)
+    a_at = packed_at[2]
     va = packed.shape[1] - 128
-    vbuf[...] = packed[:, va : va + 128]
+    ga_sum = row_sum(packed[:, a_at : a_at + 3 * wl] * wqkv[own_rows, :].astype(F32))
+    eye_b = eye.astype(F32).astype(BF)
+    for i, w in enumerate((whq, whk, whv)):
+        h_at = a_at + 4 * wl + 256 * i
+        ga_sum = ga_sum + row_sum(packed[:, h_at : h_at + wh] * mmt(eye_b, w[...]))
+    vectors = packed[:, va : va + 128]
+
+    def lane_of(i):
+        return row_sum(jnp.where(vlane == i, vectors, 0.0))
+
+    ga_sum = ga_sum + own_column(router_q) * lane_of(1) + own_column(router_k) * lane_of(2)
+    gf_sum = gf_sum + own_column(router_f) * lane_of(4)
+    vectors = jnp.where(vlane == 0, ga_sum / own_column(gain_a), vectors)
+    vectors = jnp.where(vlane == 3, gf_sum / own_column(gain_f), vectors)
+    vbuf[...] = vectors
+    pack_copy = pltpu.make_async_copy(packed, pack_o, out_s.at[4])
+    pack_copy.start()
+    out_copies.append(pack_copy)
     for k in range(1, 4):
         late.append(send(vbuf, vr.at[k - 1], v_s.at[k - 1], v_r.at[k - 1], ((b + k) % 4, s)))
     for k in range(1, 4):
         arrived(vr.at[k - 1], v_s.at[k - 1], v_r.at[k - 1], ((b + 4 - k) % 4, s))
-    packed[:, va : va + 128] = vbuf[...] + vr[0] + vr[1] + vr[2]
-    pack_copy = pltpu.make_async_copy(packed, pack_o, out_s.at[4])
-    pack_copy.start()
-    out_copies.append(pack_copy)
+    vect[...] = (vbuf[...] + vr[0] + vr[1] + vr[2]).T
+    vec_copy = pltpu.make_async_copy(vect, vec_o, out_s.at[0])
+    vec_copy.start()
+    out_copies.append(vec_copy)
 
     for entry in late:
         if isinstance(entry, tuple):
@@ -1231,33 +1325,35 @@
     span = rows + 2 * radius
     vmem = [
         ((docs, rows, width), BF), ((docs, rows, width), BF), ((width, 3 * wl), BF), ((width, wl), BF),
-        ((width, wh), BF), ((width, wh), BF), ((width, wh), BF), ((width, wh), BF),
+        ((wh, width), BF), ((wh, width), BF), ((wh, width), BF), ((wh, width), BF),
         ((width, 2 * fl_n), BF), ((width, fl_n), BF), ((width, 2 * fh_n), BF), ((width, fh_n), BF),
+        ((chunk, 2 * fh_n), BF),
         ((docs, rows, width), BF), ((docs, rows, 1), F32), ((routed, width), BF), ((routed, width), BF),
         ((routed, width), BF), ((docs, rows, wl), BF), ((docs, span, 2 * wl), BF),
         ((docs * rows // WINDOW, 2 * WINDOW, 2 * WINDOW), BF), ((docs, rows, wl), BF), ((routed, pad), BF),
         ((n_seq, routed, 2 * pad), BF), ((docs, wh // HD * slots, keys), BF), ((routed, pad), BF),
+        ((n_seq, routed, pad), BF), ((n_seq, routed, pad), BF),
         ((docs, 2 * slots, rows), BF), ((docs, rows, 2 * slots), BF), ((docs, rows, width), BF),
         ((docs, rows, width), BF), ((docs, rows, width), BF), ((docs, 2, rows // 4, width), BF),
         ((docs, 2, rows // 8, width), BF), ((6, routed, 1), F32),
         ((docs, rows, fl_n), F32), ((routed, fh_n), F32), ((routed, width), BF), ((docs, rows, width), BF),
         ((docs, rows, 1), F32), ((docs, rows, fl_n), BF), ((docs, rows, 2 * fl_n), BF), ((routed, width), BF),
         ((routed, width), BF), ((routed, fh_n), BF), ((routed, 2 * fh_n), BF),
-        ((4, docs, rows, width // 4), BF), ((3, docs, rows, width // 4), BF), ((docs, rows, width), F32),
-        ((docs, rows, width), BF), ((docs, rows, wl), BF), ((routed, pad), BF), ((routed, width), BF),
-        ((routed, pad), BF), ((docs, span, 2 * wl), F32), ((docs, 2, radius, 2 * wl), BF),
-        ((docs, 2, radius, 2 * wl), BF), ((docs, rows, 3 * wl), BF),
-        ((docs, 2, nz, slots, 2 * pad), BF), ((docs, nz, slots, 2 * pad), BF),
-        ((docs, nz - 1, slots, 2 * pad), BF), ((routed, 2 * pad), BF), ((2, 8, width), F32),
+        ((4, docs, width // 4, rows), BF), ((3, docs, width // 4, rows), BF), ((docs, width // 4, rows), F32),
+        ((docs, rows, width), F32), ((docs, rows, width), BF), ((docs, rows, wl), BF), ((routed, pad), BF),
+        ((routed, width), BF), ((routed, pad), BF), ((docs, span, 2 * wl), F32),
+        ((docs, 2, radius, 2 * wl), BF), ((docs, 2, radius, 2 * wl), BF), ((docs, rows, 3 * wl), BF),
+        ((routed, 2 * pad), BF),
         ((width, h_n), BF), ((width, l_n), BF),
         ((nz, chunk, h_n), BF), ((nz, chunk, l_n), BF), ((nz, chunk, ga_n), BF),
         ((nz - 1, chunk, h_n), BF), ((nz - 1, chunk, l_n), BF), ((nz - 1, chunk, ga_n), BF),
-        ((chunk, h_n + l_n + ga_n), F32), ((chunk, 128), F32), ((3, chunk, 128), F32),
+        ((chunk, h_n), BF), ((chunk, l_n), BF), ((chunk, ga_n), BF),
+        ((chunk, h_n + l_n + ga_n), F32), ((chunk, 128), F32), ((3, chunk, 128), F32), ((128, chunk), F32),
     ]
     sems = [
-        (16,), (3, docs, 2, 4), (3, docs, 2, 4), (nz,), (nz,), (nz,), (nz,), (docs, 2), (docs, 2),
-        (docs, 2), (docs, 2), (docs,), (docs,), (docs, nz - 1), (docs, nz - 1), (3,), (3,),
-        (3, nz), (3, nz), (3, nz - 1), (3, nz - 1), (3,), (3,), (5,),
+        (18,), (3, docs, 2, 4), (3, docs, 2, 4), (2 + docs, nz), (2 + docs, nz), (2 + docs, nz), (2 + docs, nz),
+        (docs, 2), (docs, 2), (docs, 2), (docs, 2), (3,), (3,),
+        (3, nz), (3, nz), (3, nz - 1), (3, nz - 1), (3,), (3,), (3,), (3,), (5,),
     ]
     total = 0
     for shape, kind in vmem:
@@ -1280,7 +1376,7 @@
     fits = (
         total <= 60 * 2**20
         and sizes["branch"] == 4
-        and n_seq % 2 == 0
+        and n_seq == 8
         and width % (16 * n_seq) == 0
         and wl == 2 * HD
         and wh == 3 * HD
@@ -1293,54 +1389,78 @@
     chunk = width // n_seq
     ga_n = 4 * wl + 4 * 256 + 128
     pack_n = 3 * fh_n + 3 * fl_n + ga_n
-    idx_rows = jnp.concatenate([query_index, key_index], axis=1)
-    vec = jnp.stack(
-        [gain_attn, router_query, router_key, gain_ffn, router_ffn, gain_ffn, gain_ffn, gain_ffn]
-    ).astype(F32)
     in_hbm = [
-        tokens, cotangent, wq_light, wk_light, wv_light, wo_light, wq_heavy, wk_heavy, wv_heavy, wo_heavy,
+        tokens, cotangent, wq_light, wk_light, wv_light, wo_light, wq_heavy.T, wk_heavy.T, wv_heavy.T, wo_heavy.T,
         gate_light, up_light, down_light, gate_heavy, up_heavy, down_heavy,
     ]
     whole = pl.BlockSpec(memory_space=pltpu.VMEM)
     outside = pl.BlockSpec(memory_space=pl.ANY)
-    grad_tokens, mix, attn_total, packed = pl.pallas_call(
+    grad_tokens, mix, packed, vectors = pl.pallas_call(
         functools.partial(layer_kernel, dims),
         out_shape=[
             jax.ShapeDtypeStruct((docs, rows, width), F32),
-            jax.ShapeDtypeStruct((docs, rows, fl_n), F32),
-            jax.ShapeDtypeStruct((docs, rows, width), BF),
+            jax.ShapeDtypeStruct((docs, share, rows), F32),
             jax.ShapeDtypeStruct((chunk, pack_n), F32),
+            jax.ShapeDtypeStruct((128, chunk), F32),
         ],
-        in_specs=[pl.BlockSpec(memory_space=pltpu.SMEM), whole, whole, whole] + [outside] * 16,
+        in_specs=[pl.BlockSpec(memory_space=pltpu.SMEM)] + [whole] * 7 + [outside] * 16,
         out_specs=[outside] * 4,
         scratch_shapes=[pltpu.VMEM(shape, kind) for shape, kind in vmem]
         + [pltpu.SemaphoreType.DMA(shape) for shape in sems],
         compiler_params=pltpu.CompilerParams(
             collective_id=0, has_side_effects=True, vmem_limit_bytes=64 * 2**20 - 2**16
         ),
-    )(lengths, vec, idx_rows.T, idx_rows, *in_hbm)
-    own = lax.axis_index("branch") * share
-    mixed = mix[:, :, :share] + (
-        lax.dynamic_slice_in_dim(tokens, own, share, 2).astype(F32)
-        + lax.dynamic_slice_in_dim(attn_total, own, share, 2).astype(F32)
-    )
-
-    def part(at, wide):
-        return packed[:, at : at + wide]
+    )(lengths, query_index, key_index, gain_attn, router_query, router_key, gain_ffn, router_ffn, *in_hbm)
 
     l_at = 3 * fh_n
     a_at = l_at + 3 * fl_n
     h_at = a_at + 4 * wl
-    v_at = h_at + 4 * 256
-    return (
-        mixed, grad_tokens,
-        packed[:, v_at], packed[:, v_at + 1], packed[:, v_at + 2],
-        part(a_at, wl), part(a_at + wl, wl), part(a_at + 2 * wl, wl), part(a_at + 3 * wl, wl),
-        part(h_at, wh), part(h_at + 256, wh), part(h_at + 512, wh), part(h_at + 768, wh),
-        packed[:, v_at + 3], packed[:, v_at + 4],
-        part(l_at, fl_n), part(l_at + fl_n, fl_n), part(l_at + 2 * fl_n, fl_n),
-        part(0, fh_n), part(fh_n, fh_n), part(2 * fh_n, fh_n),
-    )
+    parts = [(a_at + i * wl, wl) for i in range(4)] + [(h_at + i * 256, wh) for i in range(4)]
+    parts += [(l_at + i * fl_n, fl_n) for i in range(3)] + [(i * fh_n, fh_n) for i in range(3)]
+    outs = pl.pallas_call(
+        functools.partial(hand_out, parts),
+        out_shape=[jax.ShapeDtypeStruct(grad_tokens.shape, F32), jax.ShapeDtypeStruct(mix.shape, F32)]
+        + [jax.ShapeDtypeStruct((chunk, wide), F32) for at, wide in parts],
+        in_specs=[pl.BlockSpec(memory_space=pltpu.HBM)] * 3,
+        out_specs=[outside] * 2 + [outside if wide % 128 == 0 else whole for at, wide in parts],
+        scratch_shapes=[
+            pltpu.SemaphoreType.DMA((3 + docs,)), pltpu.SemaphoreType.DMA((1 + docs + len(parts),)),
+            pltpu.VMEM(grad_tokens.shape, F32), pltpu.VMEM(mix.shape, F32), pltpu.VMEM(packed.shape, F32),
+        ],
+        compiler_params=pltpu.CompilerParams(vmem_limit_bytes=60 * 2**20),
+    )(grad_tokens, mix, packed)
+    grad_tokens, mix = outs[:2]
+    mixed = jnp.swapaxes(mix, 1, 2)
+    vec = [vectors[i] for i in range(5)]
+    return (mixed, grad_tokens, *vec[:3], *outs[2:10], *vec[3:], *outs[10:])
+
+
+def hand_out(parts, tokens_in, mix_in, packed_in, tokens_out, mix_out, *rest):
+    in_sems, out_sems, tokens, mix, packed = rest[-5:]
+    docs = tokens.shape[0]
+    arriving = [pltpu.make_async_copy(packed_in, packed, in_sems.at[0])]
+    arriving += [pltpu.make_async_copy(tokens_in.at[d], tokens.at[d], in_sems.at[1 + d]) for d in range(docs)]
+    arriving += [pltpu.make_async_copy(mix_in, mix, in_sems.at[1 + docs])]
+    for copy in arriving:
+        copy.start()
+    leaving = [pltpu.make_async_copy(mix, mix_out, out_sems.at[0])]
+    leaving += [pltpu.make_async_copy(tokens.at[d], tokens_out.at[d], out_sems.at[1 + d]) for d in range(docs)]
+    arriving[0].wait()
+    for i, (at, wide) in enumerate(parts):
+        if wide % 128 == 0:
+            copy = pltpu.make_async_copy(packed.at[:, at : at + wide], rest[i], out_sems.at[1 + docs + i])
+            copy.start()
+            leaving.append(copy)
+    for d in range(docs):
+        arriving[1 + d].wait()
+        leaving[1 + d].start()
+    arriving[1 + docs].wait()
+    leaving[0].start()
+    for i, (at, wide) in enumerate(parts):
+        if wide % 128 != 0:
+            rest[i][...] = packed[:, at : at + wide]
+    for copy in leaving:
+        copy.wait()
 
 
 def solution(mesh):

time: 235 us -> 180 us (0.77)
  the two profiles are of different devices: /device:TPU:26 before, /device:TPU:0 now
where the time goes in v3:
time: 180 us; the launch traced here: 179 us
  Pallas kernels  177 us (98%)
    pallas_call x1, Pallas kernels, shards(): pl.pallas_call(functools.partial(layer_kernel, dims), out_shape=[jax.Shap...  172 us
    pallas_call x1, Pallas kernels, shards(): pl.pallas_call(functools.partial(hand_out, parts), out_shape=[jax.ShapeDt...  5.03 us

profile of v3, /device:TPU:0, one launch (start us, length us, event | category | flops | bytes accessed | tf_op | source)
XLA Modules:
  0.0 179.2 jit_solution(84217464400642587)
XLA Ops:
  0.7 172.1 %shard_map.391 = (f32[2,512,768]{2,1,0:T(8,128)}, f32[2,192,512]{2,1,0:T(8,128)}, f32[96,5504]{1,0:T(8,128)}, f32[128,96]{1,0:T(8,128)}) custom-call(s32[2]{0:T(128)} %refs_0_.1, s32[2,64]{1,0:T(2,128)} %refs_1_.1, s32[2,64]{1,0:T(2,128)} %refs_2_.1, bf16[768]{0:T(1024)(128)(2,1)} %refs_3_.1, bf16[768]{0:T(1024)(128)(2,1)} %refs_4_.1, ...), custom_call_target="tpu_custom_call" | custom-call | tf_op jit(solution)/shard_map/pallas_call | solution.py:1398
  172.8 5.0 %shard_map.392 = (f32[2,512,768]{2,1,0:T(8,128)}, f32[2,192,512]{2,1,0:T(8,128)}, f32[96,128]{1,0:T(8,128)}, f32[96,128]{1,0:T(8,128)}, f32[96,128]{1,0:T(8,128)...) custom-call(f32[2,512,768]{2,1,0:T(8,128)} %get-tuple-element.41.tok, ...), custom_call_target="tpu_custom_call" | custom-call | tf_op jit(solution)/shard_map/pallas_call | solution.py:1420
  177.8 1.4 slice_bitcast_fusion

commit v4 on v3

--- a/solution.py
+++ b/solution.py
@@ -394,6 +394,21 @@
     )
 
 
+ORDER = (
+    "load", "rowskv", "pre0", "norm", "qkv", "pre1", "gp0_2", "la0", "predmh", "gp0_1", "gp0_3", "wgp",
+    "hattn", "la1", "hproj", "nf00", "nf01", "fh0", "fl00", "nf10", "nf11", "fh1", "hgrA1", "hgrA0", "fl01",
+    "hgrB0", "rs0a", "fl11", "hgrB1", "rs0b", "ar101_1", "fl10", "rs1a", "lgA", "ar100_1", "lgB", "ar101_2",
+    "rs0r", "ar110_1", "ar100_2", "ar111_1", "rs1b", "hgrB2", "mixt1", "rs3a", "ar110_2", "ar100_3",
+    "ar111_2", "rs3b", "mixt0", "rs1c", "ar101_3", "gp1_1", "ar110_3", "gp1_2", "ar111_3", "ar101_4", "mx1",
+    "ar100_4", "hg00", "hg01", "rs3r", "hb0", "mx0", "rs1d", "rs1r", "lb0", "rs0c", "gp1_3", "ar110_4",
+    "mixs1", "ar111_4", "hg10", "hg11", "hgrA2", "gp2_3", "rs3c", "hb1", "gp2_1", "gp2_2", "mixs0", "awgB",
+    "lb1", "hk0", "rs2a", "rs2b", "abt00", "abt01", "gp3_1", "blank", "gp3_2", "gp3_3", "rs2r", "rs2c",
+    "ar200_1", "hk1", "rs0d", "awgA", "rs2d", "rs4a", "ar201_1", "ar200_2", "rs4b", "abt10", "ar201_2",
+    "abt11", "ar200_3", "rs4c", "aqgA", "aqgB", "rs5a", "ar210_1", "rs5b", "rs4r", "rs5d", "rs5c",
+    "ar210_2", "ar211_1", "ar201_3", "rs3d", "mixf0", "ar210_3", "rs2e", "ar211_2", "ar201_4", "rs5r",
+    "rs4d", "ar210_4", "tok10", "rs4e", "rs1e", "ar211_3", "rs3e", "rs0e", "gains", "rs5e", "vec", "tok01",
+    "ar211_4", "mixf1", "tok11", "ar200_4", "tok00", "vece",
+)
 BF = jnp.bfloat16
 F32 = jnp.float32
 MESH = pl.DeviceIdType.MESH
@@ -442,15 +457,15 @@
     (tok_h, cot_h, wql_h, wkl_h, wvl_h, wol_h, wqh_h, wkh_h, wvh_h, woh_h,
      gl_h, ul_h, dl_h, gh_h, uh_h, dh_h) = take(16)
     gt_o, mix_o, pack_o, vec_o = take(4)
-    (tok, cot, wqkv, wol, whq, whk, whv, who, wgul, wdl, wguh, wdh, wkeep) = take(13)
-    (nl, inva, hin, kin, sin, qbuf, kvw, pbuf, lo, hqx, kvall, ph, hox, qall, doall) = take(15)
+    (tok, cot, wqkv, wola, whq, whk, whv, woha, wgul, wdl, wguh, wdh, wkeep) = take(13)
+    (nl, inva, hin, kin, sin, qbuf, kvw, pbuf, loall, hqx, kvall, ph, hoall, qall, doall, hproj, backr, bothr) = take(18)
     (pqk, pqkt, parts, tot1, tot2, r1, r2, cols) = take(8)
     (dm, dmh, grow, fl, invf, mid, dgu, frow, ghr, midh, dguh) = take(11)
     (mixb, mixr, mixa, ghf, ghb, dol, dox, gah, dqh, dkvw, rims, rimr, dqkv, dkvh) = take(14)
-    (g_h, g_l, ra_h, ra_l, ra_a, rb_h, rb_l, rb_a, rl_h, rl_l, rl_a, packed, vbuf, vr, vect) = take(15)
+    (g_h, g_l, ra, rb, rl, packed, vbuf, vr, vect) = take(2) + [take(6), take(6), take(6)] + take(4)
     g_a = wguh
-    (load_s, ar_s, ar_r, ag_s, ag_r, fw_s, fw_r, halo_s, halo_r, rim_s, rim_r,
-     mx_s, mx_r, wa_s, wa_r, wz_s, wz_r, rl_s, rl_r, v_s, v_r, out_s) = take(22)
+    (load_s, wg_s, wg_r, wf_s, wf_r, lo_s, lo_r, ho_s, ho_r, ar_s, ar_r, ag_s, ag_r, fw_s, fw_r, halo_s, halo_r, rim_s, rim_r,
+     mx_s, mx_r, wa_s, wa_r, wz_s, wz_r, rl_s, rl_r, v_s, v_r, out_s) = take(30)
 
     b = lax.axis_index("branch")
     s = lax.axis_index("seq")
@@ -500,8 +515,8 @@
     load("wq", wql_h, wqkv.at[:, 0:wl], 4)
     load("wk", wkl_h, wqkv.at[:, wl : 2 * wl], 5)
     load("wv", wvl_h, wqkv.at[:, 2 * wl : 3 * wl], 6)
-    load("wol", wol_h, wol, 7)
-    load("who", woh_h, who, 8)
+    load("wol", wol_h, wola.at[b], 7)
+    load("who", woh_h, woha.at[b], 8)
     load("cot", cot_h, cot, 9)
     load("wdl", dl_h, wdl, 10)
     load("wdh", dh_h, wdh, 11)
@@ -577,55 +592,96 @@
 
         lax.fori_loop(0, eighth // 32, body, 0)
 
-    def ar_step(a, d, step, total):
-        for h in range(2):
-            first, second, keep1, send1, keep2, send2 = geometry(h)
-            at = (a, d, h)
-            if step == 1:
-                arrived(r1.at[d, h], ar_s.at[a, d, h, 0], ar_r.at[a, d, h, 0], first)
-                add_rows(d, send2, r1.at[d, h], pl.multiple_of(send2 - keep1, eighth), parts)
-                flights[at + (1,)] = send(
-                    parts.at[d, pl.ds(send2, eighth)], r2.at[d, h], ar_s.at[a, d, h, 1], ar_r.at[a, d, h, 1], second
-                )
-                add_rows(d, keep2, r1.at[d, h], pl.multiple_of(keep2 - keep1, eighth), parts)
-            elif step == 2:
-                arrived(r2.at[d, h], ar_s.at[a, d, h, 1], ar_r.at[a, d, h, 1], second)
-                add_rows(d, keep2, r2.at[d, h], 0, total)
-                own = total.at[d, pl.ds(keep2, eighth)]
-                flights[at + (2,)] = send(own, own, ar_s.at[a, d, h, 2], ar_r.at[a, d, h, 2], second)
-            elif step == 3:
-                arrived(total.at[d, pl.ds(send2, eighth)], ar_s.at[a, d, h, 2], ar_r.at[a, d, h, 2], second)
-                own = total.at[d, pl.ds(keep1, quarter)]
-                flights[at + (3,)] = send(own, own, ar_s.at[a, d, h, 3], ar_r.at[a, d, h, 3], first)
-            else:
-                arrived(total.at[d, pl.ds(send1, quarter)], ar_s.at[a, d, h, 3], ar_r.at[a, d, h, 3], first)
-                flights[at + (0,)].wait_send()
-                flights[at + (1,)].wait_send()
+    def ar_step(a, d, h, step, total):
+        first, second, keep1, send1, keep2, send2 = geometry(h)
+        at = (a, d, h)
+        if step == 1:
+            arrived(r1.at[d, h], ar_s.at[a, d, h, 0], ar_r.at[a, d, h, 0], first)
+            add_rows(d, send2, r1.at[d, h], pl.multiple_of(send2 - keep1, eighth), parts)
+            flights[at + (1,)] = send(
+                parts.at[d, pl.ds(send2, eighth)], r2.at[d, h], ar_s.at[a, d, h, 1], ar_r.at[a, d, h, 1], second
+            )
+            add_rows(d, keep2, r1.at[d, h], pl.multiple_of(keep2 - keep1, eighth), parts)
+        elif step == 2:
+            arrived(r2.at[d, h], ar_s.at[a, d, h, 1], ar_r.at[a, d, h, 1], second)
+            add_rows(d, keep2, r2.at[d, h], 0, total)
+            own = total.at[d, pl.ds(keep2, eighth)]
+            flights[at + (2,)] = send(own, own, ar_s.at[a, d, h, 2], ar_r.at[a, d, h, 2], second)
+        elif step == 3:
+            arrived(total.at[d, pl.ds(send2, eighth)], ar_s.at[a, d, h, 2], ar_r.at[a, d, h, 2], second)
+            own = total.at[d, pl.ds(keep1, quarter)]
+            flights[at + (3,)] = send(own, own, ar_s.at[a, d, h, 3], ar_r.at[a, d, h, 3], first)
+        else:
+            arrived(total.at[d, pl.ds(send1, quarter)], ar_s.at[a, d, h, 3], ar_r.at[a, d, h, 3], first)
+            flights[at + (0,)].wait_send()
+            flights[at + (1,)].wait_send()
 
     def ar_sent(a, d):
         for h in range(2):
             flights[a, d, h, 2].wait_send()
             flights[a, d, h, 3].wait_send()
 
-    loads["tok"].wait()
-    for d in range(docs):
-
-        def norm_body(t, d=d):
-            r = pl.ds(t, big)
-            x = tok[d, r, :].astype(F32)
-            inv = lax.rsqrt(row_sum(x * x) * (1.0 / width) + epsilon)
-            inva[d, r, :] = inv
-            nl[d, r, :] = (x * inv * gain_a).astype(BF)
-
-        tiles(rows, big, norm_body)
-
-    for d in range(docs):
-        lane_pos = lax.broadcasted_iota(jnp.int32, (slots, rows), 1) + offset
-        sub_pos = lax.broadcasted_iota(jnp.int32, (rows, slots), 0) + offset
-        for i in range(2):
-            here = slice(i * slots, (i + 1) * slots)
-            pqk[d, here, :] = jnp.where(idx_col[d][i] == lane_pos, 1.0, 0.0).astype(BF)
-            pqkt[d, :, here] = jnp.where(idx_row[d][i] == sub_pos, 1.0, 0.0).astype(BF)
+    steps = {}
+
+    def step(name):
+        def keep(body):
+            steps[name] = body
+            return body
+
+        return keep
+
+    def halves(core_of):
+        return (
+            (wola, pl.ds(pl.multiple_of(width // 2 * core_of, 16), width // 2)),
+            (woha, pl.ds(pl.multiple_of(wh // 2 * core_of, 16), wh // 2)),
+        )
+
+    @step("load")
+    def _():
+        loads["wol"].wait()
+        loads["who"].wait()
+        for k in range(1, 4):
+            for i, (ref, part) in enumerate(halves(core)):
+                block = ref.at[b, part]
+                late.append(send(block, block, wg_s.at[k - 1, i], wg_r.at[k - 1, i], ((b + k) % 4, s)))
+        loads["tok"].wait()
+
+    @step("wgp")
+    def _():
+        for k in range(1, 4):
+            frm = (b + 4 - k) % 4
+            for i, (ref, part) in enumerate(halves(core)):
+                block = ref.at[frm, part]
+                arrived(block, wg_s.at[k - 1, i], wg_r.at[k - 1, i], (frm, s))
+                late.append(send(block, block, wf_s.at[k - 1, i], wf_r.at[k - 1, i], sibling))
+
+    def projections_wait():
+        for k in range(1, 4):
+            frm = (b + 4 - k) % 4
+            for i, (ref, part) in enumerate(halves(1 - core)):
+                arrived(ref.at[frm, part], wf_s.at[k - 1, i], wf_r.at[k - 1, i], sibling)
+
+    @step("norm")
+    def _():
+        for d in range(docs):
+
+            def norm_body(t, d=d):
+                r = pl.ds(t, big)
+                x = tok[d, r, :].astype(F32)
+                inv = lax.rsqrt(row_sum(x * x) * (1.0 / width) + epsilon)
+                inva[d, r, :] = inv
+                nl[d, r, :] = (x * inv * gain_a).astype(BF)
+
+            tiles(rows, big, norm_body)
+
+    def selectors():
+        for d in range(docs):
+            lane_pos = lax.broadcasted_iota(jnp.int32, (slots, rows), 1) + offset
+            sub_pos = lax.broadcasted_iota(jnp.int32, (rows, slots), 0) + offset
+            for i in range(2):
+                here = slice(i * slots, (i + 1) * slots)
+                pqk[d, here, :] = jnp.where(idx_col[d][i] == lane_pos, 1.0, 0.0).astype(BF)
+                pqkt[d, :, here] = jnp.where(idx_row[d][i] == sub_pos, 1.0, 0.0).astype(BF)
 
     def alive(d, i):
         return jnp.where(idx_col[d][i] >= 0, 1.0, 0.0).astype(F32)
@@ -635,36 +691,46 @@
     def mine(d):
         return slice(d * slots, (d + 1) * slots)
 
-    for d in range(docs):
-        picked = mm(pqk[d], nl[d])
-        score_q = jax.nn.sigmoid(row_sum(picked[:slots] * router_q)) * alive(d, 0)
-        score_k = jax.nn.sigmoid(row_sum(picked[slots:] * router_k)) * alive(d, 1)
-        cols[SQ, mine(d), :] = score_q
-        cols[SK, mine(d), :] = score_k
-        hin[mine(d), :] = picked[:slots].astype(BF)
-        kin[mine(d), :] = picked[slots:].astype(BF)
-        sin[mine(d), :] = (picked[slots:] * score_k).astype(BF)
-        pad_lane = lax.broadcasted_iota(jnp.int32, (slots, 256 - wh), 1)
-        kvall[s, mine(d), wh:256] = jnp.where(
-            pad_lane == 0, (1.0 - alive(d, 1)) * masked_value, 0.0
-        ).astype(BF)
-        kvall[s, mine(d), 256 + wh : 512] = jnp.zeros((slots, 256 - wh), BF)
-    loads["whk"].wait()
-    kvall[s, :, 0:wh] = mmt(kin[...], whk[...]).astype(BF)
-    loads["whv"].wait()
-    kvall[s, :, 256 : 256 + wh] = mmt(sin[...], whv[...]).astype(BF)
+    def routed_rows():
+        for d in range(docs):
+            x = mm(pqk[d], tok[d])
+            picked = x * lax.rsqrt(row_sum(x * x) * (1.0 / width) + epsilon) * gain_a
+            score_q = jax.nn.sigmoid(row_sum(picked[:slots] * router_q)) * alive(d, 0)
+            score_k = jax.nn.sigmoid(row_sum(picked[slots:] * router_k)) * alive(d, 1)
+            cols[SQ, mine(d), :] = score_q
+            cols[SK, mine(d), :] = score_k
+            hin[mine(d), :] = picked[:slots].astype(BF)
+            kin[mine(d), :] = picked[slots:].astype(BF)
+            sin[mine(d), :] = (picked[slots:] * score_k).astype(BF)
+            pad_lane = lax.broadcasted_iota(jnp.int32, (slots, 256 - wh), 1)
+            kvall[s, mine(d), wh:256] = jnp.where(
+                pad_lane == 0, (1.0 - alive(d, 1)) * masked_value, 0.0
+            ).astype(BF)
+            kvall[s, mine(d), 256 + wh : 512] = jnp.zeros((slots, 256 - wh), BF)
+        loads["whk"].wait()
+        kvall[s, :, 0:wh] = mmt(kin[...], whk[...]).astype(BF)
+        loads["whv"].wait()
+        kvall[s, :, 256 : 256 + wh] = mmt(sin[...], whv[...]).astype(BF)
+
+    at_end = (z == 0) | (z == nz - 1)
+    inner = (z > 0) & (z < nz - 1)
+    low_side = jnp.where(z < nz // 2, 1, 0)
 
     def gather_start(g, ref, part):
         block = ref.at[s, part]
         late.append(send(block, block, ag_s.at[g, 0], ag_r.at[g, 0], sibling))
-        for k in range(1, nz):
-            late.append(send(block, block, ag_s.at[g, k], ag_r.at[g, k], same_core(k)))
-
-    def gather_pass(g, ref, part):
-        for k in range(1, nz):
-            block = ref.at[2 * zpeer(nz - k) + core, part]
-            arrived(block, ag_s.at[g, k], ag_r.at[g, k], same_core(nz - k))
-            late.append(send(block, block, fw_s.at[g, k], fw_r.at[g, k], sibling))
+        for k in (2, 1, 3):
+            near = (z != 0) if k == 3 else (z != 3) if k == 1 else (z >= 0)
+            late.append((near, send(block, block, ag_s.at[g, k], ag_r.at[g, k], same_core(k), near)))
+
+    def gather_pass(g, ref, part, k):
+        block = ref.at[2 * zpeer(nz - k) + core, part]
+        arrived(block, ag_s.at[g, k], ag_r.at[g, k], same_core(nz - k))
+        late.append(send(block, block, fw_s.at[g, k], fw_r.at[g, k], sibling))
+        if k == 2:
+            onward = (b, 2 * (z + 1 - 2 * low_side) + core)
+            slot = 3 - 2 * low_side
+            late.append((inner, send(block, block, fw_s.at[g, 0], ag_r.at[g, slot], onward, inner)))
 
     def gather_end(g, ref, part):
         arrived(ref.at[s + 1 - 2 * core, part], ag_s.at[g, 0], ag_r.at[g, 0], sibling)
@@ -676,43 +742,51 @@
         return pl.ds(d * slots, slots)
 
     every = pl.ds(0, docs * slots)
-    gather_start(0, kvall, every)
-
-    loads["whq"].wait()
-    hqx[:, 0:wh] = mmt(hin[...], whq[...]).astype(BF)
-    pad_lane = lax.broadcasted_iota(jnp.int32, (docs * slots, 256 - wh), 1)
-    hqx[:, wh:256] = jnp.where(pad_lane == 0, 8.0, 0.0).astype(BF)
-
-    for name in ("wq", "wk", "wv"):
-        loads[name].wait()
+
+    @step("rowskv")
+    def _():
+        selectors()
+        routed_rows()
+        gather_start(0, kvall, every)
+
+
     last = n_seq - 1
     left = (b, (s + last) % n_seq)
     right = (b, (s + 1) % n_seq)
-    for d in range(docs):
-
-        def qkv_body(t, d=d):
-            r = mm(nl[d, pl.ds(t, half), :], wqkv[...]).astype(BF)
-            qbuf[d, pl.ds(t, half), :] = r[:, 0:wl]
-            kvw[d, pl.ds(pl.multiple_of(t + radius, 32), half), :] = r[:, wl : 3 * wl]
-
-        tiles(rows, half, qkv_body)
-
-        @pl.when(s == 0)
-        def _(d=d):
-            kvw[d, 0:radius, :] = jnp.zeros((radius, 2 * wl), BF)
-
-        @pl.when(s == last)
-        def _(d=d):
-            kvw[d, rows + radius : rows + 2 * radius, :] = jnp.zeros((radius, 2 * wl), BF)
-
-        late.append((s > 0, send(
-            kvw.at[d, pl.ds(radius, radius)], kvw.at[d, pl.ds(rows + radius, radius)],
-            halo_s.at[d, 0], halo_r.at[d, 0], left, s > 0,
-        )))
-        late.append((s < last, send(
-            kvw.at[d, pl.ds(rows, radius)], kvw.at[d, pl.ds(0, radius)],
-            halo_s.at[d, 1], halo_r.at[d, 1], right, s < last,
-        )))
+
+    @step("qkv")
+    def _():
+        for name in ("wq", "wk", "wv"):
+            loads[name].wait()
+        for d in range(docs):
+
+            def qkv_body(t, d=d):
+                r = mm(nl[d, pl.ds(t, half), :], wqkv[...]).astype(BF)
+                qbuf[d, pl.ds(t, half), :] = r[:, 0:wl]
+                kvw[d, pl.ds(pl.multiple_of(t + radius, 32), half), :] = r[:, wl : 3 * wl]
+
+            tiles(rows, half, qkv_body)
+
+            @pl.when(s == 0)
+            def _(d=d):
+                kvw[d, 0:radius, :] = jnp.zeros((radius, 2 * wl), BF)
+
+            @pl.when(s == last)
+            def _(d=d):
+                kvw[d, rows + radius : rows + 2 * radius, :] = jnp.zeros((radius, 2 * wl), BF)
+
+            late.append((s > 0, send(
+                kvw.at[d, pl.ds(radius, radius)], kvw.at[d, pl.ds(rows + radius, radius)],
+                halo_s.at[d, 0], halo_r.at[d, 0], left, s > 0,
+            )))
+            late.append((s < last, send(
+                kvw.at[d, pl.ds(rows, radius)], kvw.at[d, pl.ds(0, radius)],
+                halo_s.at[d, 1], halo_r.at[d, 1], right, s < last,
+            )))
+        loads["whq"].wait()
+        hqx[:, 0:wh] = mmt(hin[...], whq[...]).astype(BF)
+        pad_lane = lax.broadcasted_iota(jnp.int32, (docs * slots, 256 - wh), 1)
+        hqx[:, wh:256] = jnp.where(pad_lane == 0, 8.0, 0.0).astype(BF)
 
     def halo_wait(d):
         @pl.when(s < last)
@@ -751,7 +825,7 @@
             p = (e * (1.0 / row_sum(e))).astype(BF)
             pbuf[d * n_blk + i] = p
             out = one_of_two(mm(p, v))
-            lo[d, pl.ds(at, blk), :] = (out * valid_rows(d, at, blk)).astype(BF)
+            loall[b, d, pl.ds(at, blk), :] = (out * valid_rows(d, at, blk)).astype(BF)
             return carry
 
         lax.fori_loop(0, n_blk, body, 0)
@@ -808,34 +882,57 @@
         ph[d] = p
         qall[s, mine(d), 0:wh] = hqx[mine(d), 0:wh]
         qall[s, mine(d), wh:256] = spread((top + jnp.log(sums)) * -(HD**0.5))
-        hox[mine(d), :] = one_of_three(mm(p, keys_of(d, 256))).astype(BF)
-
-    halo_wait(0)
-    light_attention(0)
-    gather_pass(0, kvall, every)
-    halo_wait(1)
-    light_attention(1)
-    gather_end(0, kvall, every)
-
-    loads["who"].wait()
-    loads["wol"].wait()
-
-    def attention_terms(d):
-        heavy_attention(d)
-        proj = (mm(hox[mine(d), 0:wh], who[...]) * cols[SQ, mine(d), :]).astype(BF)
-        for h in range(2):
-            r = pl.ds(h * half, half)
-            value = mmt(lo[d, r, :], wol[...]) + mm(pqkt[d, r, 0:slots], proj)
-            parts[d, r, :] = value.astype(BF)
-            ar_start(0, d, h)
-
-    attention_terms(0)
-    attention_terms(1)
-    gather_start(1, qall, every)
-    ar_step(0, 0, 1, tot1)
-
-    for name in ("cot", "wdl", "wdh"):
-        loads[name].wait()
+        hoall[b, mine(d), :] = one_of_three(mm(p, keys_of(d, 256))).astype(BF)
+
+    def to_branches(block, ssem, rsem, k):
+        return send(block, block, ssem, rsem, ((b + k) % 4, s))
+
+    def from_branch(ref, ssem, rsem, k):
+        frm = (b + 4 - k) % 4
+        arrived(ref.at[frm], ssem, rsem, (frm, s))
+
+    for d in range(docs):
+
+        @step("la%d" % d)
+        def _(d=d):
+            halo_wait(d)
+            light_attention(d)
+            for k in range(1, 4):
+                late.append(to_branches(loall.at[b, d], lo_s.at[d, k - 1], lo_r.at[d, k - 1], k))
+
+    @step("hattn")
+    def _():
+        gather_end(0, kvall, every)
+        for d in range(docs):
+            heavy_attention(d)
+        for k in range(1, 4):
+            late.append(to_branches(hoall.at[b], ho_s.at[k - 1], ho_r.at[k - 1], k))
+        gather_start(1, qall, every)
+
+    gathers = ((0, kvall, every), (1, qall, every)) + tuple((2 + d, doall, routed(d)) for d in range(docs))
+    for g, ref, part in gathers:
+        for k in range(1, nz):
+
+            @step("gp%d_%d" % (g, k))
+            def _(g=g, ref=ref, part=part, k=k):
+                gather_pass(g, ref, part, k)
+
+    @step("hproj")
+    def _():
+        projections_wait()
+        for k in range(1, 4):
+            from_branch(hoall, ho_s.at[k - 1], ho_r.at[k - 1], k)
+        total = mm(hoall[0, :, 0:wh], woha[0])
+        for j in range(1, 4):
+            total = total + mm(hoall[j, :, 0:wh], woha[j])
+        hproj[...] = (total * cols[SQ]).astype(BF)
+
+    def attention_total(d, h):
+        r = pl.ds(h * half, half)
+        heads = jnp.concatenate([loall[j, d, r, :] for j in range(4)], axis=1)
+        out_weights = jnp.concatenate([wola[j] for j in range(4)], axis=1)
+        value = mmt(heads, out_weights) + mm(pqkt[d, r, 0:slots], hproj[mine(d), :])
+        tot1[d, r, :] = value.astype(BF)
 
     def light_pre(d):
         def body(t):
@@ -845,28 +942,44 @@
         tiles(rows, half, body)
         grow[mine(d), :] = mm(pqk[d, 0:slots, :], cot[d]).astype(BF)
 
-    light_pre(0)
-    ar_step(0, 0, 2, tot1)
-    ar_step(0, 1, 1, tot1)
-    light_pre(1)
-    dmh[...] = mm(grow[...], wdh[...])
-    ar_step(0, 0, 3, tot1)
-    ar_step(0, 1, 2, tot1)
-    for name in ("gl", "ul", "gh", "uh"):
-        loads[name].wait()
+    for d in range(docs):
+
+        @step("pre%d" % d)
+        def _(d=d):
+            if d == 0:
+                for name in ("cot", "wdl"):
+                    loads[name].wait()
+            light_pre(d)
+
+    @step("predmh")
+    def _():
+        loads["wdh"].wait()
+        dmh[...] = mm(grow[...], wdh[...])
 
     def hidden_rows(d, r):
         return tok[d, r, :].astype(F32) + tot1[d, r, :].astype(F32)
 
-    def ffn_norm(d):
+    def ffn_norm(d, h):
         def body(t):
-            r = pl.ds(t, big)
+            r = pl.ds(pl.multiple_of(h * half + t, big), big)
             hidden = hidden_rows(d, r)
             inv = lax.rsqrt(row_sum(hidden * hidden) * (1.0 / width) + epsilon)
             invf[d, r, :] = inv
             fl[d, r, :] = (hidden * inv * gain_f).astype(BF)
 
-        tiles(rows, big, body)
+        tiles(half, big, body)
+
+    for d in range(docs):
+        for h in range(2):
+
+            @step("nf%d%d" % (d, h))
+            def _(d=d, h=h):
+                if h == 0:
+                    for k in range(1, 4):
+                        frm = (b + 4 - k) % 4
+                        arrived(loall.at[frm, d], lo_s.at[d, k - 1], lo_r.at[d, k - 1], (frm, s))
+                attention_total(d, h)
+                ffn_norm(d, h)
 
     def ffn_heavy(d):
         rowsf = mm(pqk[d, 0:slots, :], fl[d])
@@ -893,139 +1006,225 @@
         dscore = lax.fori_loop(0, fh_n // step, body, jnp.zeros((slots, 1), F32))
         pre = dscore * score * (1.0 - score)
         cols[PREF, mine(d), :] = pre
-        return (mmt(dguh[mine(d), :], wguh[...]) + pre * router_f).astype(BF)
-
-    def ffn_light(d, back_rows):
+        backr[mine(d), :] = (mmt(dguh[mine(d), :], wguh[...]) + pre * router_f).astype(BF)
+
+    for d in range(docs):
+
+        @step("fh%d" % d)
+        def _(d=d):
+            if d == 0:
+                for name in ("gh", "uh"):
+                    loads[name].wait()
+            ffn_heavy(d)
+
+
+    def ffn_light(d, h):
+        r = pl.ds(h * half, half)
+        gu = mm(fl[d, r, :], wgul[...]).astype(BF)
+        gate = gu[:, 0:fl_n].astype(F32)
+        up = gu[:, fl_n : 2 * fl_n].astype(F32)
+        act, slope = gelu_parts(gate)
+        mid[d, r, :] = (act * up * valid_rows(d, h * half, half)).astype(BF)
+        grad_mid = dm[d, r, :]
+        dgu[d, r, 0:fl_n] = (grad_mid * up * slope).astype(BF)
+        dgu[d, r, fl_n : 2 * fl_n] = (grad_mid * act).astype(BF)
+        value = mmt(dgu[d, r, :], wgul[...]) + mm(pqkt[d, r, 0:slots], backr[mine(d), :])
+        parts[d, r, :] = value.astype(BF)
+        ar_start(1, d, h)
+
+    for d in range(docs):
         for h in range(2):
-            r = pl.ds(h * half, half)
-            gu = mm(fl[d, r, :], wgul[...]).astype(BF)
-            gate = gu[:, 0:fl_n].astype(F32)
-            up = gu[:, fl_n : 2 * fl_n].astype(F32)
-            act, slope = gelu_parts(gate)
-            mid[d, r, :] = (act * up * valid_rows(d, h * half, half)).astype(BF)
-            grad_mid = dm[d, r, :]
-            dgu[d, r, 0:fl_n] = (grad_mid * up * slope).astype(BF)
-            dgu[d, r, fl_n : 2 * fl_n] = (grad_mid * act).astype(BF)
-            value = mmt(dgu[d, r, :], wgul[...]) + mm(pqkt[d, r, 0:slots], back_rows)
-            parts[d, r, :] = value.astype(BF)
-            ar_start(1, d, h)
-
-    grads = ((g_h, ra_h, rb_h, rl_h), (g_l, ra_l, rb_l, rl_l), (g_a, ra_a, rb_a, rl_a))
-    packed_at = (0, g_h.shape[1], g_h.shape[1] + g_l.shape[1])
-    at_end = (z == 0) | (z == nz - 1)
-    inner = (z > 0) & (z < nz - 1)
-    low_side = jnp.where(z < nz // 2, 1, 0)
+
+            @step("fl%d%d" % (d, h))
+            def _(d=d, h=h):
+                if d == 0 and h == 0:
+                    for name in ("gl", "ul"):
+                        loads[name].wait()
+                ffn_light(d, h)
+
+            for a in (1, 2):
+                for i in range(1, 5):
+
+                    @step("ar%d%d%d_%d" % (a, d, h, i))
+                    def _(a=a, d=d, h=h, i=i):
+                        ar_step(a, d, h, i, tot2)
+
+    pieces = (
+        (g_h, 0, fh_n), (g_h, fh_n, fh_n), (g_h, 2 * fh_n, fh_n), (g_l, 0, 3 * fl_n),
+        (g_a, 0, wl + 512), (g_a, wl + 512, 3 * wl + 640),
+    )
+    packed_at = [sum(piece[2] for piece in pieces[:p]) for p in range(len(pieces))]
 
     def chunk_rows(zz, cc):
         return pl.ds(pl.multiple_of(chunk * (2 * zz + cc), chunk), chunk)
 
-    def rs_start(p):
-        grad, ra, rb, rl = grads[p]
-        for zz in range(nz):
+    def chunk_of(p, zz, cc):
+        grad, base, wide = pieces[p]
+        return grad.at[chunk_rows(zz, cc), pl.ds(base, wide)]
+
+    def rs_start(p, t):
+        for zz in (2 * t, 2 * t + 1):
             late.append(send(
-                grad.at[chunk_rows(zz, 1 - core), pl.ds(0, ra.shape[2])], ra.at[zz],
-                wa_s.at[p, zz], wa_r.at[p, zz], sibling,
+                chunk_of(p, zz, 1 - core), ra[p].at[zz], wa_s.at[p, zz], wa_r.at[p, zz], sibling
             ))
 
-    def add_chunk(grad, zz, other):
-        cut = other.shape[1]
+    def add_chunk(p, zz, other):
+        grad, base, wide = pieces[p]
 
         def add_body(t, carry):
             r = pl.ds(pl.multiple_of(chunk * (2 * zz + core) + 16 * t, 16), 16)
-            value = grad[r, 0:cut].astype(F32) + other[pl.ds(pl.multiple_of(16 * t, 16), 16), :].astype(F32)
-            grad[r, 0:cut] = value.astype(BF)
+            value = grad[r, base : base + wide].astype(F32)
+            value = value + other[pl.ds(pl.multiple_of(16 * t, 16), 16), :].astype(F32)
+            grad[r, base : base + wide] = value.astype(BF)
             return carry
 
         lax.fori_loop(0, chunk // 16, add_body, 0)
 
     def rs_direct(p, k, when):
-        grad, ra, rb, rl = grads[p]
         late.append((when, send(
-            grad.at[chunk_rows(zpeer(k), core), pl.ds(0, ra.shape[2])], rb.at[k - 1],
-            wz_s.at[p, k - 1], wz_r.at[p, k - 1], same_core(k), when,
+            chunk_of(p, zpeer(k), core), rb[p].at[k - 1], wz_s.at[p, k - 1], wz_r.at[p, k - 1],
+            same_core(k), when,
         )))
 
-    def rs_middle(p):
-        grad, ra, rb, rl = grads[p]
-        for i in range(1, nz + 1):
-            k = low_side * (nz - i) + (1 - low_side) * i if i < nz else nz
-            zz = zpeer(k)
-            arrived(ra.at[zz], wa_s.at[p, zz], wa_r.at[p, zz], sibling)
-            add_chunk(grad, zz, ra.at[zz])
-            if i == 1:
-                neighbour = (b, 2 * (z + 2 * low_side - 1) + core)
-                late.append((at_end, send(
-                    grad.at[chunk_rows(zz, core), pl.ds(0, ra.shape[2])], rl, rl_s.at[p], rl_r.at[p],
-                    neighbour, at_end,
-                )))
-                rs_direct(p, k, inner)
-            elif i == 2:
-                rs_direct(p, k, at_end)
-            elif i == 3:
-                rs_direct(p, k, z >= 0)
+    def rs_own(p, k):
+        zz = zpeer(k)
+        arrived(ra[p].at[zz], wa_s.at[p, zz], wa_r.at[p, zz], sibling)
+        add_chunk(p, zz, ra[p].at[zz])
+
+    def rs_far(p):
+        k = 1 + 2 * low_side
+        rs_own(p, k)
+        neighbour = (b, 2 * (z + 2 * low_side - 1) + core)
+        late.append((at_end, send(
+            chunk_of(p, zpeer(k), core), rl[p], rl_s.at[p], rl_r.at[p], neighbour, at_end
+        )))
+        rs_direct(p, k, inner)
+
+    def rs_two(p):
+        rs_own(p, 2)
+        rs_direct(p, 2, at_end)
+
+    def rs_near(p):
+        k = 3 - 2 * low_side
+        rs_own(p, k)
+        rs_direct(p, k, z >= 0)
 
     def rs_relay(p):
-        grad, ra, rb, rl = grads[p]
-
         @pl.when(inner)
         def _():
-            arrived(rl, rl_s.at[p], rl_r.at[p], same_core(1))
-            add_chunk(grad, zpeer(2), rl)
+            arrived(rl[p], rl_s.at[p], rl_r.at[p], same_core(1))
+            add_chunk(p, zpeer(2), rl[p])
 
         rs_direct(p, 2, inner)
 
+    for p in range(len(pieces)):
+        steps["rs%da" % p] = functools.partial(rs_far, p)
+        steps["rs%db" % p] = functools.partial(rs_two, p)
+        steps["rs%dc" % p] = functools.partial(rs_near, p)
+        steps["rs%dd" % p] = functools.partial(rs_own, p, nz)
+        steps["rs%dr" % p] = functools.partial(rs_relay, p)
+
     def rs_end(p):
-        grad, ra, rb, rl = grads[p]
-        cut = ra.shape[2]
+        grad, base, wide = pieces[p]
         for k, when in ((1, z > 0), (2, z >= 0), (3, z < nz - 1)):
 
             @pl.when(when)
             def _(k=k):
-                arrived(rb.at[k - 1], wz_s.at[p, k - 1], wz_r.at[p, k - 1], same_core(nz - k))
+                arrived(rb[p].at[k - 1], wz_s.at[p, k - 1], wz_r.at[p, k - 1], same_core(nz - k))
+
+        at = packed_at[p]
 
         def add_body(t, carry):
             r = pl.ds(pl.multiple_of(16 * t, 16), 16)
-            value = grad[pl.ds(pl.multiple_of(chunk * s + 16 * t, 16), 16), 0:cut].astype(F32)
+            value = grad[pl.ds(pl.multiple_of(chunk * s + 16 * t, 16), 16), base : base + wide].astype(F32)
             for k in range(1, nz):
-                value = value + rb[k - 1, r, :].astype(F32)
-            packed[r, packed_at[p] : packed_at[p] + cut] = value
+                value = value + rb[p][k - 1, r, :].astype(F32)
+            packed[r, at : at + wide] = value
             return carry
 
         lax.fori_loop(0, chunk // 16, add_body, 0)
-
-    @pl.when(z == 0)
+        leave(packed.at[:, at : at + wide], pack_o.at[:, at : at + wide], 7 + p)
+
+    @step("blank")
     def _():
-        for grad, ra, rb, rl in grads:
-            rb[0] = jnp.zeros(rb.shape[1:], BF)
-
-    @pl.when(z == nz - 1)
-    def _():
-        for grad, ra, rb, rl in grads:
-            rb[2] = jnp.zeros(rb.shape[1:], BF)
-
-    def heavy_ffn_grads():
-        step = 512
-        for src, gr, base, total in ((frow, dguh, 0, 2 * fh_n), (ghr, midh, 2 * fh_n, fh_n)):
-            for t in range(2):
-                f = slice(t * (width // 2), (t + 1) * (width // 2))
-                left_t = src[:, f].T
-
-                def body(i, carry, gr=gr, f=f, base=base, left_t=left_t):
-                    c = pl.ds(pl.multiple_of(i * step, step), step)
-                    o = pl.ds(pl.multiple_of(base + i * step, step), step)
-                    g_h[f, o] = mm(left_t, gr[:, c]).astype(BF)
-                    return carry
-
-                lax.fori_loop(0, total // step, body, 0)
-
-    def all_rows(ref, f):
-        return ref[:, :, f].reshape(docs * rows, ref[:, :, f].shape[2])
-
-    def light_grad(src, gr, ref, base):
-        for t in range(2):
-            f = slice(t * (width // 2), (t + 1) * (width // 2))
-            right_side = gr[...].reshape(docs * rows, gr.shape[2])
-            ref[f, base : base + gr.shape[2]] = tmm(all_rows(src, f), right_side).astype(BF)
+        @pl.when(z == 0)
+        def _():
+            for buf in rb:
+                buf[0] = jnp.zeros(buf.shape[1:], BF)
+
+        @pl.when(z == nz - 1)
+        def _():
+            for buf in rb:
+                buf[2] = jnp.zeros(buf.shape[1:], BF)
+
+    def half_features(t):
+        return slice(t * (width // 2), (t + 1) * (width // 2))
+
+    def heavy_ffn_grads(t, p):
+        size = 512
+        f = half_features(t)
+        src, gr, first = ((frow, dguh, 0), (frow, dguh, fh_n), (ghr, midh, 0))[p]
+        left_t = src[:, f].T
+
+        def body(i, carry):
+            c = pl.ds(pl.multiple_of(first + i * size, size), size)
+            o = pl.ds(pl.multiple_of(p * fh_n + i * size, size), size)
+            g_h[f, o] = mm(left_t, gr[:, c]).astype(BF)
+            return carry
+
+        lax.fori_loop(0, fh_n // size, body, 0)
+
+    def light_grad(t, src, gr, ref, base):
+        f = half_features(t)
+        wide = gr.shape[2]
+        value = tmm(src[:, :, f].reshape(docs * rows, width // 2), gr[...].reshape(docs * rows, wide))
+        ref[f, base : base + wide] = value.astype(BF)
+
+    def rows_grad(t, src, gr, at):
+        g_a[half_features(t), at : at + wh] = tmm(src[:, half_features(t)], gr).astype(BF)
+
+    def early_grads(t):
+        light_grad(t, ghb, loall.at[b], g_a, 0)
+        rows_grad(t, gah, hoall[b, :, 0:wh], wl)
+        rows_grad(t, hin, dqh[:, 0:wh], wl + 256)
+
+    def late_grads(t):
+        f = half_features(t)
+        at = wl + 512
+        light_grad(t, nl, dqkv, g_a, at)
+        rows_grad(t, kin, dkvh[:, 0:wh], at + 3 * wl)
+        rows_grad(t, sin, dkvh[:, 256 : 256 + wh], at + 3 * wl + 256)
+        lane = lax.broadcasted_iota(jnp.int32, (docs * slots, 128), 1)
+        vectors = jnp.zeros((width // 2, 128), F32)
+        for src, which, at_lane in ((hin, PREQ, 1), (kin, PREK, 2), (frow, PREF, 4)):
+            vectors = vectors + tmm(src[:, f], jnp.where(lane == at_lane, cols[which], 0.0).astype(BF))
+        at = at + 3 * wl + 512
+        g_a[f, at : at + 128] = vectors.astype(BF)
+
+    for t in range(2):
+
+        for p in range(3):
+
+            @step("hgr%s%d" % ("AB"[t], p))
+            def _(t=t, p=p):
+                heavy_ffn_grads(t, p)
+                rs_start(p, t)
+
+        @step("lg" + "AB"[t])
+        def _(t=t):
+            light_grad(t, fl, dgu, g_l, 0)
+            light_grad(t, cot, mid, g_l, 2 * fl_n)
+            rs_start(3, t)
+
+        @step("awg" + "AB"[t])
+        def _(t=t):
+            early_grads(t)
+            rs_start(4, t)
+
+        @step("aqg" + "AB"[t])
+        def _(t=t):
+            late_grads(t)
+            rs_start(5, t)
 
     def mixed_terms(d):
         def body(j, carry):
@@ -1042,9 +1241,9 @@
         own = jnp.where(column == lax.broadcasted_iota(jnp.int32, (share, width), 0), 1.0, 0.0).astype(BF)
         mixa[d] = mmt(own, tok[d]) + mmt(own, tot1[d]) + mixb[b, d].astype(F32)
 
-    def hidden_grad(d):
+    def hidden_grad(d, h):
         def body(t):
-            r = pl.ds(t, big)
+            r = pl.ds(pl.multiple_of(h * half + t, big), big)
             unit = hidden_rows(d, r) * invf[d, r, :]
             w = tot2[d, r, :].astype(F32) * gain_f
             inner = row_sum(w * unit) * (1.0 / width)
@@ -1052,14 +1251,14 @@
             ghf[d, r, :] = value
             ghb[d, r, :] = value.astype(BF)
 
-        tiles(rows, big, body)
+        tiles(half, big, body)
 
     def heavy_back(d):
         picked = mm(pqk[d, 0:slots, :], ghb[d])
         score = cols[SQ, mine(d), :]
         gah[mine(d), :] = (picked * score).astype(BF)
-        raw = mmt(picked.astype(BF), who[...])
-        pre = row_sum(hox[mine(d), 0:wh].astype(F32) * raw) * score * (1.0 - score)
+        raw = mmt(picked.astype(BF), woha[b])
+        pre = row_sum(hoall[b, mine(d), 0:wh].astype(F32) * raw) * score * (1.0 - score)
         cols[PREQ, mine(d), :] = pre
         dox[mine(d), 0:wh] = (raw * score).astype(BF)
         dox[mine(d), wh:256] = jnp.zeros((slots, 256 - wh), BF)
@@ -1087,7 +1286,7 @@
 
         def dol_body(t):
             r = pl.ds(t, half)
-            dol[d, r, :] = (mm(ghb[d, r, :], wol[...]) * valid_rows(d, t, half)).astype(BF)
+            dol[d, r, :] = (mm(ghb[d, r, :], wola[b]) * valid_rows(d, t, half)).astype(BF)
 
         tiles(rows, half, dol_body)
 
@@ -1130,7 +1329,7 @@
         def _():
             arrived(rimr.at[d, 0], rim_s.at[d, 1], rim_r.at[d, 1], left)
 
-    def attention_back_terms(d):
+    def attention_back_rows(d):
         heavy_back_keys(d)
         ds_in = mm(dkvh[mine(d), 256 : 256 + wh], whv[...])
         score = cols[SK, mine(d), :]
@@ -1138,110 +1337,104 @@
         cols[PREK, mine(d), :] = pre_k
         key_rows = mm(dkvh[mine(d), 0:wh], whk[...]) + ds_in * score + pre_k * router_k
         query_rows = mm(dqh[mine(d), 0:wh], whq[...]) + cols[PREQ, mine(d), :] * router_q
-        both = jnp.concatenate([query_rows, key_rows], axis=0).astype(BF)
-        rim_wait(d)
-        dkvw[d, radius : 2 * radius, :] += rimr[d, 0].astype(F32)
-        dkvw[d, rows : rows + radius, :] += rimr[d, 1].astype(F32)
-        for h in range(2):
-            r = pl.ds(h * half, half)
-            dqkv[d, r, wl : 3 * wl] = dkvw[d, pl.ds(h * half + radius, half), :].astype(BF)
-            value = mmt(dqkv[d, r, :], wqkv[...]) + mm(pqkt[d, r, :], both)
-            parts[d, r, :] = value.astype(BF)
-            ar_start(2, d, h)
-
-    def token_grad(d):
+        bothr[d, 0:slots, :] = query_rows.astype(BF)
+        bothr[d, slots : 2 * slots, :] = key_rows.astype(BF)
+
+    def attention_back_terms(d, h):
+        if h == 0:
+            rim_wait(d)
+            dkvw[d, radius : 2 * radius, :] += rimr[d, 0].astype(F32)
+            dkvw[d, rows : rows + radius, :] += rimr[d, 1].astype(F32)
+            ar_sent(1, d)
+        r = pl.ds(h * half, half)
+        dqkv[d, r, wl : 3 * wl] = dkvw[d, pl.ds(h * half + radius, half), :].astype(BF)
+        value = mmt(dqkv[d, r, :], wqkv[...]) + mm(pqkt[d, r, :], bothr[d])
+        parts[d, r, :] = value.astype(BF)
+        ar_start(2, d, h)
+
+    out_copies = []
+
+    def leave(src, dst, i):
+        copy = pltpu.make_async_copy(src, dst, out_s.at[i])
+        copy.start()
+        out_copies.append(copy)
+
+    def token_grad(d, h):
         def body(t):
-            r = pl.ds(t, big)
+            r = pl.ds(pl.multiple_of(h * half + t, big), big)
             inv = inva[d, r, :]
             unit = tok[d, r, :].astype(F32) * inv
             w = tot2[d, r, :].astype(F32) * gain_a
             inner = row_sum(w * unit) * (1.0 / width)
             ghf[d, r, :] = ghf[d, r, :] + inv * (w - unit * inner)
 
-        tiles(rows, big, body)
-        copy = pltpu.make_async_copy(ghf.at[d], gt_o.at[d], out_s.at[1 + d])
-        copy.start()
-        return copy
-
-    gather_pass(1, qall, every)
-    ar_step(0, 0, 4, tot1)
-    ffn_norm(0)
-    back0 = ffn_heavy(0)
-    ar_step(0, 1, 3, tot1)
-    ffn_light(0, back0)
-    ar_step(0, 1, 4, tot1)
-    ffn_norm(1)
-    back1 = ffn_heavy(1)
-    ar_step(1, 0, 1, tot2)
-    heavy_ffn_grads()
-    rs_start(0)
-    ffn_light(1, back1)
-    ar_step(1, 0, 2, tot2)
-    rs_middle(0)
-    light_grad(fl, dgu, g_l, 0)
-    ar_step(1, 1, 1, tot2)
-    ar_step(1, 0, 3, tot2)
-    light_grad(cot, mid, g_l, 2 * fl_n)
-    rs_start(1)
-    ar_step(1, 1, 2, tot2)
-    mixed_terms(0)
-    ar_step(1, 0, 4, tot2)
-    hidden_grad(0)
-    heavy_back(0)
-    ar_step(1, 1, 3, tot2)
-    rs_middle(1)
-    light_back(0)
-    mixed_terms(1)
-    ar_step(1, 1, 4, tot2)
-    for k in range(1, 4):
-        to = (b + k) % 4
-        late.append(send(mixb.at[to], mixr.at[k - 1], mx_s.at[k - 1], mx_r.at[k - 1], (to, s)))
-    hidden_grad(1)
-    gather_end(1, qall, every)
-    gather_pass(2, doall, routed(0))
-    heavy_back(1)
-    ar_sent(1, 0)
-    gather_end(2, doall, routed(0))
-    attention_back_terms(0)
-    rs_relay(0)
-    light_back(1)
-    gather_pass(3, doall, routed(1))
-    ar_step(2, 0, 1, tot2)
-    ar_sent(1, 1)
-    gather_end(3, doall, routed(1))
-    attention_back_terms(1)
-    ar_step(2, 0, 2, tot2)
-    ar_step(2, 1, 1, tot2)
-    rs_relay(1)
-
-    light_grad(nl, dqkv, g_a, 0)
-    light_grad(ghb, lo, g_a, 3 * wl)
-    at = 4 * wl
-    for src, gr in (
-        (hin, dqh[:, 0:wh]), (kin, dkvh[:, 0:wh]), (sin, dkvh[:, 256 : 256 + wh]), (gah, hox[:, 0:wh])
-    ):
-        g_a[:, at : at + wh] = tmm(src[...], gr).astype(BF)
-        at += 256
-    lane = lax.broadcasted_iota(jnp.int32, (docs * slots, 128), 1)
-    vectors = jnp.zeros((width, 128), F32)
-    for src, which, at_lane in ((hin, PREQ, 1), (kin, PREK, 2), (frow, PREF, 4)):
-        vectors = vectors + tmm(src[...], jnp.where(lane == at_lane, cols[which], 0.0).astype(BF))
-    g_a[:, at : at + 128] = vectors.astype(BF)
-    rs_start(2)
-    mixed_start(0)
-    mixed_start(1)
-    ar_step(2, 0, 3, tot2)
-    ar_step(2, 1, 2, tot2)
-    rs_middle(2)
-    rs_end(0)
-    ar_step(2, 0, 4, tot2)
-    out_copies = [token_grad(0)]
-    ar_step(2, 1, 3, tot2)
-    rs_end(1)
-    rs_relay(2)
-
-    for name in ("gk", "uk"):
-        loads[name].wait()
+        tiles(half, big, body)
+        r = pl.ds(h * half, half)
+        leave(ghf.at[d, r], gt_o.at[d, r], 3 + 2 * d + h)
+
+    for d in range(docs):
+
+        @step("mixt%d" % d)
+        def _(d=d):
+            mixed_terms(d)
+
+        @step("mx%d" % d)
+        def _(d=d):
+            for k in range(1, 4):
+                to = (b + k) % 4
+                late.append(send(
+                    mixb.at[to, d], mixr.at[k - 1, d], mx_s.at[d, k - 1], mx_r.at[d, k - 1], (to, s)
+                ))
+
+        @step("mixs%d" % d)
+        def _(d=d):
+            mixed_start(d)
+
+        @step("mixf%d" % d)
+        def _(d=d):
+            for k in range(1, 4):
+                frm = (b + 4 - k) % 4
+                arrived(mixr.at[k - 1, d], mx_s.at[d, k - 1], mx_r.at[d, k - 1], (frm, s))
+
+            def mix_body(t, d=d):
+                r = pl.ds(t, 32)
+                value = mixa[d, r, :]
+                for k in range(3):
+                    value = value + mixr[k, d, r, :].astype(F32)
+                mixa[d, r, :] = value
+
+            tiles(share, 32, mix_body)
+            leave(mixa.at[d], mix_o.at[d], 1 + d)
+
+        for h in range(2):
+
+            @step("hg%d%d" % (d, h))
+            def _(d=d, h=h):
+                hidden_grad(d, h)
+
+            @step("abt%d%d" % (d, h))
+            def _(d=d, h=h):
+                attention_back_terms(d, h)
+
+            @step("tok%d%d" % (d, h))
+            def _(d=d, h=h):
+                token_grad(d, h)
+
+        @step("hb%d" % d)
+        def _(d=d):
+            heavy_back(d)
+
+        @step("lb%d" % d)
+        def _(d=d):
+            light_back(d)
+
+        @step("hk%d" % d)
+        def _(d=d):
+            if d == 0:
+                gather_end(1, qall, every)
+            gather_end(2 + d, doall, routed(d))
+            attention_back_rows(d)
+
     vlane = lax.broadcasted_iota(jnp.int32, (chunk, 128), 1)
     eye = lax.broadcasted_iota(jnp.int32, (chunk, width), 1) - chunk * s
     eye = eye == lax.broadcasted_iota(jnp.int32, (chunk, width), 0)
@@ -1249,57 +1442,49 @@
     def own_column(row):
         return row_sum(jnp.where(eye, row, 0.0))
 
-    gf_sum = row_sum(packed[:, 0 : 2 * fh_n] * wkeep[...].astype(F32))
-    gf_sum = gf_sum + row_sum(
-        packed[:, packed_at[1] : packed_at[1] + 2 * fl_n] * wgul[own_rows, :].astype(F32)
-    )
-    for k in range(1, 4):
-        frm = (b + 4 - k) % 4
-        arrived(mixr.at[k - 1], mx_s.at[k - 1], mx_r.at[k - 1], (frm, s))
-    for d in range(docs):
-
-        def mix_body(t, d=d):
-            r = pl.ds(t, 32)
-            value = mixa[d, r, :]
-            for k in range(3):
-                value = value + mixr[k, d, r, :].astype(F32)
-            mixa[d, r, :] = value
-
-        tiles(share, 32, mix_body)
-    mix_copy = pltpu.make_async_copy(mixa, mix_o, out_s.at[3])
-    mix_copy.start()
-    out_copies.append(mix_copy)
-    ar_step(2, 1, 4, tot2)
-    out_copies.append(token_grad(1))
-    rs_end(2)
-    a_at = packed_at[2]
-    va = packed.shape[1] - 128
-    ga_sum = row_sum(packed[:, a_at : a_at + 3 * wl] * wqkv[own_rows, :].astype(F32))
-    eye_b = eye.astype(F32).astype(BF)
-    for i, w in enumerate((whq, whk, whv)):
-        h_at = a_at + 4 * wl + 256 * i
-        ga_sum = ga_sum + row_sum(packed[:, h_at : h_at + wh] * mmt(eye_b, w[...]))
-    vectors = packed[:, va : va + 128]
-
-    def lane_of(i):
-        return row_sum(jnp.where(vlane == i, vectors, 0.0))
-
-    ga_sum = ga_sum + own_column(router_q) * lane_of(1) + own_column(router_k) * lane_of(2)
-    gf_sum = gf_sum + own_column(router_f) * lane_of(4)
-    vectors = jnp.where(vlane == 0, ga_sum / own_column(gain_a), vectors)
-    vectors = jnp.where(vlane == 3, gf_sum / own_column(gain_f), vectors)
-    vbuf[...] = vectors
-    pack_copy = pltpu.make_async_copy(packed, pack_o, out_s.at[4])
-    pack_copy.start()
-    out_copies.append(pack_copy)
-    for k in range(1, 4):
-        late.append(send(vbuf, vr.at[k - 1], v_s.at[k - 1], v_r.at[k - 1], ((b + k) % 4, s)))
-    for k in range(1, 4):
-        arrived(vr.at[k - 1], v_s.at[k - 1], v_r.at[k - 1], ((b + 4 - k) % 4, s))
-    vect[...] = (vbuf[...] + vr[0] + vr[1] + vr[2]).T
-    vec_copy = pltpu.make_async_copy(vect, vec_o, out_s.at[0])
-    vec_copy.start()
-    out_copies.append(vec_copy)
+    for p in range(len(pieces)):
+        steps["rs%de" % p] = functools.partial(rs_end, p)
+
+    @step("gains")
+    def _():
+        for name in ("gk", "uk"):
+            loads[name].wait()
+        total = row_sum(packed[:, 0 : 2 * fh_n] * wkeep[...].astype(F32))
+        vbuf[:, 0:1] = total + row_sum(
+            packed[:, packed_at[3] : packed_at[3] + 2 * fl_n] * wgul[own_rows, :].astype(F32)
+        )
+
+    @step("vec")
+    def _():
+        a_at, q_at = packed_at[4:6]
+        va = q_at + 3 * wl + 512
+        gf_sum = vbuf[:, 0:1]
+        ga_sum = row_sum(packed[:, q_at : q_at + 3 * wl] * wqkv[own_rows, :].astype(F32))
+        eye_b = eye.astype(F32).astype(BF)
+        for h_at, w in ((a_at + wl + 256, whq), (q_at + 3 * wl, whk), (q_at + 3 * wl + 256, whv)):
+            ga_sum = ga_sum + row_sum(packed[:, h_at : h_at + wh] * mmt(eye_b, w[...]))
+        vectors = packed[:, va : va + 128]
+
+        def lane_of(i):
+            return row_sum(jnp.where(vlane == i, vectors, 0.0))
+
+        ga_sum = ga_sum + own_column(router_q) * lane_of(1) + own_column(router_k) * lane_of(2)
+        gf_sum = gf_sum + own_column(router_f) * lane_of(4)
+        vectors = jnp.where(vlane == 0, ga_sum / own_column(gain_a), vectors)
+        vectors = jnp.where(vlane == 3, gf_sum / own_column(gain_f), vectors)
+        vbuf[...] = vectors
+        for k in range(1, 4):
+            late.append(send(vbuf, vr.at[k - 1], v_s.at[k - 1], v_r.at[k - 1], ((b + k) % 4, s)))
+
+    @step("vece")
+    def _():
+        for k in range(1, 4):
+            arrived(vr.at[k - 1], v_s.at[k - 1], v_r.at[k - 1], ((b + 4 - k) % 4, s))
+        vect[...] = (vbuf[...] + vr[0] + vr[1] + vr[2]).T
+        leave(vect, vec_o, 0)
+
+    for name in ORDER:
+        steps[name]()
 
     for entry in late:
         if isinstance(entry, tuple):
@@ -1307,7 +1492,6 @@
         else:
             entry.wait_send()
     for d in range(docs):
-        ar_sent(0, d)
         ar_sent(2, d)
     for copy in out_copies:
         copy.wait()
@@ -1320,19 +1504,21 @@
     keys = n_seq * slots
     pad = -(-wh // 256) * 256
     ga_n = 4 * wl + 4 * pad + 128
+    widths = [fh_n, fh_n, fh_n, 3 * fl_n, wl + 512, 3 * wl + 640]
     h_n, l_n = 3 * fh_n, 3 * fl_n
     radius = WINDOW // 2
     span = rows + 2 * radius
     vmem = [
-        ((docs, rows, width), BF), ((docs, rows, width), BF), ((width, 3 * wl), BF), ((width, wl), BF),
-        ((wh, width), BF), ((wh, width), BF), ((wh, width), BF), ((wh, width), BF),
+        ((docs, rows, width), BF), ((docs, rows, width), BF), ((width, 3 * wl), BF), ((4, width, wl), BF),
+        ((wh, width), BF), ((wh, width), BF), ((wh, width), BF), ((4, wh, width), BF),
         ((width, 2 * fl_n), BF), ((width, fl_n), BF), ((width, 2 * fh_n), BF), ((width, fh_n), BF),
         ((chunk, 2 * fh_n), BF),
         ((docs, rows, width), BF), ((docs, rows, 1), F32), ((routed, width), BF), ((routed, width), BF),
         ((routed, width), BF), ((docs, rows, wl), BF), ((docs, span, 2 * wl), BF),
-        ((docs * rows // WINDOW, 2 * WINDOW, 2 * WINDOW), BF), ((docs, rows, wl), BF), ((routed, pad), BF),
-        ((n_seq, routed, 2 * pad), BF), ((docs, wh // HD * slots, keys), BF), ((routed, pad), BF),
-        ((n_seq, routed, pad), BF), ((n_seq, routed, pad), BF),
+        ((docs * rows // WINDOW, 2 * WINDOW, 2 * WINDOW), BF), ((4, docs, rows, wl), BF), ((routed, pad), BF),
+        ((n_seq, routed, 2 * pad), BF), ((docs, wh // HD * slots, keys), BF), ((4, routed, pad), BF),
+        ((n_seq, routed, pad), BF), ((n_seq, routed, pad), BF), ((routed, width), BF), ((routed, width), BF),
+        ((docs, 2 * slots, width), BF),
         ((docs, 2 * slots, rows), BF), ((docs, rows, 2 * slots), BF), ((docs, rows, width), BF),
         ((docs, rows, width), BF), ((docs, rows, width), BF), ((docs, 2, rows // 4, width), BF),
         ((docs, 2, rows // 8, width), BF), ((6, routed, 1), F32),
@@ -1345,15 +1531,16 @@
         ((docs, 2, radius, 2 * wl), BF), ((docs, 2, radius, 2 * wl), BF), ((docs, rows, 3 * wl), BF),
         ((routed, 2 * pad), BF),
         ((width, h_n), BF), ((width, l_n), BF),
-        ((nz, chunk, h_n), BF), ((nz, chunk, l_n), BF), ((nz, chunk, ga_n), BF),
-        ((nz - 1, chunk, h_n), BF), ((nz - 1, chunk, l_n), BF), ((nz - 1, chunk, ga_n), BF),
-        ((chunk, h_n), BF), ((chunk, l_n), BF), ((chunk, ga_n), BF),
+        *[((nz, chunk, wide), BF) for wide in widths],
+        *[((nz - 1, chunk, wide), BF) for wide in widths],
+        *[((chunk, wide), BF) for wide in widths],
         ((chunk, h_n + l_n + ga_n), F32), ((chunk, 128), F32), ((3, chunk, 128), F32), ((128, chunk), F32),
     ]
     sems = [
-        (18,), (3, docs, 2, 4), (3, docs, 2, 4), (2 + docs, nz), (2 + docs, nz), (2 + docs, nz), (2 + docs, nz),
-        (docs, 2), (docs, 2), (docs, 2), (docs, 2), (3,), (3,),
-        (3, nz), (3, nz), (3, nz - 1), (3, nz - 1), (3,), (3,), (3,), (3,), (5,),
+        (18,), (3, 2), (3, 2), (3, 2), (3, 2), (docs, 3), (docs, 3), (3,), (3,),
+        (3, docs, 2, 4), (3, docs, 2, 4), (2 + docs, nz), (2 + docs, nz), (2 + docs, nz), (2 + docs, nz),
+        (docs, 2), (docs, 2), (docs, 2), (docs, 2), (docs, 3), (docs, 3),
+        (6, nz), (6, nz), (6, nz - 1), (6, nz - 1), (6,), (6,), (3,), (3,), (13,),
     ]
     total = 0
     for shape, kind in vmem:
@@ -1374,7 +1561,7 @@
     dims = (docs, rows, width, slots, n_seq, wl, wh, fl_n, fh_n)
     vmem, sems, total = kernel_scratch(*dims)
     fits = (
-        total <= 60 * 2**20
+        total <= 62 * 2**20
         and sizes["branch"] == 4
         and n_seq == 8
         and width % (16 * n_seq) == 0
@@ -1414,8 +1601,9 @@
 
     l_at = 3 * fh_n
     a_at = l_at + 3 * fl_n
-    h_at = a_at + 4 * wl
-    parts = [(a_at + i * wl, wl) for i in range(4)] + [(h_at + i * 256, wh) for i in range(4)]
+    q_at = a_at + wl + 512
+    parts = [(q_at + i * wl, wl) for i in range(3)] + [(a_at, wl)]
+    parts += [(a_at + wl + 256, wh), (q_at + 3 * wl, wh), (q_at + 3 * wl + 256, wh), (a_at + wl, wh)]
     parts += [(l_at + i * fl_n, fl_n) for i in range(3)] + [(i * fh_n, fh_n) for i in range(3)]
     outs = pl.pallas_call(
         functools.partial(hand_out, parts),

time: 180 us -> 147 us (0.82)
  Pallas kernels: 177 us -> 145 us
    pallas_call x1, Pallas kernels: 172 us -> 140 us  [shards(): pl.pallas_call(functools.partial(layer_kernel, dims), out_shape=[jax.Shap...]
where the time goes in v4:
time: 147 us
  Pallas kernels  145 us (99%)
    pallas_call x1, Pallas kernels, shards(): pl.pallas_call(functools.partial(layer_kernel, dims), out_shape=[jax.Shap...  140 us
    pallas_call x1, Pallas kernels, shards(): pl.pallas_call(functools.partial(hand_out, parts), out_shape=[jax.ShapeDt...  5.03 us

profile of v4, /device:TPU:0, one launch (start us, length us, event | category | flops | bytes accessed | tf_op | source)
XLA Modules:
  0.0 146.9 jit_solution(16421838093057409532)
XLA Ops:
  0.7 139.8 %shard_map.391 = (f32[2,512,768]{2,1,0:T(8,128)}, f32[2,192,512]{2,1,0:T(8,128)}, f32[96,5504]{1,0:T(8,128)}, f32[128,96]{1,0:T(8,128)}) custom-call(s32[2]{0:T(128)} %refs_0_.1, s32[2,64]{1,0:T(2,128)} %refs_1_.1, s32[2,64]{1,0:T(2,128)} %refs_2_.1, bf16[768]{0:T(1024)(128)(2,1)} %refs_3_.1, bf16[768]{0:T(1024)(128)(2,1)} %refs_4_.1, ...), custom_call_target="tpu_custom_call" | custom-call | tf_op jit(solution)/shard_map/pallas_call | solution.py:1585
  140.5 5.0 %shard_map.392 = (f32[2,512,768]{2,1,0:T(8,128)}, f32[2,192,512]{2,1,0:T(8,128)}, f32[96,128]{1,0:T(8,128)}, f32[96,128]{1,0:T(8,128)}, f32[96,128]{1,0:T(8,128)...) custom-call(f32[2,512,768]{2,1,0:T(8,128)} %get-tuple-element.41.tok, ...), custom_call_target="tpu_custom_call" | custom-call | tf_op jit(solution)/shard_map/pallas_call | solution.py:1608
  145.5 1.4 slice_bitcast_fusion

commit v5 on v4

--- a/solution.py
+++ b/solution.py
@@ -395,19 +395,24 @@
 
 
 ORDER = (
-    "load", "rowskv", "pre0", "norm", "qkv", "pre1", "gp0_2", "la0", "predmh", "gp0_1", "gp0_3", "wgp",
-    "hattn", "la1", "hproj", "nf00", "nf01", "fh0", "fl00", "nf10", "nf11", "fh1", "hgrA1", "hgrA0", "fl01",
-    "hgrB0", "rs0a", "fl11", "hgrB1", "rs0b", "ar101_1", "fl10", "rs1a", "lgA", "ar100_1", "lgB", "ar101_2",
-    "rs0r", "ar110_1", "ar100_2", "ar111_1", "rs1b", "hgrB2", "mixt1", "rs3a", "ar110_2", "ar100_3",
-    "ar111_2", "rs3b", "mixt0", "rs1c", "ar101_3", "gp1_1", "ar110_3", "gp1_2", "ar111_3", "ar101_4", "mx1",
-    "ar100_4", "hg00", "hg01", "rs3r", "hb0", "mx0", "rs1d", "rs1r", "lb0", "rs0c", "gp1_3", "ar110_4",
-    "mixs1", "ar111_4", "hg10", "hg11", "hgrA2", "gp2_3", "rs3c", "hb1", "gp2_1", "gp2_2", "mixs0", "awgB",
-    "lb1", "hk0", "rs2a", "rs2b", "abt00", "abt01", "gp3_1", "blank", "gp3_2", "gp3_3", "rs2r", "rs2c",
-    "ar200_1", "hk1", "rs0d", "awgA", "rs2d", "rs4a", "ar201_1", "ar200_2", "rs4b", "abt10", "ar201_2",
-    "abt11", "ar200_3", "rs4c", "aqgA", "aqgB", "rs5a", "ar210_1", "rs5b", "rs4r", "rs5d", "rs5c",
-    "ar210_2", "ar211_1", "ar201_3", "rs3d", "mixf0", "ar210_3", "rs2e", "ar211_2", "ar201_4", "rs5r",
-    "rs4d", "ar210_4", "tok10", "rs4e", "rs1e", "ar211_3", "rs3e", "rs0e", "gains", "rs5e", "vec", "tok01",
-    "ar211_4", "mixf1", "tok11", "ar200_4", "tok00", "vece",
+    "load", "rowskv", "norm", "pre0", "qkv", "gp0_2", "la0", "gp0_3", "gp0_1", "pre1", "hattn", "predmh",
+    "wgp", "la1", "hproj", "nf00", "nf01", "fh0", "fl00", "fl01", "gp1_2", "nf10", "nf11", "fh1", "hgrB1",
+    "ar1011_1", "hgrA1", "fl11", "hgrB0", "ar1001_1", "ar1010_1", "ar1011_2", "rs1a", "rs1b", "rs1c",
+    "fl10", "hgrA0", "hgrB2", "ar1011_3", "ar1010_2", "hgrA2", "ar1101_1", "ar1110_1", "lgA", "rs0a",
+    "ar1111_1", "rs1r", "ar1100_1", "ar1001_2", "ar1000_1", "ar1111_2", "gp1_3", "lgB", "ar1101_2",
+    "ar1000_2", "ar1001_3", "ar1011_4", "rs0b", "ar1111_3", "ar1000_3", "rs2d", "ar1100_2", "ar1010_3",
+    "ar1001_4", "ar1101_3", "ar1100_3", "rs2a", "rs0c", "ar1110_2", "ar1000_4", "rs0d", "mixt0", "ar1111_4",
+    "rs0r", "ar1110_3", "mixt1", "ar1010_4", "mx1", "gp1_1", "mixs0", "hg01", "hg00", "ar1100_4", "hb0",
+    "mx0", "ar1110_4", "lb0", "mixs1", "hg11", "rs2b", "gp2_2", "ar1101_4", "hg10", "hb1", "awgA", "rs3a",
+    "gp2_3", "lb1", "awgB", "rs3b", "rs3c", "gp3_2", "abt00", "rs2c", "rs4a", "gp3_3", "abt01", "rs2r",
+    "gp2_1", "abt10", "abt11", "ar2011_1", "blank", "ar2000_1", "hk0", "rs4b", "gp3_1", "ar2010_1", "hk1",
+    "ar2111_1", "rs3r", "ar2101_1", "aqgA", "ar2000_2", "mixf1", "ar2110_1", "ar2001_1", "rs4d", "kar1_1",
+    "ar2100_1", "aqgB", "ar2111_2", "rs4c", "kar0_1", "ar2010_2", "rs3d", "rs1d", "kar0_2", "ar2011_2",
+    "ar2100_2", "mixf0", "rs1e", "rs5a", "ar2101_2", "ar2110_2", "ar2000_3", "rs5b", "rs5c", "ar2111_3",
+    "ar2110_3", "ar2000_4", "ar2111_4", "ar2100_3", "ar2001_2", "ar2011_3", "rs4r", "rs5d", "kar1_2",
+    "rs5r", "rs0e", "rs3e", "ar2001_3", "kar1_3", "kar0_3", "kar0_4", "ar2101_3", "ar2100_4", "rs4e",
+    "rs2e", "gains", "ar2110_4", "ar2010_3", "rs5e", "vec", "ar2001_4", "tok00", "ar2010_4", "ar2101_4",
+    "kar1_4", "ar2011_4", "tok10", "tok01", "tok11", "vece",
 )
 BF = jnp.bfloat16
 F32 = jnp.float32
@@ -445,7 +450,6 @@
     chunk = width // n_seq
     half = rows // 2
     quarter = rows // 4
-    eighth = rows // 8
     radius = WINDOW // 2
     share = width // 4
     it = iter(refs)
@@ -458,14 +462,14 @@
      gl_h, ul_h, dl_h, gh_h, uh_h, dh_h) = take(16)
     gt_o, mix_o, pack_o, vec_o = take(4)
     (tok, cot, wqkv, wola, whq, whk, whv, woha, wgul, wdl, wguh, wdh, wkeep) = take(13)
-    (nl, inva, hin, kin, sin, qbuf, kvw, pbuf, loall, hqx, kvall, ph, hoall, qall, doall, hproj, backr, bothr) = take(18)
+    (nl, inva, hin, kin, sin, qbuf, kvw, pbuf, loall, hqx, kvall, ph, hoall, qall, doall, hproj, backr, qrow, kpart, ktot, k1, k2) = take(22)
     (pqk, pqkt, parts, tot1, tot2, r1, r2, cols) = take(8)
     (dm, dmh, grow, fl, invf, mid, dgu, frow, ghr, midh, dguh) = take(11)
     (mixb, mixr, mixa, ghf, ghb, dol, dox, gah, dqh, dkvw, rims, rimr, dqkv, dkvh) = take(14)
     (g_h, g_l, ra, rb, rl, packed, vbuf, vr, vect) = take(2) + [take(6), take(6), take(6)] + take(4)
     g_a = wguh
-    (load_s, wg_s, wg_r, wf_s, wf_r, lo_s, lo_r, ho_s, ho_r, ar_s, ar_r, ag_s, ag_r, fw_s, fw_r, halo_s, halo_r, rim_s, rim_r,
-     mx_s, mx_r, wa_s, wa_r, wz_s, wz_r, rl_s, rl_r, v_s, v_r, out_s) = take(30)
+    (load_s, wg_s, wg_r, wf_s, wf_r, lo_s, lo_r, ho_s, ho_r, ka_s, ka_r, ar_s, ar_r, ag_s, ag_r, fw_s, fw_r, halo_s, halo_r, rim_s, rim_r,
+     mx_s, mx_r, wa_s, wa_r, wz_s, wz_r, rl_s, rl_r, v_s, v_r, out_s) = take(32)
 
     b = lax.axis_index("branch")
     s = lax.axis_index("seq")
@@ -565,61 +569,89 @@
 
         lax.fori_loop(0, count // size, step, 0)
 
-    def geometry(h):
-        first, second = ((dev_x, bit_x), (dev_y, bit_y))[:: 1 if h == 0 else -1]
-        base = half * h
-        keep1 = base + quarter * first[1]
-        send1 = base + quarter * (1 - first[1])
-        keep2 = keep1 + eighth * second[1]
-        send2 = keep1 + eighth * (1 - second[1])
-        return (first[0], second[0]) + tuple(pl.multiple_of(v, eighth) for v in (keep1, send1, keep2, send2))
-
     flights = {}
 
+    def add_rows(src, at, buf, base, dst, count):
+        size = min(count, 32)
+
+        def body(t, carry):
+            r = pl.multiple_of(t * size, size)
+            here = pl.ds(pl.multiple_of(at + r, 16), size)
+            value = src[here, :].astype(F32) + buf[pl.ds(pl.multiple_of(base + r, 16), size), :].astype(F32)
+            dst[here, :] = value.astype(BF)
+            return carry
+
+        lax.fori_loop(0, count // size, body, 0)
+
+    def rows_sum(key, src, dst, b1, b2, ss, rs, base, count, way, src_base=None):
+        first, second = ((dev_x, bit_x), (dev_y, bit_y))[:: 1 - 2 * way]
+        two, four = count // 2, count // 4
+        keep1, send1 = two * first[1], two * (1 - first[1])
+        keep2, send2 = keep1 + four * second[1], keep1 + four * (1 - second[1])
+        shift = base if src_base is None else src_base
+
+        def rows_at(ref, at, size, frm):
+            return ref.at[pl.ds(pl.multiple_of(frm + at, 16), size)]
+
+        def start():
+            flights[key, 0] = send(rows_at(src, send1, two, shift), b1, ss.at[0], rs.at[0], first[0])
+
+        def one():
+            arrived(b1, ss.at[0], rs.at[0], first[0])
+            add_rows(src, shift + send2, b1, send2 - keep1, src, four)
+            flights[key, 1] = send(rows_at(src, send2, four, shift), b2, ss.at[1], rs.at[1], second[0])
+            add_rows(src, shift + keep2, b1, keep2 - keep1, src, four)
+
+        def two_():
+            arrived(b2, ss.at[1], rs.at[1], second[0])
+            size = min(four, 32)
+
+            def body(t, carry):
+                r = pl.multiple_of(t * size, size)
+                value = src[pl.ds(pl.multiple_of(shift + keep2 + r, 16), size), :].astype(F32)
+                value = value + b2[pl.ds(r, size), :].astype(F32)
+                dst[pl.ds(pl.multiple_of(base + keep2 + r, 16), size), :] = value.astype(BF)
+                return carry
+
+            lax.fori_loop(0, four // size, body, 0)
+            own = rows_at(dst, keep2, four, base)
+            flights[key, 2] = send(own, own, ss.at[2], rs.at[2], second[0])
+
+        def three():
+            arrived(rows_at(dst, send2, four, base), ss.at[2], rs.at[2], second[0])
+            own = rows_at(dst, keep1, two, base)
+            flights[key, 3] = send(own, own, ss.at[3], rs.at[3], first[0])
+
+        def last_():
+            arrived(rows_at(dst, send1, two, base), ss.at[3], rs.at[3], first[0])
+            flights[key, 0].wait_send()
+            flights[key, 1].wait_send()
+
+        return start, one, two_, three, last_
+
+    sums = {}
+    for a in (1, 2):
+        for d in range(docs):
+            for h in range(2):
+                for u in range(2):
+                    sums[a, d, h, u] = rows_sum(
+                        (a, d, h, u), parts.at[d], tot2.at[d], r1.at[d, h, u], r2.at[d, h, u],
+                        ar_s.at[a, d, h, u], ar_r.at[a, d, h, u], half * h + quarter * u, quarter, u,
+                    )
+    for d in range(docs):
+        sums[d] = rows_sum(
+            d, kpart.at[d], ktot.at[d], k1.at[d], k2.at[d], ka_s.at[d], ka_r.at[d], slots, slots, d, 0
+        )
+
     def ar_start(a, d, h):
-        first, second, keep1, send1, keep2, send2 = geometry(h)
-        flights[a, d, h, 0] = send(
-            parts.at[d, pl.ds(send1, quarter)], r1.at[d, h], ar_s.at[a, d, h, 0], ar_r.at[a, d, h, 0], first
-        )
-
-    def add_rows(d, at, buf, base, total):
-        def body(t, carry):
-            r = pl.multiple_of(t * 32, 32)
-            here = pl.ds(pl.multiple_of(at + r, 32), 32)
-            value = parts[d, here, :].astype(F32) + buf[pl.ds(base + r, 32), :].astype(F32)
-            total[d, here, :] = value.astype(BF)
-            return carry
-
-        lax.fori_loop(0, eighth // 32, body, 0)
-
-    def ar_step(a, d, h, step, total):
-        first, second, keep1, send1, keep2, send2 = geometry(h)
-        at = (a, d, h)
-        if step == 1:
-            arrived(r1.at[d, h], ar_s.at[a, d, h, 0], ar_r.at[a, d, h, 0], first)
-            add_rows(d, send2, r1.at[d, h], pl.multiple_of(send2 - keep1, eighth), parts)
-            flights[at + (1,)] = send(
-                parts.at[d, pl.ds(send2, eighth)], r2.at[d, h], ar_s.at[a, d, h, 1], ar_r.at[a, d, h, 1], second
-            )
-            add_rows(d, keep2, r1.at[d, h], pl.multiple_of(keep2 - keep1, eighth), parts)
-        elif step == 2:
-            arrived(r2.at[d, h], ar_s.at[a, d, h, 1], ar_r.at[a, d, h, 1], second)
-            add_rows(d, keep2, r2.at[d, h], 0, total)
-            own = total.at[d, pl.ds(keep2, eighth)]
-            flights[at + (2,)] = send(own, own, ar_s.at[a, d, h, 2], ar_r.at[a, d, h, 2], second)
-        elif step == 3:
-            arrived(total.at[d, pl.ds(send2, eighth)], ar_s.at[a, d, h, 2], ar_r.at[a, d, h, 2], second)
-            own = total.at[d, pl.ds(keep1, quarter)]
-            flights[at + (3,)] = send(own, own, ar_s.at[a, d, h, 3], ar_r.at[a, d, h, 3], first)
-        else:
-            arrived(total.at[d, pl.ds(send1, quarter)], ar_s.at[a, d, h, 3], ar_r.at[a, d, h, 3], first)
-            flights[at + (0,)].wait_send()
-            flights[at + (1,)].wait_send()
+        for u in range(2):
+            sums[a, d, h, u][0]()
 
     def ar_sent(a, d):
         for h in range(2):
-            flights[a, d, h, 2].wait_send()
-            flights[a, d, h, 3].wait_send()
+            for u in range(2):
+                flights[(a, d, h, u), 2].wait_send()
+                flights[(a, d, h, u), 3].wait_send()
 
     steps = {}
 
@@ -811,24 +843,31 @@
         return jnp.where(lane < HD, v[:blk], v[blk:])
 
     def light_attention(d):
+        row = lax.broadcasted_iota(jnp.int32, (2 * blk, span), 0) % blk
+        col = lax.broadcasted_iota(jnp.int32, (2 * blk, span), 1)
+        near = (col >= row) & (col <= row + WINDOW)
+
         def body(i, carry):
-            at = pl.multiple_of(i * blk, blk)
-            q2 = two_heads(qbuf[d, pl.ds(at, blk), :])
-            k = kvw[d, pl.ds(at, span), 0:wl]
-            v = kvw[d, pl.ds(at, span), wl : 2 * wl]
-            row = lax.broadcasted_iota(jnp.int32, (2 * blk, span), 0) % blk
-            col = lax.broadcasted_iota(jnp.int32, (2 * blk, span), 1)
-            pos = col + (offset + at - radius)
-            seen = (col >= row) & (col <= row + WINDOW) & (pos >= 0) & (pos < lens[d])
-            scores = jnp.where(seen, mmt(q2, k) * HD ** (-0.5), masked_value)
-            e = jnp.exp(scores - jnp.max(scores, axis=-1, keepdims=True))
-            p = (e * (1.0 / row_sum(e))).astype(BF)
-            pbuf[d * n_blk + i] = p
-            out = one_of_two(mm(p, v))
-            loall[b, d, pl.ds(at, blk), :] = (out * valid_rows(d, at, blk)).astype(BF)
+            blocks = [2 * i, 2 * i + 1]
+            ats = [pl.multiple_of(j * blk, blk) for j in blocks]
+            scores = []
+            for at in ats:
+                q2 = two_heads(qbuf[d, pl.ds(at, blk), :])
+                scores.append(mmt(q2, kvw[d, pl.ds(at, span), 0:wl]))
+            probs = []
+            for at, score in zip(ats, scores):
+                pos = col + (offset + at - radius)
+                seen = near & (pos >= 0) & (pos < lens[d])
+                e = jnp.where(seen, score * HD ** (-0.5), masked_value)
+                e = jnp.exp(e - jnp.max(e, axis=-1, keepdims=True))
+                probs.append((e * (1.0 / row_sum(e))).astype(BF))
+            for j, at, p in zip(blocks, ats, probs):
+                pbuf[d * n_blk + j] = p
+                out = one_of_two(mm(p, kvw[d, pl.ds(at, span), wl : 2 * wl]))
+                loall[b, d, pl.ds(at, blk), :] = (out * valid_rows(d, at, blk)).astype(BF)
             return carry
 
-        lax.fori_loop(0, n_blk, body, 0)
+        lax.fori_loop(0, n_blk // 2, body, 0)
 
     def three_heads(v):
         lane = lax.broadcasted_iota(jnp.int32, v.shape, 1)
@@ -987,11 +1026,11 @@
         cols[SF, mine(d), :] = score
         frow[mine(d), :] = rowsf.astype(BF)
         ghr[mine(d), :] = (grow[mine(d), :].astype(F32) * score).astype(BF)
-        step = 256
-
-        def body(t, dscore):
-            c = pl.ds(pl.multiple_of(t * step, step), step)
-            c2 = pl.ds(pl.multiple_of(fh_n + t * step, step), step)
+        size = 512
+        dscore = jnp.zeros((slots, 1), F32)
+        for t in range(fh_n // size):
+            c = slice(t * size, (t + 1) * size)
+            c2 = slice(fh_n + t * size, fh_n + (t + 1) * size)
             gate = mm(frow[mine(d), :], wguh[:, c]).astype(BF).astype(F32)
             up = mm(frow[mine(d), :], wguh[:, c2]).astype(BF).astype(F32)
             act, slope = gelu_parts(gate)
@@ -1001,9 +1040,7 @@
             midh[mine(d), c] = middle
             dguh[mine(d), c] = (grad_mid * up * slope).astype(BF)
             dguh[mine(d), c2] = (grad_mid * act).astype(BF)
-            return dscore + row_sum(middle.astype(F32) * raw)
-
-        dscore = lax.fori_loop(0, fh_n // step, body, jnp.zeros((slots, 1), F32))
+            dscore = dscore + row_sum(middle.astype(F32) * raw)
         pre = dscore * score * (1.0 - score)
         cols[PREF, mine(d), :] = pre
         backr[mine(d), :] = (mmt(dguh[mine(d), :], wguh[...]) + pre * router_f).astype(BF)
@@ -1043,15 +1080,15 @@
                 ffn_light(d, h)
 
             for a in (1, 2):
-                for i in range(1, 5):
-
-                    @step("ar%d%d%d_%d" % (a, d, h, i))
-                    def _(a=a, d=d, h=h, i=i):
-                        ar_step(a, d, h, i, tot2)
+                for u in range(2):
+                    for i in range(1, 5):
+                        steps["ar%d%d%d%d_%d" % (a, d, h, u, i)] = sums[a, d, h, u][i]
+        for i in range(1, 5):
+            steps["kar%d_%d" % (d, i)] = sums[d][i]
 
     pieces = (
         (g_h, 0, fh_n), (g_h, fh_n, fh_n), (g_h, 2 * fh_n, fh_n), (g_l, 0, 3 * fl_n),
-        (g_a, 0, wl + 512), (g_a, wl + 512, 3 * wl + 640),
+        (g_a, 0, wl + 2 * wh), (g_a, wl + 2 * wh, 3 * wl + 2 * wh + 128),
     )
     packed_at = [sum(piece[2] for piece in pieces[:p]) for p in range(len(pieces))]
 
@@ -1147,6 +1184,8 @@
 
     @step("blank")
     def _():
+        ktot[:, 0:slots, :] = jnp.zeros((docs, slots, width), BF)
+
         @pl.when(z == 0)
         def _():
             for buf in rb:
@@ -1180,25 +1219,25 @@
         value = tmm(src[:, :, f].reshape(docs * rows, width // 2), gr[...].reshape(docs * rows, wide))
         ref[f, base : base + wide] = value.astype(BF)
 
-    def rows_grad(t, src, gr, at):
-        g_a[half_features(t), at : at + wh] = tmm(src[:, half_features(t)], gr).astype(BF)
+    def rows_grads(t, pairs, at):
+        f = half_features(t)
+        value = jnp.concatenate([tmm(src[:, f], gr) for src, gr in pairs], axis=1)
+        g_a[f, at : at + 2 * wh] = value.astype(BF)
 
     def early_grads(t):
         light_grad(t, ghb, loall.at[b], g_a, 0)
-        rows_grad(t, gah, hoall[b, :, 0:wh], wl)
-        rows_grad(t, hin, dqh[:, 0:wh], wl + 256)
+        rows_grads(t, ((gah, hoall[b, :, 0:wh]), (hin, dqh[:, 0:wh])), wl)
 
     def late_grads(t):
         f = half_features(t)
-        at = wl + 512
+        at = wl + 2 * wh
         light_grad(t, nl, dqkv, g_a, at)
-        rows_grad(t, kin, dkvh[:, 0:wh], at + 3 * wl)
-        rows_grad(t, sin, dkvh[:, 256 : 256 + wh], at + 3 * wl + 256)
+        rows_grads(t, ((kin, dkvh[:, 0:wh]), (sin, dkvh[:, 256 : 256 + wh])), at + 3 * wl)
         lane = lax.broadcasted_iota(jnp.int32, (docs * slots, 128), 1)
         vectors = jnp.zeros((width // 2, 128), F32)
         for src, which, at_lane in ((hin, PREQ, 1), (kin, PREK, 2), (frow, PREF, 4)):
             vectors = vectors + tmm(src[:, f], jnp.where(lane == at_lane, cols[which], 0.0).astype(BF))
-        at = at + 3 * wl + 512
+        at = at + 3 * wl + 2 * wh
         g_a[f, at : at + 128] = vectors.astype(BF)
 
     for t in range(2):
@@ -1227,14 +1266,12 @@
             rs_start(5, t)
 
     def mixed_terms(d):
-        def body(j, carry):
-            w = pl.ds(pl.multiple_of(j * share, share), share)
+        for t in range(2):
+            w = half_features(t)
             heavy = (mmt(midh[mine(d), :], wdh[w, :]) * cols[SF, mine(d), :]).astype(BF)
             value = mmt(wdl[w, :], mid[d]) + tmm(heavy, pqk[d, 0:slots, :])
-            mixb[j, d] = value.astype(BF)
-            return carry
-
-        lax.fori_loop(0, 4, body, 0)
+            for j in range(2):
+                mixb[2 * t + j, d] = value[j * share : (j + 1) * share].astype(BF)
 
     def mixed_start(d):
         column = lax.broadcasted_iota(jnp.int32, (share, width), 1) - b * share
@@ -1271,6 +1308,8 @@
         gather_start(2 + d, doall, routed(d))
         ds = (pf * (dp - delta) * HD ** (-0.5)).astype(BF)
         dqh[mine(d), :] = one_of_three(mm(ds, keys_of(d, 0))).astype(BF)
+        query_rows = mm(dqh[mine(d), 0:wh], whq[...]) + cols[PREQ, mine(d), :] * router_q
+        qrow[mine(d), :] = query_rows.astype(BF)
 
     def heavy_back_keys(d):
         q = qall[:, mine(d), :].reshape(n_seq * slots, 256)
@@ -1291,21 +1330,22 @@
         tiles(rows, half, dol_body)
 
         def body(i, carry):
-            at = pl.multiple_of(i * blk, blk)
-            q2 = two_heads(qbuf[d, pl.ds(at, blk), :])
-            do2 = two_heads(dol[d, pl.ds(at, blk), :])
-            k = kvw[d, pl.ds(at, span), 0:wl]
-            v = kvw[d, pl.ds(at, span), wl : 2 * wl]
-            p = pbuf[d * n_blk + i]
-            pf = p.astype(F32)
-            dp = mmt(do2, v)
-            ds = (pf * (dp - row_sum(dp * pf)) * HD ** (-0.5)).astype(BF)
-            dqkv[d, pl.ds(at, blk), 0:wl] = one_of_two(mm(ds, k)).astype(BF)
-            dkvw[d, pl.ds(at, span), 0:wl] += tmm(ds, q2)
-            dkvw[d, pl.ds(at, span), wl : 2 * wl] += tmm(p, do2)
+            blocks = [2 * i, 2 * i + 1]
+            ats = [pl.multiple_of(j * blk, blk) for j in blocks]
+            do2s = [two_heads(dol[d, pl.ds(at, blk), :]) for at in ats]
+            dps = [mmt(do2, kvw[d, pl.ds(at, span), wl : 2 * wl]) for at, do2 in zip(ats, do2s)]
+            grads_s = []
+            for j, dp in zip(blocks, dps):
+                pf = pbuf[d * n_blk + j].astype(F32)
+                grads_s.append((pf * (dp - row_sum(dp * pf)) * HD ** (-0.5)).astype(BF))
+            for j, at, do2, ds in zip(blocks, ats, do2s, grads_s):
+                q2 = two_heads(qbuf[d, pl.ds(at, blk), :])
+                dqkv[d, pl.ds(at, blk), 0:wl] = one_of_two(mm(ds, kvw[d, pl.ds(at, span), 0:wl])).astype(BF)
+                dkvw[d, pl.ds(at, span), 0:wl] += tmm(ds, q2)
+                dkvw[d, pl.ds(at, span), wl : 2 * wl] += tmm(pbuf[d * n_blk + j], do2)
             return carry
 
-        lax.fori_loop(0, n_blk, body, 0)
+        lax.fori_loop(0, n_blk // 2, body, 0)
         rims[d, 0] = dkvw[d, 0:radius, :].astype(BF)
         rims[d, 1] = dkvw[d, rows + radius : rows + 2 * radius, :].astype(BF)
 
@@ -1336,9 +1376,8 @@
         pre_k = row_sum(ds_in * kin[mine(d), :].astype(F32)) * score * (1.0 - score)
         cols[PREK, mine(d), :] = pre_k
         key_rows = mm(dkvh[mine(d), 0:wh], whk[...]) + ds_in * score + pre_k * router_k
-        query_rows = mm(dqh[mine(d), 0:wh], whq[...]) + cols[PREQ, mine(d), :] * router_q
-        bothr[d, 0:slots, :] = query_rows.astype(BF)
-        bothr[d, slots : 2 * slots, :] = key_rows.astype(BF)
+        kpart[d] = key_rows.astype(BF)
+        sums[d][0]()
 
     def attention_back_terms(d, h):
         if h == 0:
@@ -1348,7 +1387,7 @@
             ar_sent(1, d)
         r = pl.ds(h * half, half)
         dqkv[d, r, wl : 3 * wl] = dkvw[d, pl.ds(h * half + radius, half), :].astype(BF)
-        value = mmt(dqkv[d, r, :], wqkv[...]) + mm(pqkt[d, r, :], bothr[d])
+        value = mmt(dqkv[d, r, :], wqkv[...]) + mm(pqkt[d, r, 0:slots], qrow[mine(d), :])
         parts[d, r, :] = value.astype(BF)
         ar_start(2, d, h)
 
@@ -1364,7 +1403,7 @@
             r = pl.ds(pl.multiple_of(h * half + t, big), big)
             inv = inva[d, r, :]
             unit = tok[d, r, :].astype(F32) * inv
-            w = tot2[d, r, :].astype(F32) * gain_a
+            w = (tot2[d, r, :].astype(F32) + mm(pqkt[d, r, :], ktot[d])) * gain_a
             inner = row_sum(w * unit) * (1.0 / width)
             ghf[d, r, :] = ghf[d, r, :] + inv * (w - unit * inner)
 
@@ -1457,11 +1496,11 @@
     @step("vec")
     def _():
         a_at, q_at = packed_at[4:6]
-        va = q_at + 3 * wl + 512
+        va = q_at + 3 * wl + 2 * wh
         gf_sum = vbuf[:, 0:1]
         ga_sum = row_sum(packed[:, q_at : q_at + 3 * wl] * wqkv[own_rows, :].astype(F32))
         eye_b = eye.astype(F32).astype(BF)
-        for h_at, w in ((a_at + wl + 256, whq), (q_at + 3 * wl, whk), (q_at + 3 * wl + 256, whv)):
+        for h_at, w in ((a_at + wl + wh, whq), (q_at + 3 * wl, whk), (q_at + 3 * wl + wh, whv)):
             ga_sum = ga_sum + row_sum(packed[:, h_at : h_at + wh] * mmt(eye_b, w[...]))
         vectors = packed[:, va : va + 128]
 
@@ -1493,6 +1532,8 @@
             entry.wait_send()
     for d in range(docs):
         ar_sent(2, d)
+        flights[d, 2].wait_send()
+        flights[d, 3].wait_send()
     for copy in out_copies:
         copy.wait()
 
@@ -1503,8 +1544,8 @@
     routed = docs * slots
     keys = n_seq * slots
     pad = -(-wh // 256) * 256
-    ga_n = 4 * wl + 4 * pad + 128
-    widths = [fh_n, fh_n, fh_n, 3 * fl_n, wl + 512, 3 * wl + 640]
+    ga_n = 4 * wl + 4 * wh + 128
+    widths = [fh_n, fh_n, fh_n, 3 * fl_n, wl + 2 * wh, 3 * wl + 2 * wh + 128]
     h_n, l_n = 3 * fh_n, 3 * fl_n
     radius = WINDOW // 2
     span = rows + 2 * radius
@@ -1518,10 +1559,11 @@
         ((docs * rows // WINDOW, 2 * WINDOW, 2 * WINDOW), BF), ((4, docs, rows, wl), BF), ((routed, pad), BF),
         ((n_seq, routed, 2 * pad), BF), ((docs, wh // HD * slots, keys), BF), ((4, routed, pad), BF),
         ((n_seq, routed, pad), BF), ((n_seq, routed, pad), BF), ((routed, width), BF), ((routed, width), BF),
-        ((docs, 2 * slots, width), BF),
+        ((routed, width), BF), ((docs, slots, width), BF), ((docs, 2 * slots, width), BF),
+        ((docs, slots // 2, width), BF), ((docs, slots // 4, width), BF),
         ((docs, 2 * slots, rows), BF), ((docs, rows, 2 * slots), BF), ((docs, rows, width), BF),
-        ((docs, rows, width), BF), ((docs, rows, width), BF), ((docs, 2, rows // 4, width), BF),
-        ((docs, 2, rows // 8, width), BF), ((6, routed, 1), F32),
+        ((docs, rows, width), BF), ((docs, rows, width), BF), ((docs, 2, 2, rows // 8, width), BF),
+        ((docs, 2, 2, rows // 16, width), BF), ((6, routed, 1), F32),
         ((docs, rows, fl_n), F32), ((routed, fh_n), F32), ((routed, width), BF), ((docs, rows, width), BF),
         ((docs, rows, 1), F32), ((docs, rows, fl_n), BF), ((docs, rows, 2 * fl_n), BF), ((routed, width), BF),
         ((routed, width), BF), ((routed, fh_n), BF), ((routed, 2 * fh_n), BF),
@@ -1538,7 +1580,7 @@
     ]
     sems = [
         (18,), (3, 2), (3, 2), (3, 2), (3, 2), (docs, 3), (docs, 3), (3,), (3,),
-        (3, docs, 2, 4), (3, docs, 2, 4), (2 + docs, nz), (2 + docs, nz), (2 + docs, nz), (2 + docs, nz),
+        (docs, 4), (docs, 4), (3, docs, 2, 2, 4), (3, docs, 2, 2, 4), (2 + docs, nz), (2 + docs, nz), (2 + docs, nz), (2 + docs, nz),
         (docs, 2), (docs, 2), (docs, 2), (docs, 2), (docs, 3), (docs, 3),
         (6, nz), (6, nz), (6, nz - 1), (6, nz - 1), (6,), (6,), (3,), (3,), (13,),
     ]
@@ -1574,7 +1616,7 @@
         return plain_shards(*args)
     share = width // 4
     chunk = width // n_seq
-    ga_n = 4 * wl + 4 * 256 + 128
+    ga_n = 4 * wl + 4 * wh + 128
     pack_n = 3 * fh_n + 3 * fl_n + ga_n
     in_hbm = [
         tokens, cotangent, wq_light, wk_light, wv_light, wo_light, wq_heavy.T, wk_heavy.T, wv_heavy.T, wo_heavy.T,
@@ -1601,9 +1643,9 @@
 
     l_at = 3 * fh_n
     a_at = l_at + 3 * fl_n
-    q_at = a_at + wl + 512
+    q_at = a_at + wl + 2 * wh
     parts = [(q_at + i * wl, wl) for i in range(3)] + [(a_at, wl)]
-    parts += [(a_at + wl + 256, wh), (q_at + 3 * wl, wh), (q_at + 3 * wl + 256, wh), (a_at + wl, wh)]
+    parts += [(a_at + wl + wh, wh), (q_at + 3 * wl, wh), (q_at + 3 * wl + wh, wh), (a_at + wl, wh)]
     parts += [(l_at + i * fl_n, fl_n) for i in range(3)] + [(i * fh_n, fh_n) for i in range(3)]
     outs = pl.pallas_call(
         functools.partial(hand_out, parts),

time: 147 us -> 138 us (0.939)
  Pallas kernels: 145 us -> 135 us
    pallas_call x1, Pallas kernels: 140 us -> 130 us  [shards(): pl.pallas_call(functools.partial(layer_kernel, dims), out_shape=[jax.Shap...]
where the time goes in v5:
time: 138 us; the launch traced here: 137 us
  Pallas kernels  135 us (98%)
  local copies, waits for them, and re-layouts  1.4 us (1%)
    pallas_call x1, Pallas kernels, shards(): pl.pallas_call(functools.partial(layer_kernel, dims), out_shape=[jax.Shap...  130 us
    pallas_call x1, Pallas kernels, shards(): pl.pallas_call(functools.partial(hand_out, parts), out_shape=[jax.ShapeDt...  5.01 us

profile of v5, /device:TPU:0, one launch (start us, length us, event | category | flops | bytes accessed | tf_op | source)
XLA Modules:
  0.0 137.4 jit_solution(11485273906607651379)
XLA Ops:
  0.7 130.2 %shard_map.391 = (f32[2,512,768]{2,1,0:T(8,128)}, f32[2,192,512]{2,1,0:T(8,128)}, f32[96,5248]{1,0:T(8,128)}, f32[128,96]{1,0:T(8,128)}) custom-call(s32[2]{0:T(128)} %refs_0_.1, s32[2,64]{1,0:T(2,128)} %refs_1_.1, s32[2,64]{1,0:T(2,128)} %refs_2_.1, bf16[768]{0:T(1024)(128)(2,1)} %refs_3_.1, bf16[768]{0:T(1024)(128)(2,1)} %refs_4_.1, ...), custom_call_target="tpu_custom_call" | custom-call | tf_op jit(solution)/shard_map/pallas_call | solution.py:1627
  130.9 1.4 %slice_bitcast_fusion = (f32[96]{0:T(128)}, f32[96]{0:T(128)}, f32[96]{0:T(128)}, f32[96]{0:T(128)}, f32[96]{0:T(128)}) fusion(f32[128,96]{1,0:T(8,128)} %get-tuple-element.46), kind=kLoop, calls=%fused_computation | loop fusion | bytes 3840 | tf_op jit(solution)/shard_map/squeeze | solution.py:1664
  132.3 5.0 %shard_map.392 = (f32[2,512,768]{2,1,0:T(8,128)}, f32[2,192,512]{2,1,0:T(8,128)}, f32[96,128]{1,0:T(8,128)}, f32[96,128]{1,0:T(8,128)}, f32[96,128]{1,0:T(8,128)...) custom-call(f32[2,512,768]{2,1,0:T(8,128)} %get-tuple-element.41.tok, ...), custom_call_target="tpu_custom_call" | custom-call | tf_op jit(solution)/shard_map/pallas_call | solution.py:1650

commit v6 on v5

--- a/solution.py
+++ b/solution.py
@@ -395,24 +395,24 @@
 
 
 ORDER = (
-    "load", "rowskv", "norm", "pre0", "qkv", "gp0_2", "la0", "gp0_3", "gp0_1", "pre1", "hattn", "predmh",
-    "wgp", "la1", "hproj", "nf00", "nf01", "fh0", "fl00", "fl01", "gp1_2", "nf10", "nf11", "fh1", "hgrB1",
-    "ar1011_1", "hgrA1", "fl11", "hgrB0", "ar1001_1", "ar1010_1", "ar1011_2", "rs1a", "rs1b", "rs1c",
-    "fl10", "hgrA0", "hgrB2", "ar1011_3", "ar1010_2", "hgrA2", "ar1101_1", "ar1110_1", "lgA", "rs0a",
-    "ar1111_1", "rs1r", "ar1100_1", "ar1001_2", "ar1000_1", "ar1111_2", "gp1_3", "lgB", "ar1101_2",
-    "ar1000_2", "ar1001_3", "ar1011_4", "rs0b", "ar1111_3", "ar1000_3", "rs2d", "ar1100_2", "ar1010_3",
-    "ar1001_4", "ar1101_3", "ar1100_3", "rs2a", "rs0c", "ar1110_2", "ar1000_4", "rs0d", "mixt0", "ar1111_4",
-    "rs0r", "ar1110_3", "mixt1", "ar1010_4", "mx1", "gp1_1", "mixs0", "hg01", "hg00", "ar1100_4", "hb0",
-    "mx0", "ar1110_4", "lb0", "mixs1", "hg11", "rs2b", "gp2_2", "ar1101_4", "hg10", "hb1", "awgA", "rs3a",
-    "gp2_3", "lb1", "awgB", "rs3b", "rs3c", "gp3_2", "abt00", "rs2c", "rs4a", "gp3_3", "abt01", "rs2r",
-    "gp2_1", "abt10", "abt11", "ar2011_1", "blank", "ar2000_1", "hk0", "rs4b", "gp3_1", "ar2010_1", "hk1",
-    "ar2111_1", "rs3r", "ar2101_1", "aqgA", "ar2000_2", "mixf1", "ar2110_1", "ar2001_1", "rs4d", "kar1_1",
-    "ar2100_1", "aqgB", "ar2111_2", "rs4c", "kar0_1", "ar2010_2", "rs3d", "rs1d", "kar0_2", "ar2011_2",
-    "ar2100_2", "mixf0", "rs1e", "rs5a", "ar2101_2", "ar2110_2", "ar2000_3", "rs5b", "rs5c", "ar2111_3",
-    "ar2110_3", "ar2000_4", "ar2111_4", "ar2100_3", "ar2001_2", "ar2011_3", "rs4r", "rs5d", "kar1_2",
-    "rs5r", "rs0e", "rs3e", "ar2001_3", "kar1_3", "kar0_3", "kar0_4", "ar2101_3", "ar2100_4", "rs4e",
-    "rs2e", "gains", "ar2110_4", "ar2010_3", "rs5e", "vec", "ar2001_4", "tok00", "ar2010_4", "ar2101_4",
-    "kar1_4", "ar2011_4", "tok10", "tok01", "tok11", "vece",
+    "load", "rowskv", "norm", "pre0", "qkv", "pre1", "gp0_2", "la0", "predmh", "gp0_1", "gp0_3", "hattn",
+    "wgp", "la1", "hproj", "nf00", "nf01", "fh0", "fl00", "fl01", "nf10", "nf11", "fh1", "hgrB1",
+    "ar1000_1", "ar1011_1", "hgrA1", "fl11", "hgrA0", "ar1011_2", "rs1a", "rs1b", "fl10", "rs1c",
+    "ar1010_1", "ar1001_1", "hgrB2", "ar1111_1", "hgrB0", "ar1000_2", "ar1110_1", "ar1001_2", "ar1010_2",
+    "ar1101_1", "rs1r", "mixt1", "ar1100_1", "ar1010_3", "rs0d", "mixs1", "ar1001_3", "ar1110_2",
+    "ar1101_2", "rs0a", "lgB", "ar1100_2", "ar1011_3", "rs0b", "mixt0", "ar1111_2", "ar1110_3", "hgrA2",
+    "ar1100_3", "ar1111_3", "gp1_2", "ar1101_3", "ar1000_3", "rs0c", "mx0", "rs0r", "mixs0", "lgA",
+    "ar1000_4", "ar1110_4", "mx1", "ar1001_4", "ar1111_4", "hg00", "ar1010_4", "ar1011_4", "ar1101_4",
+    "hg01", "ar1100_4", "rs2a", "hg11", "hg10", "hb1", "lb1", "lb0", "hb0", "rs2b", "rs2c", "rs2r", "abt10",
+    "rs3a", "gp1_3", "rs3b", "abt11", "gp1_1", "gp2_2", "awgA", "abt00", "gp3_2", "awgB", "abt01", "rs4a",
+    "gp2_1", "gp3_3", "ar2000_1", "ar2001_1", "ar2110_1", "rs3c", "mixf0", "rs1d", "ar2100_1", "ar2111_1",
+    "rs3r", "gp2_3", "blank", "ar2010_1", "gp3_1", "ar2101_1", "ar2000_2", "ar2011_1", "hk0", "hk1", "aqgA",
+    "rs0e", "rs4b", "rs4r", "aqgB", "ar2011_2", "rs4d", "ar2000_3", "kar0_1", "rs2d", "ar2010_2", "rs3d",
+    "ar2101_2", "rs1e", "rs5a", "ar2100_2", "kar0_2", "ar2110_2", "rs5d", "ar2011_3", "rs4c", "rs5b",
+    "rs5c", "kar1_1", "ar2100_3", "rs3e", "kar0_3", "kar1_2", "ar2001_2", "rs2e", "ar2101_3", "rs5r",
+    "gains", "ar2111_2", "rs4e", "ar2001_3", "kar1_3", "ar2111_3", "ar2010_3", "ar2110_3", "kar1_4",
+    "kar0_4", "ar2100_4", "rs5e", "vec", "ar2111_4", "ar2000_4", "ar2001_4", "ar2011_4", "ar2101_4",
+    "ar2010_4", "mixf1", "tok10", "tok00", "ar2110_4", "tok11", "tok01", "vece",
 )
 BF = jnp.bfloat16
 F32 = jnp.float32
@@ -560,7 +560,7 @@
         at = lax.broadcasted_iota(jnp.int32, (count, 1), 0) + (offset + first)
         return jnp.where(at < lens[d], 1.0, 0.0).astype(F32)
 
-    big = 64
+    big = 128
 
     def tiles(count, size, body):
         def step(t, carry):

time: 138 us -> 134 us (0.971)
  Pallas kernels: 135 us -> 131 us
    pallas_call x1, Pallas kernels: 130 us -> 126 us  [shards(): pl.pallas_call(functools.partial(layer_kernel, dims), out_shape=[jax.Shap...]
where the time goes in v6:
time: 134 us
  Pallas kernels  131 us (98%)
  local copies, waits for them, and re-layouts  1.4 us (1%)
    pallas_call x1, Pallas kernels, shards(): pl.pallas_call(functools.partial(layer_kernel, dims), out_shape=[jax.Shap...  126 us
    pallas_call x1, Pallas kernels, shards(): pl.pallas_call(functools.partial(hand_out, parts), out_shape=[jax.ShapeDt...  5.01 us

profile of v6, /device:TPU:0, one launch (start us, length us, event | category | flops | bytes accessed | tf_op | source)
XLA Modules:
  0.0 133.7 jit_solution(13149970099819984195)
XLA Ops:
  0.7 126.5 %shard_map.391 = (f32[2,512,768]{2,1,0:T(8,128)}, f32[2,192,512]{2,1,0:T(8,128)}, f32[96,5248]{1,0:T(8,128)}, f32[128,96]{1,0:T(8,128)}) custom-call(s32[2]{0:T(128)} %refs_0_.1, s32[2,64]{1,0:T(2,128)} %refs_1_.1, s32[2,64]{1,0:T(2,128)} %refs_2_.1, bf16[768]{0:T(1024)(128)(2,1)} %refs_3_.1, bf16[768]{0:T(1024)(128)(2,1)} %refs_4_.1, ...), custom_call_target="tpu_custom_call" | custom-call | tf_op jit(solution)/shard_map/pallas_call | solution.py:1627
  127.1 1.4 %slice_bitcast_fusion = (f32[96]{0:T(128)}, f32[96]{0:T(128)}, f32[96]{0:T(128)}, f32[96]{0:T(128)}, f32[96]{0:T(128)}) fusion(f32[128,96]{1,0:T(8,128)} %get-tuple-element.46), kind=kLoop, calls=%fused_computation | loop fusion | bytes 3840 | tf_op jit(solution)/shard_map/squeeze | solution.py:1664
  128.5 5.0 %shard_map.392 = (f32[2,512,768]{2,1,0:T(8,128)}, f32[2,192,512]{2,1,0:T(8,128)}, f32[96,128]{1,0:T(8,128)}, f32[96,128]{1,0:T(8,128)}, f32[96,128]{1,0:T(8,128)...) custom-call(f32[2,512,768]{2,1,0:T(8,128)} %get-tuple-element.41.tok, ...), custom_call_target="tpu_custom_call" | custom-call | tf_op jit(solution)/shard_map/pallas_call | solution.py:1650
